TPU v7x, 32 devices: a whole 2x2x4 slice. The times are simulated.
32 devices in a mesh: face: 4 (over z), tile: 8 (over y, x, core).
Axes of the slice: x: 2, y: 2, z: 4, core: 2. Of those that a mesh axis runs over, the one named last changes fastest.
Arguments:
- state: bfloat16 [4, 8, 2, 4, 512, 128], P('face', 'tile'), may hold values from -6 to 6
- obs_values: bfloat16 [32768, 256], P(('face', 'tile')), may hold values from -6 to 6
- obs_dest: int32 [32768, 1], P(('face', 'tile')), may hold values from 0 to 31; in each aligned block of 1024 rows (0 to 1023, 1024 to 2047, ...) at most 64 rows name the same one
- obs_pixel: int32 [32768], P(('face', 'tile')), may hold values from 0 to 4095
- matching: int32 [4, 2, 3], replicated, may hold values from 0 to 3, as said below
- kernel_one: bfloat16 [9, 128, 256], replicated, may hold values from -0.1875 to 0.1875
- bias_one: float32 [256], replicated, may hold values from -3 to 3
- kernel_two: bfloat16 [9, 256, 128], replicated, may hold values from -0.125 to 0.125
- bias_two: float32 [128], replicated, may hold values from -3 to 3
- cotangent: bfloat16 [4, 8, 2, 4, 512, 128], P('face', 'tile'), may hold values from -6 to 6
Outputs:
- analysis: bfloat16 [4, 8, 2, 4, 512, 128], P('face', 'tile')
- grad_state: float32 [4, 8, 2, 4, 512, 128], P('face', 'tile')
Inputs may be any that keep to these rules, and one draw needn't show every extreme that they name: `obs_dest`: of the rows of one device, at most 64 name the same pixel tile, and in every draw some device names some tile exactly 64 times. The matching pairs sides: if side s of face block f is matched with side s2 of block g and flag r, then side s2 of g is matched with side s of f and the same flag. A block may be matched with itself on its other side.
All inputs are finite; a program needn't handle non-finite values.
Results may differ from a plain program's by a relative error of at most 0.0034.
Values may be sent and summed in bfloat16 or wider, within the bound.
No kernel may reach another device: no remote copies, remote signals or barrier semaphores. Data moves between devices by JAX's collectives and lax.ppermute only.
A program may use at most 192 MiB of HBM per device.

v0:
```python
import functools
import math

import jax
import jax.numpy as jnp
from jax import lax
from jax.experimental import pallas as pl
from jax.experimental.pallas import tpu as pltpu
from jax.sharding import PartitionSpec as P

F32 = jnp.float32
BF16 = jnp.bfloat16
GROUP = 8
HIGH = 64
PIXEL_ROWS = 8
VMEM_LIMIT = 48 * 1024 * 1024
ROOT = math.sqrt(2.0 / math.pi)
CUBIC = 0.044715


def params():
    return pltpu.CompilerParams(vmem_limit_bytes=VMEM_LIMIT)


def cost(flops, nbytes):
    return pl.CostEstimate(flops=int(flops), bytes_accessed=int(nbytes), transcendentals=0)


def whole(shape):
    return pl.BlockSpec(shape, lambda *_: (0,) * len(shape))


def dot(a, b):
    return jnp.dot(a, b, preferred_element_type=F32)


def matched(matching_ref, side, faces):
    face = lax.axis_index("face")
    partner = matching_ref[face, side, 0]
    return lax.rem(partner - face + faces, faces), matching_ref[face, side, 1], matching_ref[face, side, 2]


def partner_rows(part_refs, array, hop, their_side, flipped):
    rows = None
    for k, ref in enumerate(part_refs):
        mine = jnp.where(their_side == 1, ref[array, 1], ref[array, 0])
        rows = mine if rows is None else jnp.where(hop == k, mine, rows)
    swapped = jnp.concatenate([rows[GROUP:], rows[:GROUP]], axis=0)
    return jnp.where(flipped == 1, swapped, rows)


def rolled_rows(rows, step):
    first, second = rows[:GROUP], rows[GROUP:]
    if step:
        first = pltpu.roll(first, (-step) % GROUP, 0)
        second = pltpu.roll(second, step % GROUP, 0)
    return jnp.concatenate([first, second], axis=0).astype(BF16)


def side_forward(rows, side, taps_ref):
    total = None
    for dy in (-1, 0, 1):
        term = dot(rolled_rows(rows, dy), taps_ref[3 * (dy + 1) + 2 * side])
        total = term if total is None else total + term
    return total


def side_adjoint(rows, their_side, flipped, taps_ref):
    total = None
    for dy in (-1, 0, 1):
        row_tap = jnp.where(flipped == 1, 1 - dy, 1 + dy)
        term = dot(rolled_rows(rows, -dy), taps_ref[3 * row_tap + 2 * their_side])
        total = term if total is None else total + term
    return total


def shift_columns(values, step):
    count = values.shape[0]
    at = lax.broadcasted_iota(jnp.int32, values.shape, 0)
    moved = pltpu.roll(values, (-step) % count, 0)
    edge = count - 1 if step == 1 else 0
    return jnp.where(at == edge, 0.0, moved)


def pack_body(capacity, dest_ref, pixel_ref, values_ref, out_ref):
    count = values_ref.shape[0]
    devices = out_ref.shape[0]
    block = 128
    dest_row = dest_ref[...].astype(F32)
    pixel_row = pixel_ref[...]
    eye = lax.broadcasted_iota(jnp.int32, (block, block), 0) == lax.broadcasted_iota(
        jnp.int32, (block, block), 1
    )

    def column(row, start):
        piece = row[:, start : start + block]
        return jnp.sum(jnp.where(eye, piece, 0.0), axis=1, keepdims=True)

    high_row = lax.shift_right_logical(pixel_row, 6).astype(F32) + 1.0
    low_row = (pixel_row & (HIGH - 1)).astype(F32)
    own = lax.broadcasted_iota(jnp.int32, (block, count), 0)
    other = lax.broadcasted_iota(jnp.int32, (block, count), 1)
    lane = lax.broadcasted_iota(jnp.int32, (block, 128), 1)
    lane_rank = (lane & (HIGH - 1)).astype(F32)
    rank_row = jnp.zeros((1, count), F32)
    coded = []
    for start in range(0, count, block):
        same = column(dest_row, start) == dest_row
        later = (own + start) < other
        earlier = (own + start) > other
        rank_row = rank_row + jnp.sum(
            jnp.where(same & later, 1.0, 0.0), axis=0, keepdims=True
        )
        rank = jnp.sum(jnp.where(same & earlier, 1.0, 0.0), axis=1, keepdims=True)
        code = jnp.where(lane < HIGH, column(high_row, start), column(low_row, start))
        coded.append(jnp.where(rank == lane_rank, code, 0.0).astype(BF16))
    to_device = (
        lax.broadcasted_iota(jnp.int32, (devices, count), 0).astype(F32) == dest_row
    )
    pixels = dot(
        jnp.where(to_device, 1.0, 0.0).astype(BF16), jnp.concatenate(coded, axis=0)
    )
    out_ref[:, 2 * capacity :, :] = jnp.broadcast_to(
        pixels[:, None, :], (devices, PIXEL_ROWS, 128)
    ).astype(BF16)
    slot_row = dest_row * capacity + rank_row
    slots = 256
    per_block = slots // capacity
    values = values_ref[...]
    slot_at = lax.broadcasted_iota(jnp.int32, (slots, count), 0).astype(F32)
    for start in range(0, devices * capacity, slots):
        onehot = jnp.where(slot_at == slot_row - start, 1.0, 0.0).astype(BF16)
        rows = dot(onehot, values).astype(BF16)
        first = start // capacity
        for half in range(2):
            out_ref[first : first + per_block, half * capacity : (half + 1) * capacity, :] = (
                rows[:, half * 128 : (half + 1) * 128].reshape(per_block, capacity, 128)
            )


def edge_body(rows, x_lo, x_hi, c_lo, c_hi, p_lo, p_hi, n_lo, n_hi, out_ref):
    tiles = lax.axis_size("tile")
    last = lax.axis_index("tile") == tiles - 1
    out_ref[...] = jnp.zeros_like(out_ref)
    for side in range(2):
        at = 0 if side == 0 else -1
        prev = (p_lo, p_hi)[side][...].astype(F32)
        after = (n_lo, n_hi)[side][...].astype(F32)
        at = 0 if side == 0 else prev.shape[1] - 1
        for array in range(2):
            own = ((x_lo, x_hi), (c_lo, c_hi))[array][side][...].astype(F32)
            for band in range(2):
                base = band * GROUP
                out_ref[array, side, base, :] = prev[2 * array + band, at]
                for r in range(rows):
                    out_ref[array, side, base + 1 + r, :] = own[band * rows + r, at]
                fold = own[(1 - band) * rows + rows - 1, at]
                out_ref[array, side, base + 1 + rows, :] = jnp.where(
                    last, fold, after[2 * array + band, at]
                )


def lift_body(
    rows, faces, matching_ref, x_ref, c_ref, prev_ref, next_ref, k1_ref, b1_ref, k2t_ref, *rest
):
    parts = rest[:faces]
    pre_ref, grad_ref, x_cat, c_cat, x_side, c_side = rest[faces:]
    step = pl.program_id(0)
    ext = rows + 2
    channels = x_ref.shape[2]
    last = lax.axis_index("tile") == lax.axis_size("tile") - 1

    @pl.when(step == 0)
    def _():
        for array, (own, cat) in enumerate(((x_ref, x_cat), (c_ref, c_cat))):
            order = (-1, 0, 1) if array == 0 else (1, 0, -1)
            for band in range(2):
                for e in range(ext):
                    if e == 0:
                        row = prev_ref[2 * array + band].astype(F32)
                    elif e <= rows:
                        row = own[band * rows + e - 1].astype(F32)
                    else:
                        fold = own[(1 - band) * rows + rows - 1].astype(F32)
                        row = jnp.where(last, fold, next_ref[2 * array + band].astype(F32))
                    for place, shift in enumerate(order):
                        moved = row if shift == 0 else shift_columns(row, shift)
                        cat[band * ext + e, :, place * channels : (place + 1) * channels] = (
                            moved.astype(BF16)
                        )
        for side in range(2):
            hop, their_side, flipped = matched(matching_ref, side, faces)
            x_side[side] = side_forward(
                partner_rows(parts, 0, hop, their_side, flipped), side, k1_ref
            )
            c_side[side] = side_adjoint(
                partner_rows(parts, 1, hop, their_side, flipped), their_side, flipped, k2t_ref
            )

    band = step // rows
    r = lax.rem(step, rows)
    centre = band * ext + r + 1
    sign = 1 - 2 * band
    taps = k1_ref.shape[0] * channels
    for cat, side_ref, weights, out_ref, way in (
        (x_cat, x_side, k1_ref, pre_ref, sign),
        (c_cat, c_side, k2t_ref, grad_ref, -sign),
    ):
        lhs = jnp.concatenate([cat[centre - way], cat[centre], cat[centre + way]], axis=1)
        total = dot(lhs, weights[...].reshape(taps, weights.shape[2]))
        if out_ref is pre_ref:
            total = total + b1_ref[...]
        out_ref[0] = total
        width = out_ref.shape[1]
        at = band * GROUP + r + 1
        out_ref[0, 0:1, :] += side_ref[0, pl.ds(at, 1), :]
        out_ref[0, width - 1 : width, :] += side_ref[1, pl.ds(at, 1), :]


def row_taps(taps_ref, row):
    return jnp.concatenate([taps_ref[3 * row + dx] for dx in range(3)], axis=1)


def merge_shifts(wide, forward):
    channels = wide.shape[1] // 3
    left, mid, right = (wide[:, k * channels : (k + 1) * channels] for k in range(3))
    step = -1 if forward else 1
    return mid + shift_columns(left, step) + shift_columns(right, -step)


def gelu_body(
    rows, capacity, recv_ref, pre_ref, grad_ref, k2_ref, k1t_ref, inner_ref, gp_ref, up_ref, down_ref,
    edge_ref, values, keys,
):
    step = pl.program_id(0)
    devices = recv_ref.shape[0]
    width = pre_ref.shape[1]
    slots = devices * capacity
    per_lane = 128 // capacity

    @pl.when(step == 0)
    def _():
        edge_ref[...] = jnp.zeros_like(edge_ref)
        for half in range(2):
            values[:, half * 128 : (half + 1) * 128] = recv_ref[
                :, half * capacity : (half + 1) * capacity, :
            ].reshape(slots, 128)
        owner = lax.broadcasted_iota(jnp.int32, (GROUP, 128), 1) // capacity
        for start in range(0, devices, per_lane):
            key = jnp.zeros((GROUP, 128), F32)
            for k in range(per_lane):
                code = recv_ref[start + k, 2 * capacity :, :].astype(F32)
                mine = (code - 1.0) * HIGH + pltpu.roll(code, HIGH, 1)
                if k:
                    mine = pltpu.roll(mine, k * capacity, 1)
                key = jnp.where(owner == k, mine, key)
            keys[:, start * capacity : start * capacity + 128] = key

    band = step // rows
    r = lax.rem(step, rows)
    local = keys[0:1, :] - (step * width).astype(F32)
    column = lax.broadcasted_iota(jnp.int32, (width, slots), 0).astype(F32)
    onehot = jnp.where(column == local, 1.0, 0.0).astype(BF16)
    v = pre_ref[0] + dot(onehot, values[...])
    square = v * v
    t = jnp.tanh(v * (ROOT + (ROOT * CUBIC) * square))
    half = 0.5 + 0.5 * t
    inner = (v * half).astype(BF16)
    slope = half + (0.5 * v) * (1.0 - t * t) * (ROOT + (3.0 * ROOT * CUBIC) * square)
    gp = (grad_ref[0] * slope).astype(BF16)
    inner_ref[0] = inner
    gp_ref[0] = gp
    at = band * GROUP + r + 1
    for array, (ref, _) in enumerate(((inner_ref, inner), (gp_ref, gp))):
        edge_ref[array, 0, pl.ds(at, 1), :] = ref[0, 0:16, :].astype(F32)[0:1]
        edge_ref[array, 1, pl.ds(at, 1), :] = ref[0, width - 16 :, :].astype(F32)[15:16]

    for edge_row, out_ref in ((0, down_ref), (rows - 1, up_ref)):

        @pl.when(r == edge_row)
        def _():
            sign = 1 - 2 * band
            outward = -1 if edge_row == 0 else 1
            tap = 1 - outward * sign
            up = merge_shifts(dot(inner_ref[0], row_taps(k2_ref, tap)), True)
            out_ref[band] = up.astype(BF16)
            tap = 1 + outward * sign
            back = merge_shifts(dot(gp_ref[0], row_taps(k1t_ref, tap)), False)
            out_ref[2 + band] = back.astype(BF16)


def inside_body(rows, inner_ref, gp_ref, k2_ref, k1t_ref, ana_ref, grad_ref, w2, w1):
    step = pl.program_id(0)
    band = step // rows
    r = lax.rem(step, rows)
    sign = 1 - 2 * band
    lifted, channels = k2_ref.shape[1], k2_ref.shape[2]

    @pl.when(step == 0)
    def _():
        for taps, w in ((k2_ref, w2), (k1t_ref, w1)):
            for dy in range(3):
                for dx in range(3):
                    w[dy * lifted : (dy + 1) * lifted, dx * channels : (dx + 1) * channels] = taps[
                        3 * dy + dx
                    ]

    for source, w, out_ref, forward in ((inner_ref, w2, ana_ref, True), (gp_ref, w1, grad_ref, False)):
        way = sign if forward else -sign
        pieces = []
        for dy in (-1, 0, 1):
            at = r + way * dy
            if dy == 0:
                pieces.append(source[step])
            else:
                inside = (at >= 0) & (at < rows)
                piece = source[band * rows + jnp.clip(at, 0, rows - 1)]
                pieces.append(jnp.where(inside, piece, jnp.zeros_like(piece)))
        out_ref[0] = merge_shifts(dot(jnp.concatenate(pieces, axis=1), w[...]), forward)


def side_body(faces, matching_ref, k2_ref, k1t_ref, *rest):
    parts = rest[:faces]
    out_ref = rest[faces]
    for side in range(2):
        hop, their_side, flipped = matched(matching_ref, side, faces)
        out_ref[0, side] = side_forward(
            partner_rows(parts, 0, hop, their_side, flipped), side, k2_ref
        )
        out_ref[1, side] = side_adjoint(
            partner_rows(parts, 1, hop, their_side, flipped), their_side, flipped, k1t_ref
        )


def final_body(
    rows, x_ref, c_ref, ana_ref, grad_ref, b2_ref, up_ref, prev_ref, next_ref, own_ref, below_ref,
    above_ref, out_ana, out_grad, held,
):
    step = pl.program_id(0)
    band = step // rows
    r = lax.rem(step, rows)
    last = lax.axis_index("tile") == lax.axis_size("tile") - 1
    width = x_ref.shape[1]
    for array, (own, acc, out) in enumerate(
        ((x_ref, ana_ref, out_ana), (c_ref, grad_ref, out_grad))
    ):
        total = own[0].astype(F32) + acc[0]
        if array == 0:
            total = total + b2_ref[...]
        held[...] = total

        @pl.when(r == 0)
        def _():
            held[...] += prev_ref[2 * array + band].astype(F32)

        @pl.when(r == rows - 1)
        def _():
            fold = up_ref[2 * array + 1 - band].astype(F32)
            held[...] += jnp.where(last, fold, next_ref[2 * array + band].astype(F32))

        for side in range(2):
            column = 0 if side == 0 else width - 1
            base = band * GROUP
            extra = own_ref[array, side, pl.ds(base + r + 1, 1), :]
            before = below_ref[array, side, pl.ds(base + rows + 1, 1), :]
            fold = own_ref[array, side, pl.ds((1 - band) * GROUP + rows + 1, 1), :]
            after = jnp.where(last, fold, above_ref[array, side, pl.ds(base, 1), :])
            extra = extra + jnp.where(r == 0, before, 0.0) + jnp.where(r == rows - 1, after, 0.0)
            held[column : column + 1, :] += extra
        out[0] = held[...].astype(out.dtype)


def per_device(
    state,
    obs_values,
    obs_dest,
    obs_pixel,
    matching,
    kernel_one,
    bias_one,
    kernel_two,
    bias_two,
    cotangent,
):
    rows, width, channels = state.shape[3], state.shape[4], state.shape[5]
    lifted = kernel_one.shape[2]
    tiles, faces = lax.axis_size("tile"), lax.axis_size("face")
    devices = tiles * faces
    count = obs_values.shape[0]
    capacity = 2 * count // devices
    all_rows = 2 * rows
    chunk = 2 * capacity + PIXEL_ROWS
    x = state.reshape(all_rows, width, channels)
    c = cotangent.reshape(all_rows, width, channels)
    forward = [(i, i + 1) for i in range(tiles - 1)]
    backward = [(i + 1, i) for i in range(tiles - 1)]
    up_rows = jnp.concatenate([x[rows - 1 :: rows], c[rows - 1 :: rows]], axis=0)
    down_rows = jnp.concatenate([x[0::rows], c[0::rows]], axis=0)
    prev_rows = lax.ppermute(up_rows, "tile", forward)
    next_rows = lax.ppermute(down_rows, "tile", backward)

    packed = pl.pallas_call(
        functools.partial(pack_body, capacity),
        out_shape=jax.ShapeDtypeStruct((devices, chunk, 128), BF16),
        compiler_params=params(),
        cost_estimate=cost(2 * devices * capacity * count * lifted, 2 << 20),
        name="pack",
    )(obs_dest.reshape(1, count), obs_pixel.reshape(1, count), obs_values)
    received = lax.all_to_all(packed, ("face", "tile"), 0, 0, tiled=True)

    def exchange(own):
        parts = [own]
        for k in range(1, faces):
            parts.append(
                lax.ppermute(own, "face", [((i + k) % faces, i) for i in range(faces)])
            )
        return parts

    strip = 16
    low = lambda n: pl.BlockSpec((n, strip, channels), lambda *_: (0, 0, 0))
    high = lambda n: pl.BlockSpec((n, strip, channels), lambda *_: (0, width // strip - 1, 0))
    edges = pl.pallas_call(
        functools.partial(edge_body, rows),
        grid=(1,),
        in_specs=[low(all_rows), high(all_rows)] * 2 + [low(4), high(4)] * 2,
        out_specs=whole((2, 2, 2 * GROUP, channels)),
        out_shape=jax.ShapeDtypeStruct((2, 2, 2 * GROUP, channels), F32),
        compiler_params=params(),
        cost_estimate=cost(0, 1 << 18),
        name="edges",
    )(x, x, c, c, prev_rows, prev_rows, next_rows, next_rows)
    parts = exchange(edges)

    k1t = jnp.transpose(kernel_one, (0, 2, 1))
    k2t = jnp.transpose(kernel_two, (0, 2, 1))
    b1 = bias_one.reshape(1, lifted)
    b2 = bias_two.reshape(1, channels)
    smem = pl.BlockSpec(memory_space=pltpu.SMEM)
    row_block = lambda n: pl.BlockSpec((1, width, n), lambda i: (i, 0, 0))
    part_shape = (2, 2, 2 * GROUP, channels)
    conv_flops = 2 * 9 * all_rows * width * channels * lifted
    pre, grad_inner = pl.pallas_call(
        functools.partial(lift_body, rows, faces),
        grid=(all_rows,),
        in_specs=[
            smem,
            whole(x.shape),
            whole(c.shape),
            whole(prev_rows.shape),
            whole(next_rows.shape),
            whole(kernel_one.shape),
            whole(b1.shape),
            whole(k2t.shape),
        ]
        + [whole(part_shape)] * faces,
        out_specs=[row_block(lifted)] * 2,
        out_shape=[jax.ShapeDtypeStruct((all_rows, width, lifted), F32)] * 2,
        scratch_shapes=[
            pltpu.VMEM((2 * (rows + 2), width, 3 * channels), BF16),
            pltpu.VMEM((2 * (rows + 2), width, 3 * channels), BF16),
            pltpu.VMEM((2, 2 * GROUP, lifted), F32),
            pltpu.VMEM((2, 2 * GROUP, lifted), F32),
        ],
        compiler_params=params(),
        cost_estimate=cost(2 * conv_flops, 12 << 20),
        name="lift",
    )(matching, x, c, prev_rows, next_rows, kernel_one, b1, k2t, *parts)

    grown = (2, 2, 2 * GROUP, lifted)
    inner, grad_pre, up, down, edges_two = pl.pallas_call(
        functools.partial(gelu_body, rows, capacity),
        grid=(all_rows,),
        in_specs=[
            whole(received.shape),
            row_block(lifted),
            row_block(lifted),
            whole(kernel_two.shape),
            whole(k1t.shape),
        ],
        out_specs=[
            row_block(lifted),
            row_block(lifted),
            whole((4, width, channels)),
            whole((4, width, channels)),
            whole(grown),
        ],
        out_shape=[
            jax.ShapeDtypeStruct((all_rows, width, lifted), BF16),
            jax.ShapeDtypeStruct((all_rows, width, lifted), BF16),
            jax.ShapeDtypeStruct((4, width, channels), BF16),
            jax.ShapeDtypeStruct((4, width, channels), BF16),
            jax.ShapeDtypeStruct(grown, F32),
        ],
        scratch_shapes=[
            pltpu.VMEM((devices * capacity, 2 * 128), BF16),
            pltpu.VMEM((GROUP, devices * capacity), F32),
        ],
        compiler_params=params(),
        cost_estimate=cost(2 * all_rows * width * devices * capacity * lifted, 14 << 20),
        name="activate",
    )(received, pre, grad_inner, kernel_two, k1t)
    from_prev = lax.ppermute(up, "tile", forward)
    from_next = lax.ppermute(down, "tile", backward)
    parts_two = exchange(edges_two)

    ana, grad = pl.pallas_call(
        functools.partial(inside_body, rows),
        grid=(all_rows,),
        in_specs=[
            whole(inner.shape),
            whole(inner.shape),
            whole(kernel_two.shape),
            whole(k1t.shape),
        ],
        out_specs=[row_block(channels)] * 2,
        out_shape=[jax.ShapeDtypeStruct((all_rows, width, channels), F32)] * 2,
        scratch_shapes=[
            pltpu.VMEM((3 * lifted, 3 * channels), BF16),
            pltpu.VMEM((3 * lifted, 3 * channels), BF16),
        ],
        compiler_params=params(),
        cost_estimate=cost(2 * conv_flops, 10 << 20),
        name="inside",
    )(inner, grad_pre, kernel_two, k1t)

    side_shape = (2, 2, 2 * GROUP, channels)
    sides = pl.pallas_call(
        functools.partial(side_body, faces),
        in_specs=[smem] + [pl.BlockSpec(memory_space=pltpu.VMEM)] * (2 + faces),
        out_shape=jax.ShapeDtypeStruct(side_shape, F32),
        compiler_params=params(),
        cost_estimate=cost(0, 2 << 20),
        name="sides",
    )(matching, kernel_two, k1t, *parts_two)
    below = lax.ppermute(sides, "tile", forward)
    above = lax.ppermute(sides, "tile", backward)

    analysis, grad_state = pl.pallas_call(
        functools.partial(final_body, rows),
        grid=(all_rows,),
        in_specs=[
            row_block(channels),
            row_block(channels),
            row_block(channels),
            row_block(channels),
            whole(b2.shape),
            whole(up.shape),
            whole(up.shape),
            whole(up.shape),
            whole(side_shape),
            whole(side_shape),
            whole(side_shape),
        ],
        out_specs=[row_block(channels)] * 2,
        out_shape=[
            jax.ShapeDtypeStruct((all_rows, width, channels), BF16),
            jax.ShapeDtypeStruct((all_rows, width, channels), F32),
        ],
        scratch_shapes=[pltpu.VMEM((width, channels), F32)],
        compiler_params=params(),
        cost_estimate=cost(0, 12 << 20),
        name="final",
    )(x, c, ana, grad, b2, up, from_prev, from_next, sides, below, above)
    return analysis.reshape(state.shape), grad_state.reshape(cotangent.shape)


def solution(mesh):
    return jax.shard_map(
        per_device,
        mesh=mesh,
        in_specs=(
            P("face", "tile", None, None, None, None),
            P(("face", "tile"), None),
            P(("face", "tile"), None),
            P(("face", "tile")),
            P(),
            P(),
            P(),
            P(),
            P(),
            P("face", "tile", None, None, None, None),
        ),
        out_specs=(
            P("face", "tile", None, None, None, None),
            P("face", "tile", None, None, None, None),
        ),
        check_vma=False,
    )
```

profile of v0, /device:TPU:1, one launch (start us, length us, event | category | flops | bytes accessed | tf_op | source)
XLA Modules:
  0.0 115.1 jit_solution(2278941166841119534)
XLA Ops:
  3.0 3.1 %pack.1 = bf16[32,136,128]{2,1,0:T(8,128)(2,1)} custom-call(s32[1,1024]{1,0:T(1,128)S(1)} %bitcast.25, s32[1,1024]{1,0:T(1,128)S(1)} %bitcast.26, bf16[1024,256]{1,0:T(8,128)(2,1)S(1)} %copy-done.11), custom_call_target="tpu_custom_call" | custom-call | flops 1073741824 | bytes 2097152 | tf_op jit(solution)/shard_map/pack/pallas_call | solution.py:402
  6.1 7.1 %all-to-all-start = ((bf16[32,136,128]{2,1,0:T(8,128)(2,1)}), bf16[32,136,128]{2,1,0:T(8,128)(2,1)}, u32[]{:S(2)}, u32[]{:S(2)}) async-start(bf16[32,136,128]{2,1,0:T(8,128)(2,1)} %pack.1), calls=%async_computation | async-start | bytes 2228224 | tf_op jit(solution)/shard_map/all_to_all | solution.py:409
  13.4 3.5 %collective-permute-start = (bf16[4,512,128]{2,1,0:T(8,128)(2,1)S(1)}, bf16[4,512,128]{2,1,0:T(8,128)(2,1)S(1)}, u32[]{:S(2)}, u32[]{:S(2)}) collective-permute-start(bf16[4,512,128]{2,1,0:T(8,128)(2,1)S(1)} %pad_maximum_fusion), channel_id=1, source_target_pairs={{0,1},{1,2},{2,3},{3,4},{4,5},{5,6},{6,7},{8,9},{9,10},{10,11},{11... | collective-permute-start | bytes 1572872 | tf_op jit(solution)/shard_map/ppermute | solution.py:399
  17.0 2.1 %collective-permute-start.1 = (bf16[4,512,128]{2,1,0:T(8,128)(2,1)S(1)}, bf16[4,512,128]{2,1,0:T(8,128)(2,1)S(1)}, u32[]{:S(2)}, u32[]{:S(2)}) collective-permute-start(bf16[4,512,128]{2,1,0:T(8,128)(2,1)S(1)} %pad_maximum_fusion.1), channel_id=1, source_target_pairs={{1,0},{2,1},{3,2},{4,3},{5,4},{6,5},{7,6},{9,8},{10,9},{11,10},{12... | collective-permute-start | bytes 1572872 | tf_op jit(solution)/shard_map/ppermute | solution.py:400
  19.1 10.4 %collective-permute-done.p_lo.p_hi.prev_ref = bf16[4,512,128]{2,1,0:T(8,128)(2,1)S(1)} collective-permute-done((bf16[4,512,128]{2,1,0:T(8,128)(2,1)S(1)}, bf16[4,512,128]{2,1,0:T(8,128)(2,1)S(1)}, u32[]{:S(2)}, u32[]{:S(2)}) %collective-permute-start) | collective-permute-done | bytes 524320 | tf_op jit(solution)/shard_map/ppermute | solution.py:399
  29.5 9.2 %collective-permute-done.1.n_lo.n_hi.next_ref = bf16[4,512,128]{2,1,0:T(8,128)(2,1)S(1)} collective-permute-done((bf16[4,512,128]{2,1,0:T(8,128)(2,1)S(1)}, bf16[4,512,128]{2,1,0:T(8,128)(2,1)S(1)}, u32[]{:S(2)}, u32[]{:S(2)}) %collective-permute-start.1) | collective-permute-done | bytes 524320 | tf_op jit(solution)/shard_map/ppermute | solution.py:400
  39.5 3.9 %collective-permute-start.3 = (f32[2,2,16,128]{3,2,1,0:T(8,128)S(1)}, f32[2,2,16,128]{3,2,1,0:T(8,128)S(1)}, u32[]{:S(2)}, u32[]{:S(2)}) collective-permute-start(f32[2,2,16,128]{3,2,1,0:T(8,128)S(1)} %edges.1.rest_0_), channel_id=1, source_target_pairs={{16,0},{24,8},{0,16},{8,24},{17,1},{25,9},{1,17},{9,25},{18,2},{26... | collective-permute-start | bytes 98312 | tf_op jit(solution)/shard_map/ppermute | solution.py:415
  43.4 1.1 collective-permute-start.2
  44.5 1.4 %copy.14 = bf16[9,128,256]{1,2,0:T(8,128)(2,1)S(1)} copy(bf16[9,128,256]{2,1,0:T(8,128)(2,1)} %k1_ref.1) | data formatting | bytes 1179648 | tf_op args[5]
  45.9 1.1 copy.12
  49.1 1.1 copy-done.8
  51.2 11.8 %lift.1 = (f32[8,512,256]{2,1,0:T(8,128)}, f32[8,512,256]{2,1,0:T(8,128)}) custom-call(s32[4,2,3]{2,1,0:T(2,128)S(1)} %copy.13.matching_ref, bf16[8,512,128]{2,1,0:T(8,128)(2,1)S(1)} %bitcast.13, bf16[8,512,128]{2,1,0:T(8,128)(2,1)S(1)} %bitcast.18, bf16[4,512,128]{2,1,0:T(8,128)(2,1)S(1)} %copy-done.4, bf16[4,512,128]{2,1,0:T(8,128)(2,1)S(1)} %copy-done.6, ...), custom_call_target="tpu_custom_call" | custom-call | flops 4831838208 | bytes 12582912 | tf_op jit(solution)/shard_map/lift/pallas_call | solution.py:442
  63.1 12.8 %activate.1 = (bf16[8,512,256]{2,1,0:T(8,128)(2,1)S(1)}, bf16[8,512,256]{2,1,0:T(8,128)(2,1)}, bf16[4,512,128]{2,1,0:T(8,128)(2,1)S(1)}, bf16[4,512,128]{2,1,0:T(8,128)(2,1)S(1)}, f32[2,2,16,256]{3,2,1,0:T(8,128)S(1)}) custom-call(bf16[32,136,128]{2,1,0:T(8,128)(2,1)} %all-to-all-done.recv_ref, f32[8,512,256]{2,1,0:T(8,128)} %get-tuple-element.13.pre_ref, ...), custom_call_target="tpu_custom_call" | custom-call | flops 4294967296 | bytes 14680064 | tf_op jit(solution)/shard_map/activate/pallas_call | solution.py:470
  75.9 1.3 %copy-done.15 = bf16[8,512,256]{2,1,0:T(8,128)(2,1)} copy-done((bf16[8,512,256]{2,1,0:T(8,128)(2,1)}, bf16[8,512,256]{2,1,0:T(8,128)(2,1)S(1)}, u32[]{:S(2)}) %copy-start.15) | copy-done | bytes 2097176
  77.2 1.9 %collective-permute-start.6 = (bf16[4,512,128]{2,1,0:T(8,128)(2,1)S(1)}, bf16[4,512,128]{2,1,0:T(8,128)(2,1)S(1)}, u32[]{:S(2)}, u32[]{:S(2)}) collective-permute-start(bf16[4,512,128]{2,1,0:T(8,128)(2,1)S(1)} %get-tuple-element.20), channel_id=1, source_target_pairs={{1,0},{2,1},{3,2},{4,3},{5,4},{6,5},{7,6},{9,8},{10,9},{11,10},{12... | collective-permute-start | bytes 1572872 | tf_op jit(solution)/shard_map/ppermute | solution.py:503
  79.1 3.6 %collective-permute-start.5 = (bf16[4,512,128]{2,1,0:T(8,128)(2,1)S(1)}, bf16[4,512,128]{2,1,0:T(8,128)(2,1)S(1)}, u32[]{:S(2)}, u32[]{:S(2)}) collective-permute-start(bf16[4,512,128]{2,1,0:T(8,128)(2,1)S(1)} %get-tuple-element.19.up_ref), channel_id=1, source_target_pairs={{0,1},{1,2},{2,3},{3,4},{4,5},{5,6},{6,7},{8,9},{9,10},{10,11},{11... | collective-permute-start | bytes 1572872 | tf_op jit(solution)/shard_map/ppermute | solution.py:502
  83.2 1.9 %collective-permute-start.8 = (f32[2,2,16,256]{3,2,1,0:T(8,128)S(1)}, f32[2,2,16,256]{3,2,1,0:T(8,128)S(1)}, u32[]{:S(2)}, u32[]{:S(2)}) collective-permute-start(f32[2,2,16,256]{3,2,1,0:T(8,128)S(1)} %get-tuple-element.21.rest_0_), channel_id=1, source_target_pairs={{16,0},{24,8},{0,16},{8,24},{17,1},{25,9},{1,17},{9,25},{18,2},{26... | collective-permute-start | bytes 196616 | tf_op jit(solution)/shard_map/ppermute | solution.py:415
  86.1 2.4 %collective-permute-done.9.rest_3_ = f32[2,2,16,256]{3,2,1,0:T(8,128)S(1)} collective-permute-done((f32[2,2,16,256]{3,2,1,0:T(8,128)S(1)}, f32[2,2,16,256]{3,2,1,0:T(8,128)S(1)}, u32[]{:S(2)}, u32[]{:S(2)}) %collective-permute-start.9) | collective-permute-done | bytes 65568 | tf_op jit(solution)/shard_map/ppermute | solution.py:415
  88.5 2.1 %collective-permute-done.8.rest_2_ = f32[2,2,16,256]{3,2,1,0:T(8,128)S(1)} collective-permute-done((f32[2,2,16,256]{3,2,1,0:T(8,128)S(1)}, f32[2,2,16,256]{3,2,1,0:T(8,128)S(1)}, u32[]{:S(2)}, u32[]{:S(2)}) %collective-permute-start.8) | collective-permute-done | bytes 65568 | tf_op jit(solution)/shard_map/ppermute | solution.py:415
  91.4 2.1 %collective-permute-start.11 = (f32[2,2,16,128]{3,2,1,0:T(8,128)S(1)}, f32[2,2,16,128]{3,2,1,0:T(8,128)S(1)}, u32[]{:S(2)}, u32[]{:S(2)}) collective-permute-start(f32[2,2,16,128]{3,2,1,0:T(8,128)S(1)} %sides.1.own_ref), channel_id=1, source_target_pairs={{1,0},{2,1},{3,2},{4,3},{5,4},{6,5},{7,6},{9,8},{10,9},{11,10},{12... | collective-permute-start | bytes 98312 | tf_op jit(solution)/shard_map/ppermute | solution.py:536
  93.5 3.5 %collective-permute-start.10 = (f32[2,2,16,128]{3,2,1,0:T(8,128)S(1)}, f32[2,2,16,128]{3,2,1,0:T(8,128)S(1)}, u32[]{:S(2)}, u32[]{:S(2)}) collective-permute-start(f32[2,2,16,128]{3,2,1,0:T(8,128)S(1)} %sides.1.own_ref), channel_id=1, source_target_pairs={{0,1},{1,2},{2,3},{3,4},{4,5},{5,6},{6,7},{8,9},{9,10},{10,11},{11... | collective-permute-start | bytes 98312 | tf_op jit(solution)/shard_map/ppermute | solution.py:535
  97.0 10.5 %inside.1 = (f32[8,512,128]{2,1,0:T(8,128)S(1)}, f32[8,512,128]{2,1,0:T(8,128)S(1)}) custom-call(bf16[8,512,256]{2,1,0:T(8,128)(2,1)} %copy-done.15, bf16[8,512,256]{2,1,0:T(8,128)(2,1)} %get-tuple-element.16.gp_ref, bf16[9,256,128]{2,1,0:T(8,128)(2,1)S(1)} %copy-done.2, bf16[9,256,128]{2,1,0:T(8,128)(2,1)S(1)} %bitcast.22), custom_call_target="tpu_custom_call" | custom-call | flops 4831838208 | bytes 10485760 | tf_op jit(solution)/shard_map/inside/pallas_call | solution.py:506
  107.5 1.3 %copy-done.7 = f32[8,512,128]{2,1,0:T(8,128)} copy-done((f32[8,512,128]{2,1,0:T(8,128)}, f32[8,512,128]{2,1,0:T(8,128)S(1)}, u32[]{:S(2)}) %copy-start.7) | copy-done | bytes 2097176
  108.9 6.2 %final.1 = (bf16[8,512,128]{2,1,0:T(8,128)(2,1)}, f32[8,512,128]{2,1,0:T(8,128)}) custom-call(bf16[8,512,128]{2,1,0:T(8,128)(2,1)S(1)} %bitcast.14, bf16[8,512,128]{2,1,0:T(8,128)(2,1)S(1)} %bitcast.19, f32[8,512,128]{2,1,0:T(8,128)S(1)} %get-tuple-element.17.ana_ref, f32[8,512,128]{2,1,0:T(8,128)} %copy-done.7, f32[1,128]{1,0:T(1,128)S(1)} %bitcast.24, ...), custom_call_target="tpu_custom_call" | custom-call | bytes 12582912 | tf_op jit(solution)/shard_map/final/pallas_call | solution.py:538
  (49 shorter events, 8.9 us)
Async XLA Ops:
  6.1 7.2 %copy-start = (bf16[1,1,2,4,512,128]{5,4,3,2,1,0:T(8,128)(2,1)S(1)}, bf16[1,1,2,4,512,128]{5,4,3,2,1,0:T(8,128)(2,1)}, u32[]{:S(2)}) copy-start(bf16[1,1,2,4,512,128]{5,4,3,2,1,0:T(8,128)(2,1)} %param.10) | copy-start | bytes 3145732
  6.1 7.2 %copy-start.1 = (bf16[1,1,2,4,512,128]{5,4,3,2,1,0:T(8,128)(2,1)S(1)}, bf16[1,1,2,4,512,128]{5,4,3,2,1,0:T(8,128)(2,1)}, u32[]{:S(2)}) copy-start(bf16[1,1,2,4,512,128]{5,4,3,2,1,0:T(8,128)(2,1)} %param.19) | copy-start | bytes 3145732
  6.1 56.9 %all-to-all-start = ((bf16[32,136,128]{2,1,0:T(8,128)(2,1)}), bf16[32,136,128]{2,1,0:T(8,128)(2,1)}, u32[]{:S(2)}, u32[]{:S(2)}) async-start(bf16[32,136,128]{2,1,0:T(8,128)(2,1)} %pack.1), calls=%async_computation | async-start | bytes 2228224 | tf_op jit(solution)/shard_map/all_to_all | solution.py:409
  13.4 16.1 %collective-permute-start = (bf16[4,512,128]{2,1,0:T(8,128)(2,1)S(1)}, bf16[4,512,128]{2,1,0:T(8,128)(2,1)S(1)}, u32[]{:S(2)}, u32[]{:S(2)}) collective-permute-start(bf16[4,512,128]{2,1,0:T(8,128)(2,1)S(1)} %pad_maximum_fusion), channel_id=1, source_target_pairs={{0,1},{1,2},{2,3},{3,4},{4,5},{5,6},{6,7},{8,9},{9,10},{10,11},{11... | collective-permute-start | bytes 1572872 | tf_op jit(solution)/shard_map/ppermute | solution.py:399
  17.0 27.4 %copy-start.16 = (s32[4,2,3]{0,1,2:T(2,128)S(1)}, s32[4,2,3]{0,1,2:T(2,128)}, u32[]{:S(2)}) copy-start(s32[4,2,3]{0,1,2:T(2,128)} %param.14) | copy-start | bytes 292
  17.0 28.9 %copy-start.2 = (bf16[9,256,128]{2,1,0:T(8,128)(2,1)S(1)}, bf16[9,256,128]{2,1,0:T(8,128)(2,1)}, u32[]{:S(2)}) copy-start(bf16[9,256,128]{2,1,0:T(8,128)(2,1)} %k2_ref.5) | copy-start | bytes 1769476
  17.0 21.6 %collective-permute-start.1 = (bf16[4,512,128]{2,1,0:T(8,128)(2,1)S(1)}, bf16[4,512,128]{2,1,0:T(8,128)(2,1)S(1)}, u32[]{:S(2)}, u32[]{:S(2)}) collective-permute-start(bf16[4,512,128]{2,1,0:T(8,128)(2,1)S(1)} %pad_maximum_fusion.1), channel_id=1, source_target_pairs={{1,0},{2,1},{3,2},{4,3},{5,4},{6,5},{7,6},{9,8},{10,9},{11,10},{12... | collective-permute-start | bytes 1572872 | tf_op jit(solution)/shard_map/ppermute | solution.py:400
  29.5 9.2 %copy-start.3 = (bf16[4,512,128]{2,1,0:T(8,128)(2,1)}, bf16[4,512,128]{2,1,0:T(8,128)(2,1)S(1)}, u32[]{:S(2)}) copy-start(bf16[4,512,128]{2,1,0:T(8,128)(2,1)S(1)} %collective-permute-done.p_lo.p_hi.prev_ref) | copy-start | bytes 1572868
  39.5 7.5 %copy-start.14 = (f32[256]{0:T(256)S(1)}, f32[256]{0:T(256)}, u32[]{:S(2)}) copy-start(f32[256]{0:T(256)} %param.16) | copy-start | bytes 3076
  39.5 7.5 %collective-permute-start.4 = (f32[2,2,16,128]{3,2,1,0:T(8,128)S(1)}, f32[2,2,16,128]{3,2,1,0:T(8,128)S(1)}, u32[]{:S(2)}, u32[]{:S(2)}) collective-permute-start(f32[2,2,16,128]{3,2,1,0:T(8,128)S(1)} %edges.1.rest_0_), channel_id=1, source_target_pairs={{24,0},{0,8},{8,16},{16,24},{25,1},{1,9},{9,17},{17,25},{26,2},{2,... | collective-permute-start | bytes 98312 | tf_op jit(solution)/shard_map/ppermute | solution.py:415
  39.5 7.5 %collective-permute-start.3 = (f32[2,2,16,128]{3,2,1,0:T(8,128)S(1)}, f32[2,2,16,128]{3,2,1,0:T(8,128)S(1)}, u32[]{:S(2)}, u32[]{:S(2)}) collective-permute-start(f32[2,2,16,128]{3,2,1,0:T(8,128)S(1)} %edges.1.rest_0_), channel_id=1, source_target_pairs={{16,0},{24,8},{0,16},{8,24},{17,1},{25,9},{1,17},{9,25},{18,2},{26... | collective-permute-start | bytes 98312 | tf_op jit(solution)/shard_map/ppermute | solution.py:415
  43.4 3.6 %collective-permute-start.2 = (f32[2,2,16,128]{3,2,1,0:T(8,128)S(1)}, f32[2,2,16,128]{3,2,1,0:T(8,128)S(1)}, u32[]{:S(2)}, u32[]{:S(2)}) collective-permute-start(f32[2,2,16,128]{3,2,1,0:T(8,128)S(1)} %edges.1.rest_0_), channel_id=1, source_target_pairs={{8,0},{16,8},{24,16},{0,24},{9,1},{17,9},{25,17},{1,25},{10,2},{18... | collective-permute-start | bytes 98312 | tf_op jit(solution)/shard_map/ppermute | solution.py:415
  49.1 1.1 copy-start.8
  50.1 1.1 copy-start.9
  75.9 1.3 %copy-start.15 = (bf16[8,512,256]{2,1,0:T(8,128)(2,1)}, bf16[8,512,256]{2,1,0:T(8,128)(2,1)S(1)}, u32[]{:S(2)}) copy-start(bf16[8,512,256]{2,1,0:T(8,128)(2,1)S(1)} %get-tuple-element.15.inner_ref) | copy-start | bytes 6291460
  77.2 31.6 %collective-permute-start.6 = (bf16[4,512,128]{2,1,0:T(8,128)(2,1)S(1)}, bf16[4,512,128]{2,1,0:T(8,128)(2,1)S(1)}, u32[]{:S(2)}, u32[]{:S(2)}) collective-permute-start(bf16[4,512,128]{2,1,0:T(8,128)(2,1)S(1)} %get-tuple-element.20), channel_id=1, source_target_pairs={{1,0},{2,1},{3,2},{4,3},{5,4},{6,5},{7,6},{9,8},{10,9},{11,10},{12... | collective-permute-start | bytes 1572872 | tf_op jit(solution)/shard_map/ppermute | solution.py:503
  79.1 29.7 %collective-permute-start.5 = (bf16[4,512,128]{2,1,0:T(8,128)(2,1)S(1)}, bf16[4,512,128]{2,1,0:T(8,128)(2,1)S(1)}, u32[]{:S(2)}, u32[]{:S(2)}) collective-permute-start(bf16[4,512,128]{2,1,0:T(8,128)(2,1)S(1)} %get-tuple-element.19.up_ref), channel_id=1, source_target_pairs={{0,1},{1,2},{2,3},{3,4},{4,5},{5,6},{6,7},{8,9},{9,10},{10,11},{11... | collective-permute-start | bytes 1572872 | tf_op jit(solution)/shard_map/ppermute | solution.py:502
  82.8 5.7 %collective-permute-start.9 = (f32[2,2,16,256]{3,2,1,0:T(8,128)S(1)}, f32[2,2,16,256]{3,2,1,0:T(8,128)S(1)}, u32[]{:S(2)}, u32[]{:S(2)}) collective-permute-start(f32[2,2,16,256]{3,2,1,0:T(8,128)S(1)} %get-tuple-element.21.rest_0_), channel_id=1, source_target_pairs={{24,0},{0,8},{8,16},{16,24},{25,1},{1,9},{9,17},{17,25},{26,2},{2,... | collective-permute-start | bytes 196616 | tf_op jit(solution)/shard_map/ppermute | solution.py:415
  83.2 7.4 %collective-permute-start.8 = (f32[2,2,16,256]{3,2,1,0:T(8,128)S(1)}, f32[2,2,16,256]{3,2,1,0:T(8,128)S(1)}, u32[]{:S(2)}, u32[]{:S(2)}) collective-permute-start(f32[2,2,16,256]{3,2,1,0:T(8,128)S(1)} %get-tuple-element.21.rest_0_), channel_id=1, source_target_pairs={{16,0},{24,8},{0,16},{8,24},{17,1},{25,9},{1,17},{9,25},{18,2},{26... | collective-permute-start | bytes 196616 | tf_op jit(solution)/shard_map/ppermute | solution.py:415
  85.1 5.5 %collective-permute-start.7 = (f32[2,2,16,256]{3,2,1,0:T(8,128)S(1)}, f32[2,2,16,256]{3,2,1,0:T(8,128)S(1)}, u32[]{:S(2)}, u32[]{:S(2)}) collective-permute-start(f32[2,2,16,256]{3,2,1,0:T(8,128)S(1)} %get-tuple-element.21.rest_0_), channel_id=1, source_target_pairs={{8,0},{16,8},{24,16},{0,24},{9,1},{17,9},{25,17},{1,25},{10,2},{18... | collective-permute-start | bytes 196616 | tf_op jit(solution)/shard_map/ppermute | solution.py:415
  91.4 17.4 %collective-permute-start.11 = (f32[2,2,16,128]{3,2,1,0:T(8,128)S(1)}, f32[2,2,16,128]{3,2,1,0:T(8,128)S(1)}, u32[]{:S(2)}, u32[]{:S(2)}) collective-permute-start(f32[2,2,16,128]{3,2,1,0:T(8,128)S(1)} %sides.1.own_ref), channel_id=1, source_target_pairs={{1,0},{2,1},{3,2},{4,3},{5,4},{6,5},{7,6},{9,8},{10,9},{11,10},{12... | collective-permute-start | bytes 98312 | tf_op jit(solution)/shard_map/ppermute | solution.py:536
  93.5 15.3 %collective-permute-start.10 = (f32[2,2,16,128]{3,2,1,0:T(8,128)S(1)}, f32[2,2,16,128]{3,2,1,0:T(8,128)S(1)}, u32[]{:S(2)}, u32[]{:S(2)}) collective-permute-start(f32[2,2,16,128]{3,2,1,0:T(8,128)S(1)} %sides.1.own_ref), channel_id=1, source_target_pairs={{0,1},{1,2},{2,3},{3,4},{4,5},{5,6},{6,7},{8,9},{9,10},{10,11},{11... | collective-permute-start | bytes 98312 | tf_op jit(solution)/shard_map/ppermute | solution.py:535
  97.0 11.9 %copy-start.10 = (f32[128]{0:T(128)S(1)}, f32[128]{0:T(128)}, u32[]{:S(2)}) copy-start(f32[128]{0:T(128)} %param.18) | copy-start | bytes 1540
  107.5 1.3 %copy-start.7 = (f32[8,512,128]{2,1,0:T(8,128)}, f32[8,512,128]{2,1,0:T(8,128)S(1)}, u32[]{:S(2)}) copy-start(f32[8,512,128]{2,1,0:T(8,128)S(1)} %get-tuple-element.18.grad_ref) | copy-start | bytes 6291460
  (6 other events, 5.3 us)
where the time goes:
time: 116 us; the launch traced here: 115 us
  Pallas kernels  45.2 us (39%)
  starting transfers between devices  32.1 us (28%)
  waiting for transfers between devices  24.1 us (21%)
  local copies, waits for them, and re-layouts  12.7 us (11%)
    pallas_call x1, Pallas kernels, per_device(): pl.pallas_call(functools.partial(gelu_body, rows, capacity), grid=(all_ro...  12.8 us
    unnamed x37, local copies, waits for them, and re-layouts  12.6 us
    pallas_call x1, Pallas kernels, per_device(): pl.pallas_call(functools.partial(lift_body, rows, faces), grid=(all_rows,...  11.8 us
    pallas_call x1, Pallas kernels, per_device(): pl.pallas_call(functools.partial(inside_body, rows), grid=(all_rows,), in...  10.5 us
    ppermute x1, waiting for transfers between devices, per_device(): prev_rows = lax.ppermute(up_rows, 'tile', forward)  10.4 us
    ppermute x1, waiting for transfers between devices, per_device(): next_rows = lax.ppermute(down_rows, 'tile', backward)  9.17 us
    ppermute x6, starting transfers between devices, exchange(): lax.ppermute(own, 'face', [((i + k) % faces, i) for i in range(faces)])  8.25 us
    all_to_all x1, starting transfers between devices, per_device(): received = lax.all_to_all(packed, ('face', 'tile'), 0, 0, tiled=True)  7.14 us
  transfers between devices with their start and end apart: 13, of which 4 were waited for; matrix products, arithmetic and copies ran while one was open for 2% of the time, Pallas kernels for 20%

commit v1 on v0

v1 whole, which is shorter than its diff:
```python
import functools
import math

import jax
import jax.numpy as jnp
from jax import lax
from jax.experimental import pallas as pl
from jax.experimental.pallas import tpu as pltpu
from jax.sharding import PartitionSpec as P

F32 = jnp.float32
BF16 = jnp.bfloat16
GROUP = 8
HIGH = 64
PIXEL_ROWS = 8
ROOT = math.sqrt(2.0 / math.pi)
CUBIC = 0.044715


def params(mib=24):
    return pltpu.CompilerParams(vmem_limit_bytes=mib << 20)


def cost(flops, nbytes):
    return pl.CostEstimate(flops=int(flops), bytes_accessed=int(nbytes), transcendentals=0)


def hold(shape, kind):
    return pltpu.VMEM(shape, kind)


def held(array):
    return pltpu.with_memory_space_constraint(array, pltpu.VMEM)


def far(array):
    return pltpu.with_memory_space_constraint(array, pltpu.HBM)


def fixed(shape):
    return pl.BlockSpec(shape, lambda *_: (0,) * len(shape))


def dot(a, b):
    return jnp.dot(a, b, preferred_element_type=F32)


def matched(matching_ref, side, faces):
    face = lax.axis_index("face")
    partner = matching_ref[face, side, 0]
    return lax.rem(partner - face + faces, faces), matching_ref[face, side, 1], matching_ref[face, side, 2]


def partner_rows(part_refs, array, hop, their_side, flipped):
    rows = None
    for k, ref in enumerate(part_refs):
        mine = jnp.where(their_side == 1, ref[array, 1], ref[array, 0])
        rows = mine if rows is None else jnp.where(hop == k, mine, rows)
    swapped = jnp.concatenate([rows[GROUP:], rows[:GROUP]], axis=0)
    return jnp.where(flipped == 1, swapped, rows)


def rolled_rows(rows, step):
    first, second = rows[:GROUP], rows[GROUP:]
    if step:
        first = pltpu.roll(first, (-step) % GROUP, 0)
        second = pltpu.roll(second, step % GROUP, 0)
    return jnp.concatenate([first, second], axis=0).astype(BF16)


def side_forward(rows, side, taps_ref):
    lhs = jnp.concatenate([rolled_rows(rows, dy) for dy in (-1, 0, 1)], axis=1)
    taps = jnp.concatenate([taps_ref[3 * row + 2 * side] for row in range(3)], axis=0)
    return dot(lhs, taps)


def side_adjoint(rows, their_side, flipped, taps_ref):
    lhs = jnp.concatenate([rolled_rows(rows, -dy) for dy in (-1, 0, 1)], axis=1)
    order = [jnp.where(flipped == 1, 2 - row, row) for row in range(3)]
    taps = jnp.concatenate([taps_ref[3 * row + 2 * their_side] for row in order], axis=0)
    return dot(lhs, taps)


def shift_columns(values, step):
    count = values.shape[0]
    at = lax.broadcasted_iota(jnp.int32, values.shape, 0)
    moved = pltpu.roll(values, (-step) % count, 0)
    edge = count - 1 if step == 1 else 0
    return jnp.where(at == edge, 0.0, moved)


def spread_columns(row, order):
    wide = row.astype(F32)
    return jnp.concatenate(
        [row if s == 0 else shift_columns(wide, s).astype(BF16) for s in order], axis=1
    )


def add_edges(values, left, right):
    count = values.shape[0]
    at = lax.broadcasted_iota(jnp.int32, (GROUP, values.shape[1]), 0)
    first = values[:GROUP] + jnp.where(at == 0, left, 0.0)
    tail = values[count - GROUP :] + jnp.where(at == GROUP - 1, right, 0.0)
    return jnp.concatenate([first, values[GROUP : count - GROUP], tail], axis=0)


def pack_body(
    capacity, dest_in, pixel_in, values_in, out_hbm, dest_ref, pixel_ref, values_ref, out_ref, in_sem,
    out_sem,
):
    count = values_ref.shape[0]
    devices = out_ref.shape[0]
    block = 128
    loads = [
        pltpu.make_async_copy(source, target, in_sem.at[k])
        for k, (source, target) in enumerate(
            ((dest_in, dest_ref), (pixel_in, pixel_ref), (values_in, values_ref))
        )
    ]
    for load in loads:
        load.start()
    loads[0].wait()
    loads[1].wait()
    dest_row = dest_ref[...].astype(F32)
    pixel_row = pixel_ref[...]
    eye = lax.broadcasted_iota(jnp.int32, (block, block), 0) == lax.broadcasted_iota(
        jnp.int32, (block, block), 1
    )

    def column(row, start):
        piece = row[:, start : start + block]
        return jnp.sum(jnp.where(eye, piece, 0.0), axis=1, keepdims=True)

    high_row = lax.shift_right_logical(pixel_row, 6).astype(F32) + 1.0
    low_row = (pixel_row & (HIGH - 1)).astype(F32)
    own = lax.broadcasted_iota(jnp.int32, (block, count), 0)
    other = lax.broadcasted_iota(jnp.int32, (block, count), 1)
    lane = lax.broadcasted_iota(jnp.int32, (block, 128), 1)
    lane_rank = (lane & (HIGH - 1)).astype(F32)
    rank_row = jnp.zeros((1, count), F32)
    coded = []
    for start in range(0, count, block):
        same = column(dest_row, start) == dest_row
        later = (own + start) < other
        earlier = (own + start) > other
        rank_row = rank_row + jnp.sum(
            jnp.where(same & later, 1.0, 0.0), axis=0, keepdims=True
        )
        rank = jnp.sum(jnp.where(same & earlier, 1.0, 0.0), axis=1, keepdims=True)
        code = jnp.where(lane < HIGH, column(high_row, start), column(low_row, start))
        coded.append(jnp.where(rank == lane_rank, code, 0.0).astype(BF16))
    to_device = (
        lax.broadcasted_iota(jnp.int32, (devices, count), 0).astype(F32) == dest_row
    )
    pixels = dot(
        jnp.where(to_device, 1.0, 0.0).astype(BF16), jnp.concatenate(coded, axis=0)
    )
    out_ref[:, 2 * capacity :, :] = jnp.broadcast_to(
        pixels[:, None, :], (devices, PIXEL_ROWS, 128)
    ).astype(BF16)
    slot_row = dest_row * capacity + rank_row
    slots = 256
    per_block = slots // capacity
    loads[2].wait()
    values = values_ref[...]
    stores = []
    slot_at = lax.broadcasted_iota(jnp.int32, (slots, count), 0).astype(F32)
    for start in range(0, devices * capacity, slots):
        onehot = jnp.where(slot_at == slot_row - start, 1.0, 0.0).astype(BF16)
        rows = dot(onehot, values).astype(BF16)
        first = start // capacity
        for half in range(2):
            out_ref[first : first + per_block, half * capacity : (half + 1) * capacity, :] = (
                rows[:, half * 128 : (half + 1) * 128].reshape(per_block, capacity, 128)
            )
        store = pltpu.make_async_copy(
            out_ref.at[first : first + per_block],
            out_hbm.at[first : first + per_block],
            out_sem.at[len(stores)],
        )
        store.start()
        stores.append(store)
    for store in stores:
        store.wait()


def edge_body(rows, _, x_lo, x_hi, c_lo, c_hi, p_lo, p_hi, n_lo, n_hi, out_ref):
    tiles = lax.axis_size("tile")
    last = lax.axis_index("tile") == tiles - 1
    out_ref[...] = jnp.zeros_like(out_ref)
    for side in range(2):
        prev = (p_lo, p_hi)[side][...].astype(F32)
        after = (n_lo, n_hi)[side][...].astype(F32)
        at = 0 if side == 0 else prev.shape[1] - 1
        for array in range(2):
            own = ((x_lo, x_hi), (c_lo, c_hi))[array][side][...].astype(F32)
            for band in range(2):
                base = band * GROUP
                out_ref[array, side, base, :] = prev[2 * array + band, at]
                for r in range(rows):
                    out_ref[array, side, base + 1 + r, :] = own[band * rows + r, at]
                fold = own[(1 - band) * rows + rows - 1, at]
                out_ref[array, side, base + 1 + rows, :] = jnp.where(
                    last, fold, after[2 * array + band, at]
                )


def border_row(j, rows):
    return (j // 2) * rows + lax.rem(j, 2) * (rows - 1)


def lift_body(
    rows, x_ref, c_ref, k1_ref, b1_ref, k2_ref, pre_ref, grad_ref, k1t_ref, k2t_ref, k2t
):
    step = pl.program_id(0)
    band = step // rows
    r = lax.rem(step, rows)
    taps = k1_ref.shape[0] * x_ref.shape[2]
    lifted = k1_ref.shape[2]

    @pl.when(step == 0)
    def _():
        for t in range(k1_ref.shape[0]):
            k2t[t] = k2_ref[t].astype(F32).T.astype(BF16)
            k1t_ref[t] = k1_ref[t].astype(F32).T.astype(BF16)
        k2t_ref[...] = k2t[...]

    for source, weights, order, way, out_ref in (
        (x_ref, k1_ref, (-1, 0, 1), 1 - 2 * band, pre_ref),
        (c_ref, k2t, (1, 0, -1), 2 * band - 1, grad_ref),
    ):
        pieces = []
        for dy in (-1, 0, 1):
            at = r + way * dy
            row = source[band * rows + jnp.clip(at, 0, rows - 1)]
            if dy:
                row = jnp.where((at >= 0) & (at < rows), row, jnp.zeros_like(row))
            pieces.append(spread_columns(row, order))
        total = dot(jnp.concatenate(pieces, axis=1), weights[...].reshape(taps, lifted))
        if out_ref is pre_ref:
            total = total + b1_ref[...]
        out_ref[0] = total


def side_in_body(faces, matching_ref, k1_ref, k2t_ref, *rest):
    parts = rest[:faces]
    x_side, c_side = rest[faces:]
    for side in range(2):
        hop, their_side, flipped = matched(matching_ref, side, faces)
        near = partner_rows(parts, 0, hop, their_side, flipped)
        x_side[side] = side_forward(near, side, k1_ref)
        near = partner_rows(parts, 1, hop, their_side, flipped)
        c_side[side] = side_adjoint(near, their_side, flipped, k2t_ref)


def gelu_pair(v, grad):
    square = v * v
    t = jnp.tanh(v * (ROOT + (ROOT * CUBIC) * square))
    half = 0.5 + 0.5 * t
    slope = half + (0.5 * v) * (1.0 - t * t) * (ROOT + (3.0 * ROOT * CUBIC) * square)
    return (v * half).astype(BF16), (grad * slope).astype(BF16)


def unpack_received(capacity, recv_ref, values, keys):
    devices = recv_ref.shape[0]
    slots = devices * capacity
    per_lane = 128 // capacity
    for half in range(2):
        values[:, half * 128 : (half + 1) * 128] = recv_ref[
            :, half * capacity : (half + 1) * capacity, :
        ].reshape(slots, 128)
    owner = lax.broadcasted_iota(jnp.int32, (PIXEL_ROWS, 128), 1) // capacity
    for start in range(0, devices, per_lane):
        key = jnp.zeros((PIXEL_ROWS, 128), F32)
        for k in range(per_lane):
            code = recv_ref[start + k, 2 * capacity :, :].astype(F32)
            mine = (code - 1.0) * HIGH + pltpu.roll(code, HIGH, 1)
            if k:
                mine = pltpu.roll(mine, k * capacity, 1)
            key = jnp.where(owner == k, mine, key)
        keys[:, start * capacity : start * capacity + 128] = key


def row_taps(taps_ref, row):
    return jnp.concatenate([taps_ref[3 * row + dx] for dx in range(3)], axis=1)


def merge_shifts(wide, forward):
    channels = wide.shape[1] // 3
    left, mid, right = (wide[:, k * channels : (k + 1) * channels] for k in range(3))
    step = -1 if forward else 1
    return mid + shift_columns(left, step) + shift_columns(right, -step)


def border_body(
    rows, capacity, recv_in, pre_in, grad_in, prev_in, next_in, x_in, c_in, k1_in, k2t_in, x_side,
    c_side, inner_ref, gp_ref, edge_ref, values, keys, recv_ref, base, outside, strips, k1_ref, k2t_ref,
    edge_sums, sem,
):
    width = base.shape[2]
    channels = outside.shape[3]
    last = lax.axis_index("tile") == lax.axis_size("tile") - 1
    at_row = [0, rows - 1, rows, 2 * rows - 1]
    loads = []

    def load(source, target):
        copy = pltpu.make_async_copy(source, target, sem.at[len(loads)])
        loads.append(copy)
        copy.start()

    load(recv_in, recv_ref)
    for array, own in enumerate((x_in, c_in)):
        for band in range(2):
            plane = 2 * array + band
            load(prev_in.at[plane], outside.at[array, 2 * band])
            target = outside.at[array, 2 * band + 1]
            after = pltpu.make_async_copy(next_in.at[plane], target, sem.at[len(loads)])
            fold = pltpu.make_async_copy(
                own.at[(1 - band) * rows + rows - 1], target, sem.at[len(loads)]
            )

            @pl.when(last)
            def _():
                fold.start()

            @pl.when(jnp.logical_not(last))
            def _():
                after.start()

            loads.append(after)
    load(k1_in, k1_ref)
    load(k2t_in, k2t_ref)
    for array, source in enumerate((pre_in, grad_in)):
        for j in range(4):
            load(source.at[at_row[j]], base.at[array, j])
    for array, source in enumerate((pre_in, grad_in)):
        for side in range(2):
            start = 0 if side == 0 else width - GROUP
            load(source.at[:, start : start + GROUP], strips.at[array, side])
    loads[0].wait()
    unpack_received(capacity, recv_ref, values, keys)
    for copy in loads[1:]:
        copy.wait()

    lifted = base.shape[3]
    column = lax.broadcasted_iota(jnp.int32, (width, keys.shape[1]), 0).astype(F32)
    kept = []
    for pair, dy in (((0, 3), -1), ((1, 2), 1)):
        totals = []
        for array, (weights, order, way) in enumerate(
            ((k1_ref, (-1, 0, 1), 1), (k2t_ref, (1, 0, -1), -1))
        ):
            lhs = jnp.concatenate([spread_columns(outside[array, j], order) for j in pair], axis=0)
            row = 3 * (way * dy + 1)
            tap = weights[row : row + 3].reshape(3 * channels, lifted)
            own = jnp.concatenate([base[array, j] for j in pair], axis=0)
            totals.append(own + dot(lhs, tap))
        onehot = jnp.concatenate(
            [
                jnp.where(column == keys[0:1, :] - float(at_row[j] * width), 1.0, 0.0).astype(BF16)
                for j in pair
            ],
            axis=0,
        )
        v = totals[0] + dot(onehot, values[...])
        for k, j in enumerate(pair):
            at = GROUP * (j // 2) + 1 + (rows - 1) * (j % 2)
            piece = slice(k * width, (k + 1) * width)
            inner, gp = gelu_pair(
                add_edges(v[piece], x_side[0, at : at + 1, :], x_side[1, at : at + 1, :]),
                add_edges(totals[1][piece], c_side[0, at : at + 1, :], c_side[1, at : at + 1, :]),
            )
            inner_ref[j] = inner
            gp_ref[j] = gp
            kept.append(at)

    count = 4 * GROUP
    for array, side_ref in enumerate((x_side, c_side)):
        edge_sums[array] = side_ref[...].reshape(count, lifted)
        for b in range(2):
            for r in range(1, rows - 1):
                for side in range(2):
                    at = 2 * GROUP * side + GROUP * b + r + 1
                    spot = 0 if side == 0 else GROUP - 1
                    edge_sums[array, at : at + 1, :] += strips[
                        array, side, b * rows + r, spot : spot + 1, :
                    ]
    at = lax.broadcasted_iota(jnp.int32, (count, 1), 0)
    e = at & (GROUP - 1)
    b = (at // GROUP) & 1
    side = at // (2 * GROUP)
    inside = (e >= 2) & (e < rows)
    pixel = (b * rows + e - 1) * width + side * (width - 1)
    wanted = jnp.where(inside, pixel, -1).astype(F32)
    onehot = jnp.where(keys[0:1, :] == wanted, 1.0, 0.0).astype(BF16)
    v = edge_sums[0] + dot(onehot, values[...])
    inner, gp = gelu_pair(v, edge_sums[1])
    shape = (2, 2 * GROUP, lifted)
    edge_ref[0] = jnp.where(inside, inner.astype(F32), 0.0).reshape(shape)
    edge_ref[1] = jnp.where(inside, gp.astype(F32), 0.0).reshape(shape)
    for array, ref in enumerate((inner_ref, gp_ref)):
        for j in range(4):
            at = GROUP * (j // 2) + 1 + (rows - 1) * (j % 2)
            edge_ref[array, 0, at : at + 1, :] = ref[j, :16].astype(F32)[0:1]
            edge_ref[array, 1, at : at + 1, :] = ref[j, width - 16 :].astype(F32)[15:16]


def send_body(rows, faces, matching_ref, inner_ref, gp_ref, k2_ref, k1t_ref, *rest):
    parts = rest[:faces]
    up_ref, down_ref, side_ref = rest[faces:]
    width = inner_ref.shape[1]
    for side in range(2):
        hop, their_side, flipped = matched(matching_ref, side, faces)
        near = partner_rows(parts, 0, hop, their_side, flipped)
        side_ref[0, side] = side_forward(near, side, k2_ref)
        near = partner_rows(parts, 1, hop, their_side, flipped)
        side_ref[1, side] = side_adjoint(near, their_side, flipped, k1t_ref)
    for array, (source, taps, first) in enumerate(((inner_ref, k2_ref, 2), (gp_ref, k1t_ref, 0))):
        for pair, tap in (((0, 3), first), ((1, 2), 2 - first)):
            lhs = jnp.concatenate([source[j] for j in pair], axis=0)
            wide = dot(lhs, row_taps(taps, tap))
            for k, j in enumerate(pair):
                part = merge_shifts(wide[k * width : (k + 1) * width], array == 0)
                corner = GROUP * (j // 2) + (rows + 1) * (j % 2)
                part = add_edges(
                    part,
                    side_ref[array, 0, corner : corner + 1, :],
                    side_ref[array, 1, corner : corner + 1, :],
                )
                target = up_ref if j % 2 else down_ref
                target[2 * array + j // 2] = part.astype(BF16)


def middle_body(rows, _, values, keys, *rest):
    middle = rows - 2
    pre_refs, grad_refs = rest[:middle], rest[middle : 2 * middle]
    x_side, c_side, inner_ref, gp_ref = rest[2 * middle :]
    band = pl.program_id(0)
    width, lifted = pre_refs[0].shape[1], pre_refs[0].shape[2]
    column = lax.broadcasted_iota(jnp.int32, (width, keys.shape[1]), 0).astype(F32)
    onehots = []
    for k in range(middle):
        local = keys[0:1, :] - ((band * rows + k + 1) * width).astype(F32)
        onehots.append(jnp.where(column == local, 1.0, 0.0).astype(BF16))
    found = dot(jnp.concatenate(onehots, axis=0), values[...])
    for k in range(middle):
        at = band * GROUP + k + 2
        inner, gp = gelu_pair(
            add_edges(
                pre_refs[k][0] + found[k * width : (k + 1) * width],
                x_side[0, pl.ds(at, 1), :],
                x_side[1, pl.ds(at, 1), :],
            ),
            add_edges(grad_refs[k][0], c_side[0, pl.ds(at, 1), :], c_side[1, pl.ds(at, 1), :]),
        )
        inner_ref[k] = inner
        gp_ref[k] = gp


def inside_body(
    rows, inner_b, gp_b, inner_m, gp_m, side_ref, k2_ref, k1t_ref, x_ref, c_ref, b2_ref, ana_ref,
    ana_b, out_grad, grad_b, w2, w1,
):
    step = pl.program_id(0)
    band = step // rows
    r = lax.rem(step, rows)
    middle = rows - 2
    lifted, channels = k2_ref.shape[1], k2_ref.shape[2]

    @pl.when(step == 0)
    def _():
        for taps, w, way in ((k2_ref, w2, 1), (k1t_ref, w1, -1)):
            for b in range(2):
                for offset in (-1, 0, 1):
                    dy = offset * way * (1 - 2 * b)
                    for dx in range(3):
                        w[
                            b,
                            (offset + 1) * lifted : (offset + 2) * lifted,
                            dx * channels : (dx + 1) * channels,
                        ] = taps[3 * (dy + 1) + dx]

    def finish(row):
        low = max(row - 1, 0)
        high = min(row + 1, rows - 1)
        at = band * GROUP + row + 1
        for array, (border, inner, w, own) in enumerate(
            ((inner_b, inner_m, w2, x_ref), (gp_b, gp_m, w1, c_ref))
        ):
            pieces = []
            for k in range(low, high + 1):
                if k == 0 or k == rows - 1:
                    pieces.append(border[2 * band + k // (rows - 1)])
                else:
                    pieces.append(inner[middle * band + k - 1])
            taps = w[band, (low - row + 1) * lifted : (high - row + 2) * lifted, :]
            total = merge_shifts(dot(jnp.concatenate(pieces, axis=1), taps), array == 0)
            total = add_edges(
                total + own[0].astype(F32),
                side_ref[array, 0, pl.ds(at, 1), :],
                side_ref[array, 1, pl.ds(at, 1), :],
            )
            if array == 0:
                total = total + b2_ref[...]
            if row == 0 or row == rows - 1:
                (ana_b, grad_b)[array][0] = total
            elif array == 0:
                ana_ref[0] = total.astype(BF16)
            else:
                out_grad[0] = total

    for row in range(rows):

        @pl.when(r == row)
        def _():
            finish(row)


def final_body(
    rows, ana_b, grad_b, _, __, up_ref, prev_ref, next_ref, out_ana, out_grad
):
    j = pl.program_id(0)
    band = j // 2
    bottom = lax.rem(j, 2)
    last = lax.axis_index("tile") == lax.axis_size("tile") - 1
    for array, (acc, out) in enumerate(((ana_b, out_ana), (grad_b, out_grad))):
        after = jnp.where(last, up_ref[2 * array + 1 - band], next_ref[2 * array + band])
        add = jnp.where(bottom == 1, after, prev_ref[2 * array + band])
        out[0] = (acc[0] + add.astype(F32)).astype(out.dtype)


def per_device(
    state,
    obs_values,
    obs_dest,
    obs_pixel,
    matching,
    kernel_one,
    bias_one,
    kernel_two,
    bias_two,
    cotangent,
):
    rows, width, channels = state.shape[3], state.shape[4], state.shape[5]
    lifted = kernel_one.shape[2]
    tiles, faces = lax.axis_size("tile"), lax.axis_size("face")
    devices = tiles * faces
    count = obs_values.shape[0]
    capacity = 2 * count // devices
    all_rows = 2 * rows
    middle = rows - 2
    chunk = 2 * capacity + PIXEL_ROWS
    x = state.reshape(all_rows, width, channels)
    c = cotangent.reshape(all_rows, width, channels)
    forward = [(i, i + 1) for i in range(tiles - 1)]
    backward = [(i + 1, i) for i in range(tiles - 1)]
    up_rows = jnp.concatenate([x[rows - 1 :: rows], c[rows - 1 :: rows]], axis=0)
    down_rows = jnp.concatenate([x[0::rows], c[0::rows]], axis=0)
    prev_rows = lax.ppermute(up_rows, "tile", forward)
    next_rows = lax.ppermute(down_rows, "tile", backward)
    strip = 16

    def ends(planes):
        return jnp.concatenate([planes[:, :strip], planes[:, width - strip :]], axis=1)

    prev_ends = lax.ppermute(ends(up_rows), "tile", forward)
    next_ends = lax.ppermute(ends(down_rows), "tile", backward)
    smem = pl.BlockSpec(memory_space=pltpu.SMEM)
    vmem = pl.BlockSpec(memory_space=pltpu.VMEM)
    hbm = pl.BlockSpec(memory_space=pl.ANY)

    def exchange(own):
        parts = [own]
        for k in range(1, faces):
            parts.append(
                lax.ppermute(own, "face", [((i + k) % faces, i) for i in range(faces)])
            )
        return parts

    packed = pl.pallas_call(
        functools.partial(pack_body, capacity),
        in_specs=[hbm] * 3,
        out_specs=hbm,
        out_shape=pltpu.HBM((devices, chunk, 128), BF16),
        scratch_shapes=[
            pltpu.VMEM((1, count), jnp.int32),
            pltpu.VMEM((1, count), jnp.int32),
            pltpu.VMEM((count, lifted), BF16),
            pltpu.VMEM((devices, chunk, 128), BF16),
            pltpu.SemaphoreType.DMA((3,)),
            pltpu.SemaphoreType.DMA((devices * capacity // 256,)),
        ],
        compiler_params=params(16),
        cost_estimate=cost(2 * devices * capacity * count * lifted, 2 << 20),
        name="pack",
    )(far(obs_dest.reshape(1, count)), far(obs_pixel.reshape(1, count)), far(obs_values))
    received = lax.all_to_all(packed, ("face", "tile"), 0, 0, tiled=True)

    b1 = bias_one.reshape(1, lifted)
    b2 = bias_two.reshape(1, channels)
    row_block = lambda n: pl.BlockSpec((1, width, n), lambda i: (i, 0, 0))
    edge_block = lambda n: pl.BlockSpec((1, width, n), lambda i: (border_row(i, rows), 0, 0))
    conv_flops = 2 * 9 * all_rows * width * channels * lifted
    pre, grad_inner, k1t, k2t = pl.pallas_call(
        functools.partial(lift_body, rows),
        grid=(all_rows,),
        in_specs=[
            fixed(x.shape), fixed(c.shape), fixed(kernel_one.shape), fixed(b1.shape),
            fixed(kernel_two.shape),
        ],
        out_specs=[row_block(lifted)] * 2
        + [fixed(kernel_two.shape), fixed(kernel_one.shape)],
        out_shape=[pltpu.HBM((all_rows, width, lifted), F32)] * 2
        + [pltpu.HBM(kernel_two.shape, BF16), pltpu.HBM(kernel_one.shape, BF16)],
        scratch_shapes=[pltpu.VMEM(kernel_one.shape, BF16)],
        compiler_params=params(),
        cost_estimate=cost(2 * conv_flops, 12 << 20),
        name="lift",
    )(x, c, kernel_one, b1, kernel_two)
    pre, grad_inner = far(pre), far(grad_inner)

    low = lambda n: pl.BlockSpec((n, strip, channels), lambda *_: (0, 0, 0))
    high = lambda n, at: pl.BlockSpec((n, strip, channels), lambda *_: (0, at, 0))
    tail = width // strip - 1
    edge_shape = (2, 2, 2 * GROUP, channels)
    edges = pl.pallas_call(
        functools.partial(edge_body, rows),
        grid=(1,),
        in_specs=[hbm] + [low(all_rows), high(all_rows, tail)] * 2 + [low(4), high(4, 1)] * 2,
        out_specs=fixed(edge_shape),
        out_shape=jax.ShapeDtypeStruct(edge_shape, F32),
        compiler_params=params(8),
        cost_estimate=cost(0, 1 << 18),
        name="edges",
    )(k1t, x, x, c, c, prev_ends, prev_ends, next_ends, next_ends)
    parts = exchange(edges)

    side_in = (2, 2 * GROUP, lifted)
    x_side, c_side = pl.pallas_call(
        functools.partial(side_in_body, faces),
        in_specs=[smem] + [vmem] * (2 + faces),
        out_specs=[vmem] * 2,
        out_shape=[jax.ShapeDtypeStruct(side_in, F32)] * 2,
        compiler_params=params(8),
        cost_estimate=cost(0, 2 << 20),
        name="sides_in",
    )(matching, kernel_one, k2t, *parts)
    plane = (4, width, channels)
    side_two = (2, 2, 2 * GROUP, lifted)
    slots = devices * capacity
    onehot_flops = 2 * width * slots * lifted
    other_block = pl.BlockSpec(
        (1, width, channels), lambda j: ((1 - j // 2) * rows + rows - 1, 0, 0)
    )
    border_shape = hold((4, width, lifted), BF16)
    border_shape = hold((4, width, lifted), BF16)
    inner_b, gp_b, edges_two, values, keys = pl.pallas_call(
        functools.partial(border_body, rows, capacity),
        in_specs=[hbm] * 9 + [vmem] * 2,
        out_specs=[vmem] * 5,
        out_shape=[
            border_shape,
            border_shape,
            jax.ShapeDtypeStruct(side_two, F32),
            hold((slots, lifted), BF16),
            hold((PIXEL_ROWS, slots), F32),
        ],
        scratch_shapes=[
            pltpu.VMEM(received.shape, BF16),
            pltpu.VMEM((2, 4, width, lifted), F32),
            pltpu.VMEM((2, 4, width, channels), BF16),
            pltpu.VMEM((2, 2, all_rows, GROUP, lifted), F32),
            pltpu.VMEM(kernel_one.shape, BF16),
            pltpu.VMEM(k2t.shape, BF16),
            pltpu.VMEM((2, 4 * GROUP, lifted), F32),
            pltpu.SemaphoreType.DMA((23,)),
        ],
        compiler_params=params(32),
        cost_estimate=cost(4 * onehot_flops + conv_flops // 6, 10 << 20),
        name="border",
    )(
        far(received), pre, grad_inner, far(prev_rows), far(next_rows), far(x), far(c),
        far(kernel_one), far(k2t), x_side, c_side,
    )
    inner_b, gp_b, values, keys = held(inner_b), held(gp_b), held(values), held(keys)
    parts_two = exchange(edges_two)

    side_out = (2, 2, 2 * GROUP, channels)
    up, down, sides = pl.pallas_call(
        functools.partial(send_body, rows, faces),
        in_specs=[smem] + [vmem] * (4 + faces),
        out_specs=[vmem] * 3,
        out_shape=[
            jax.ShapeDtypeStruct(plane, BF16),
            jax.ShapeDtypeStruct(plane, BF16),
            jax.ShapeDtypeStruct(side_out, F32),
        ],
        compiler_params=params(16),
        cost_estimate=cost(conv_flops // 6, 4 << 20),
        name="send",
    )(matching, inner_b, gp_b, kernel_two, k1t, *parts_two)
    from_prev = lax.ppermute(up, "tile", forward)
    from_next = lax.ppermute(down, "tile", backward)

    middle_block = lambda k: pl.BlockSpec((1, width, lifted), lambda i: (i * rows + k + 1, 0, 0))
    inner_m, gp_m = pl.pallas_call(
        functools.partial(middle_body, rows),
        grid=(2,),
        in_specs=[hbm, fixed(values.shape), fixed(keys.shape)]
        + [middle_block(k) for k in range(middle)] * 2
        + [fixed(side_in)] * 2,
        out_specs=[pl.BlockSpec((middle, width, lifted), lambda i: (i, 0, 0))] * 2,
        out_shape=[hold((2 * middle, width, lifted), BF16)] * 2,
        compiler_params=params(),
        cost_estimate=cost(2 * middle * onehot_flops, 10 << 20),
        name="middle",
    )(down, values, keys, *[pre] * middle, *[grad_inner] * middle, x_side, c_side)
    inner_m, gp_m = held(inner_m), held(gp_m)

    inner_block = lambda n: pl.BlockSpec(
        (1, width, n),
        lambda i: ((i // rows) * rows + jnp.clip(lax.rem(i, rows), 1, rows - 2), 0, 0),
    )
    held_block = pl.BlockSpec(
        (1, width, channels), lambda i: (2 * (i // rows) + lax.rem(i, rows) // (rows - 1), 0, 0)
    )
    analysis, ana_b, grad_state, grad_b = pl.pallas_call(
        functools.partial(inside_body, rows),
        grid=(all_rows,),
        in_specs=[
            fixed(inner_b.shape),
            fixed(gp_b.shape),
            fixed(inner_m.shape),
            fixed(gp_m.shape),
            fixed(side_out),
            fixed(kernel_two.shape),
            fixed(k1t.shape),
            row_block(channels),
            row_block(channels),
            fixed(b2.shape),
        ],
        out_specs=[inner_block(channels), held_block, inner_block(channels), held_block],
        out_shape=[
            pltpu.HBM((all_rows, width, channels), BF16),
            hold(plane, F32),
            pltpu.HBM((all_rows, width, channels), F32),
            hold(plane, F32),
        ],
        scratch_shapes=[pltpu.VMEM((2, 3 * lifted, 3 * channels), BF16)] * 2,
        compiler_params=params(),
        cost_estimate=cost(2 * conv_flops, 14 << 20),
        name="inside",
    )(inner_b, gp_b, inner_m, gp_m, sides, kernel_two, k1t, x, c, b2)
    ana_b, grad_b = held(ana_b), held(grad_b)

    analysis, grad_state = pl.pallas_call(
        functools.partial(final_body, rows),
        grid=(4,),
        in_specs=[row_block(channels)] * 2
        + [hbm] * 2
        + [fixed(plane)] * 3,
        out_specs=[edge_block(channels)] * 2,
        out_shape=[
            pltpu.HBM((all_rows, width, channels), BF16),
            pltpu.HBM((all_rows, width, channels), F32),
        ],
        input_output_aliases={2: 0, 3: 1},
        compiler_params=params(16),
        cost_estimate=cost(0, 6 << 20),
        name="final",
    )(ana_b, grad_b, far(analysis), far(grad_state), up, from_prev, from_next)
    return analysis.reshape(state.shape), grad_state.reshape(cotangent.shape)


def solution(mesh):
    return jax.shard_map(
        per_device,
        mesh=mesh,
        in_specs=(
            P("face", "tile", None, None, None, None),
            P(("face", "tile"), None),
            P(("face", "tile"), None),
            P(("face", "tile")),
            P(),
            P(),
            P(),
            P(),
            P(),
            P("face", "tile", None, None, None, None),
        ),
        out_specs=(
            P("face", "tile", None, None, None, None),
            P("face", "tile", None, None, None, None),
        ),
        check_vma=False,
    )
```

time: 116 us -> 86 us (0.74)
  waiting for transfers between devices: 24.1 us -> 7.63 us
  local copies, waits for them, and re-layouts: 12.7 us -> 1.31 us
  Pallas kernels: 45.2 us -> 39.1 us
  starting transfers between devices: 32.1 us -> 34.6 us
  other arithmetic: 0.1 us -> 1.71 us
    unnamed x37 -> x27, local copies, waits for them, and re-layouts: 12.6 us -> 1.23 us
    ppermute x1, waiting for transfers between devices: 10.4 us -> 0.01 us  [per_device(): prev_rows = lax.ppermute(up_rows, 'tile', forward)]
    ppermute x1, waiting for transfers between devices: 9.17 us -> 0.01 us  [per_device(): next_rows = lax.ppermute(down_rows, 'tile', backward)]
    pallas_call x6 -> x8, Pallas kernels: 34.8 us -> 30.6 us  [the longest x1 8.61 us: per_device(): pl.pallas_call(functools.partial(lift_body, rows), grid=(all_rows,), in_s...]
    pallas_call x1, Pallas kernels: 10.5 us -> 8.53 us  [per_device(): pl.pallas_call(functools.partial(inside_body, rows), grid=(all_rows,), in...]
    ppermute x6, waiting for transfers between devices: 4.53 us -> 6.11 us  [exchange(): lax.ppermute(own, 'face', [((i + k) % faces, i) for i in range(faces)])]
    ppermute x1, starting transfers between devices: 3.64 us -> 5.17 us  [per_device(): from_prev = lax.ppermute(up, 'tile', forward)]
    ppermute x2, waiting for transfers between devices: 0.01 us -> 1.51 us  [the longest x1 1.51 us: per_device(): next_ends = lax.ppermute(ends(down_rows), 'tile', backward)]
  transfers between devices with their start and end apart: 13 -> 13, of which waited for: 4 -> 7; matrix products, arithmetic and copies ran while one was open for 2% -> 2% of each run, Pallas kernels for 20% -> 27%
where the time goes in v1:
time: 86 us; the launch traced here: 85.3 us
  Pallas kernels  39.1 us (45%)
  starting transfers between devices  34.6 us (40%)
  waiting for transfers between devices  7.63 us (9%)
  other arithmetic  1.71 us (2%)
  local copies, waits for them, and re-layouts  1.31 us (2%)
  between operations  0.93 us (1%)
    ppermute x6, starting transfers between devices, exchange(): lax.ppermute(own, 'face', [((i + k) % faces, i) for i in range(faces)])  8.88 us
    pallas_call x1, Pallas kernels, per_device(): pl.pallas_call(functools.partial(lift_body, rows), grid=(all_rows,), in_s...  8.61 us
    pallas_call x1, Pallas kernels, per_device(): pl.pallas_call(functools.partial(inside_body, rows), grid=(all_rows,), in...  8.53 us
    pallas_call x1, Pallas kernels, per_device(): pl.pallas_call(functools.partial(border_body, rows, capacity), in_specs=[...  8.18 us
    all_to_all x1, starting transfers between devices, per_device(): received = lax.all_to_all(packed, ('face', 'tile'), 0, 0, tiled=True)  7.15 us
    ppermute x6, waiting for transfers between devices, exchange(): lax.ppermute(own, 'face', [((i + k) % faces, i) for i in range(faces)])  6.11 us
    ppermute x1, starting transfers between devices, per_device(): from_prev = lax.ppermute(up, 'tile', forward)  5.17 us
    pallas_call x1, Pallas kernels, per_device(): pl.pallas_call(functools.partial(middle_body, rows), grid=(2,), in_specs=...  5.16 us
  transfers between devices with their start and end apart: 13, of which 7 were waited for; matrix products, arithmetic and copies ran while one was open for 2% of the time, Pallas kernels for 27%

profile of v1, /device:TPU:1, one launch (start us, length us, event | category | flops | bytes accessed | tf_op | source)
XLA Modules:
  0.0 85.3 jit_solution(5892845149060871659)
XLA Ops:
  0.6 4.0 %pack.1 = bf16[32,136,128]{2,1,0:T(8,128)(2,1)} custom-call(s32[1,1024]{1,0:T(1,128)} %bitcast.24, s32[1,1024]{1,0:T(1,128)} %bitcast.25, bf16[1024,256]{1,0:T(8,128)(2,1)} %values_in.1), custom_call_target="tpu_custom_call" | custom-call | flops 1073741824 | bytes 2097152 | tf_op jit(solution)/shard_map/pack/pallas_call | solution.py:580
  4.6 7.2 %all-to-all-start = ((bf16[32,136,128]{2,1,0:T(8,128)(2,1)}), bf16[32,136,128]{2,1,0:T(8,128)(2,1)}, u32[]{:S(2)}, u32[]{:S(2)}) async-start(bf16[32,136,128]{2,1,0:T(8,128)(2,1)} %pack.1), calls=%async_computation | async-start | bytes 2228224 | tf_op jit(solution)/shard_map/all_to_all | solution.py:597
  11.9 3.7 %collective-permute-start.2 = (bf16[4,32,128]{2,1,0:T(8,128)(2,1)S(1)}, bf16[4,32,128]{2,1,0:T(8,128)(2,1)S(1)}, u32[]{:S(2)}, u32[]{:S(2)}) collective-permute-start(bf16[4,32,128]{2,1,0:T(8,128)(2,1)S(1)} %pad_maximum_fusion.2), channel_id=1, source_target_pairs={{0,1},{1,2},{2,3},{3,4},{4,5},{5,6},{6,7},{8,9},{9,10},{10,11},{11... | collective-permute-start | bytes 98312 | tf_op jit(solution)/shard_map/ppermute | solution.py:566
  15.6 0.8 pad_maximum_fusion.1
  16.5 1.9 %collective-permute-start.1 = (bf16[4,512,128]{2,1,0:T(8,128)(2,1)}, bf16[4,512,128]{2,1,0:T(8,128)(2,1)}, u32[]{:S(2)}, u32[]{:S(2)}) collective-permute-start(bf16[4,512,128]{2,1,0:T(8,128)(2,1)} %pad_maximum_fusion.1), channel_id=1, source_target_pairs={{1,0},{2,1},{3,2},{4,3},{5,4},{6,5},{7,6},{9,8},{10,9},{11,10},{12... | collective-permute-start | bytes 1572872 | tf_op jit(solution)/shard_map/ppermute | solution.py:560
  18.4 0.8 pad_maximum_fusion
  19.2 3.6 %collective-permute-start = (bf16[4,512,128]{2,1,0:T(8,128)(2,1)}, bf16[4,512,128]{2,1,0:T(8,128)(2,1)}, u32[]{:S(2)}, u32[]{:S(2)}) collective-permute-start(bf16[4,512,128]{2,1,0:T(8,128)(2,1)} %pad_maximum_fusion), channel_id=1, source_target_pairs={{0,1},{1,2},{2,3},{3,4},{4,5},{5,6},{6,7},{8,9},{9,10},{10,11},{11... | collective-permute-start | bytes 1572872 | tf_op jit(solution)/shard_map/ppermute | solution.py:559
  22.9 1.9 %collective-permute-start.3 = (bf16[4,32,128]{2,1,0:T(8,128)(2,1)S(1)}, bf16[4,32,128]{2,1,0:T(8,128)(2,1)S(1)}, u32[]{:S(2)}, u32[]{:S(2)}) collective-permute-start(bf16[4,32,128]{2,1,0:T(8,128)(2,1)S(1)} %pad_maximum_fusion.3), channel_id=1, source_target_pairs={{1,0},{2,1},{3,2},{4,3},{5,4},{6,5},{7,6},{9,8},{10,9},{11,10},{12... | collective-permute-start | bytes 98312 | tf_op jit(solution)/shard_map/ppermute | solution.py:567
  24.8 8.6 %lift.1 = (f32[8,512,256]{2,1,0:T(8,128)}, f32[8,512,256]{2,1,0:T(8,128)}, bf16[9,256,128]{2,1,0:T(8,128)(2,1)}, bf16[9,128,256]{2,1,0:T(8,128)(2,1)}) custom-call(bf16[8,512,128]{2,1,0:T(8,128)(2,1)S(1)} %bitcast.10, bf16[8,512,128]{2,1,0:T(8,128)(2,1)S(1)} %bitcast.16, bf16[9,128,256]{2,1,0:T(8,128)(2,1)S(1)} %copy-done.6, f32[1,256]{1,0:T(1,128)S(1)} %bitcast.20, ...), custom_call_target="tpu_custom_call" | custom-call | flops 4831838208 | bytes 12582912 | tf_op jit(solution)/shard_map/lift/pallas_call | solution.py:604
  33.5 1.5 %collective-permute-done.3.n_lo.n_hi = bf16[4,32,128]{2,1,0:T(8,128)(2,1)S(1)} collective-permute-done((bf16[4,32,128]{2,1,0:T(8,128)(2,1)S(1)}, bf16[4,32,128]{2,1,0:T(8,128)(2,1)S(1)}, u32[]{:S(2)}, u32[]{:S(2)}) %collective-permute-start.3) | collective-permute-done | bytes 32800 | tf_op jit(solution)/shard_map/ppermute | solution.py:567
  35.0 1.1 %copy-done.4 = bf16[9,256,128]{2,1,0:T(8,128)(2,1)S(1)} copy-done((bf16[9,256,128]{2,1,0:T(8,128)(2,1)S(1)}, bf16[9,256,128]{2,1,0:T(8,128)(2,1)}, u32[]{:S(2)}) %copy-start.4) | copy-done | bytes 589848
  36.1 1.5 %collective-permute-start.6 = (f32[2,2,16,128]{3,2,1,0:T(8,128)S(1)}, f32[2,2,16,128]{3,2,1,0:T(8,128)S(1)}, u32[]{:S(2)}, u32[]{:S(2)}) collective-permute-start(f32[2,2,16,128]{3,2,1,0:T(8,128)S(1)} %edges.1.rest_0_), channel_id=1, source_target_pairs={{24,0},{0,8},{8,16},{16,24},{25,1},{1,9},{9,17},{17,25},{26,2},{2,... | collective-permute-start | bytes 98312 | tf_op jit(solution)/shard_map/ppermute | solution.py:576
  37.6 3.7 %collective-permute-start.5 = (f32[2,2,16,128]{3,2,1,0:T(8,128)S(1)}, f32[2,2,16,128]{3,2,1,0:T(8,128)S(1)}, u32[]{:S(2)}, u32[]{:S(2)}) collective-permute-start(f32[2,2,16,128]{3,2,1,0:T(8,128)S(1)} %edges.1.rest_0_), channel_id=1, source_target_pairs={{16,0},{24,8},{0,16},{8,24},{17,1},{25,9},{1,17},{9,25},{18,2},{26... | collective-permute-start | bytes 98312 | tf_op jit(solution)/shard_map/ppermute | solution.py:576
  42.9 1.0 %collective-permute-done.4.rest_1_ = f32[2,2,16,128]{3,2,1,0:T(8,128)S(1)} collective-permute-done((f32[2,2,16,128]{3,2,1,0:T(8,128)S(1)}, f32[2,2,16,128]{3,2,1,0:T(8,128)S(1)}, u32[]{:S(2)}, u32[]{:S(2)}) %collective-permute-start.4) | collective-permute-done | bytes 32800 | tf_op jit(solution)/shard_map/ppermute | solution.py:576
  44.9 8.2 %border.1 = (bf16[4,512,256]{2,1,0:T(8,128)(2,1)S(1)}, bf16[4,512,256]{2,1,0:T(8,128)(2,1)S(1)}, f32[2,2,16,256]{3,2,1,0:T(8,128)S(1)}, bf16[2048,256]{1,0:T(8,128)(2,1)S(1)}, f32[8,2048]{1,0:T(8,128)S(1)}) custom-call(bf16[32,136,128]{2,1,0:T(8,128)(2,1)} %all-to-all-done.recv_in, f32[8,512,256]{2,1,0:T(8,128)} %get-tuple-element.24.pre_in.rest_0_.rest_1_, ...), custom_call_target="tpu_custom_call" | custom-call | flops 2550136832 | bytes 10485760 | tf_op jit(solution)/shard_map/border/pallas_call | solution.py:657
  53.2 2.4 %collective-permute-start.8 = (f32[2,2,16,256]{3,2,1,0:T(8,128)S(1)}, f32[2,2,16,256]{3,2,1,0:T(8,128)S(1)}, u32[]{:S(2)}, u32[]{:S(2)}) collective-permute-start(f32[2,2,16,256]{3,2,1,0:T(8,128)S(1)} %get-tuple-element.32.rest_0_), channel_id=1, source_target_pairs={{16,0},{24,8},{0,16},{8,24},{17,1},{25,9},{1,17},{9,25},{18,2},{26... | collective-permute-start | bytes 196616 | tf_op jit(solution)/shard_map/ppermute | solution.py:576
  56.4 1.8 %collective-permute-done.9.rest_3_ = f32[2,2,16,256]{3,2,1,0:T(8,128)S(1)} collective-permute-done((f32[2,2,16,256]{3,2,1,0:T(8,128)S(1)}, f32[2,2,16,256]{3,2,1,0:T(8,128)S(1)}, u32[]{:S(2)}, u32[]{:S(2)}) %collective-permute-start.9) | collective-permute-done | bytes 65568 | tf_op jit(solution)/shard_map/ppermute | solution.py:576
  58.2 1.3 %collective-permute-done.8.rest_2_ = f32[2,2,16,256]{3,2,1,0:T(8,128)S(1)} collective-permute-done((f32[2,2,16,256]{3,2,1,0:T(8,128)S(1)}, f32[2,2,16,256]{3,2,1,0:T(8,128)S(1)}, u32[]{:S(2)}, u32[]{:S(2)}) %collective-permute-start.8) | collective-permute-done | bytes 65568 | tf_op jit(solution)/shard_map/ppermute | solution.py:576
  60.2 2.0 %send.1 = (bf16[4,512,128]{2,1,0:T(8,128)(2,1)S(1)}, bf16[4,512,128]{2,1,0:T(8,128)(2,1)S(1)}, f32[2,2,16,128]{3,2,1,0:T(8,128)S(1)}) custom-call(s32[4,2,3]{2,1,0:T(2,128)S(1)} %copy.14.matching_ref, bf16[4,512,256]{2,1,0:T(8,128)(2,1)S(1)} %get-tuple-element.30.inner_ref.inner_b, bf16[4,512,256]{2,1,0:T(8,128)(2,1)S(1)} %get-tuple-element.31.gp_ref.gp_b, ...), custom_call_target="tpu_custom_call" | custom-call | flops 402653184 | bytes 4194304 | tf_op jit(solution)/shard_map/send/pallas_call | solution.py:689
  62.2 2.3 %collective-permute-start.11 = (bf16[4,512,128]{2,1,0:T(8,128)(2,1)S(1)}, bf16[4,512,128]{2,1,0:T(8,128)(2,1)S(1)}, u32[]{:S(2)}, u32[]{:S(2)}) collective-permute-start(bf16[4,512,128]{2,1,0:T(8,128)(2,1)S(1)} %get-tuple-element.33._), channel_id=1, source_target_pairs={{1,0},{2,1},{3,2},{4,3},{5,4},{6,5},{7,6},{9,8},{10,9},{11,10},{12... | collective-permute-start | bytes 1572872 | tf_op jit(solution)/shard_map/ppermute | solution.py:703
  64.5 5.2 %collective-permute-start.10 = (bf16[4,512,128]{2,1,0:T(8,128)(2,1)S(1)}, bf16[4,512,128]{2,1,0:T(8,128)(2,1)S(1)}, u32[]{:S(2)}, u32[]{:S(2)}) collective-permute-start(bf16[4,512,128]{2,1,0:T(8,128)(2,1)S(1)} %get-tuple-element.43.up_ref), channel_id=1, source_target_pairs={{0,1},{1,2},{2,3},{3,4},{4,5},{5,6},{6,7},{8,9},{9,10},{10,11},{11... | collective-permute-start | bytes 1572872 | tf_op jit(solution)/shard_map/ppermute | solution.py:702
  69.8 5.2 %middle.1 = (bf16[4,512,256]{2,1,0:T(8,128)(2,1)S(1)}, bf16[4,512,256]{2,1,0:T(8,128)(2,1)S(1)}) custom-call(bf16[4,512,128]{2,1,0:T(8,128)(2,1)S(1)} %get-tuple-element.33._, bf16[2048,256]{1,0:T(8,128)(2,1)S(1)} %get-tuple-element.34.values, f32[8,2048]{1,0:T(8,128)S(1)} %get-tuple-element.35.keys, ...), custom_call_target="tpu_custom_call" | custom-call | flops 2147483648 | bytes 10485760 | tf_op jit(solution)/shard_map/middle/pallas_call | solution.py:706
  74.9 8.5 %inside.1 = (bf16[8,512,128]{2,1,0:T(8,128)(2,1)}, f32[4,512,128]{2,1,0:T(8,128)S(1)}, f32[8,512,128]{2,1,0:T(8,128)}, f32[4,512,128]{2,1,0:T(8,128)S(1)}) custom-call(bf16[4,512,256]{2,1,0:T(8,128)(2,1)S(1)} %get-tuple-element.30.inner_ref.inner_b, bf16[4,512,256]{2,1,0:T(8,128)(2,1)S(1)} %get-tuple-element.31.gp_ref.gp_b, ...), custom_call_target="tpu_custom_call" | custom-call | flops 4831838208 | bytes 14680064 | tf_op jit(solution)/shard_map/inside/pallas_call | solution.py:727
  83.5 1.9 %final.1 = (bf16[8,512,128]{2,1,0:T(8,128)(2,1)}, f32[8,512,128]{2,1,0:T(8,128)}) custom-call(f32[4,512,128]{2,1,0:T(8,128)S(1)} %get-tuple-element.39.ana_b, f32[4,512,128]{2,1,0:T(8,128)S(1)} %get-tuple-element.40.grad_b, bf16[8,512,128]{2,1,0:T(8,128)(2,1)} %get-tuple-element.41._, ...), custom_call_target="tpu_custom_call", output_to_operand_aliasing={{0}: (2, {}), {1}: (3, {})} | custom-call | bytes 6291456 | tf_op jit(solution)/shard_map/final/pallas_call | solution.py:756
  (45 shorter events, 4.4 us)
Async XLA Ops:
  4.6 7.2 %copy-start = (bf16[1,1,2,4,512,128]{5,4,3,2,1,0:T(8,128)(2,1)S(1)}, bf16[1,1,2,4,512,128]{5,4,3,2,1,0:T(8,128)(2,1)}, u32[]{:S(2)}) copy-start(bf16[1,1,2,4,512,128]{5,4,3,2,1,0:T(8,128)(2,1)} %param.10) | copy-start | bytes 3145732
  4.6 7.2 %copy-start.2 = (bf16[1,1,2,4,512,128]{5,4,3,2,1,0:T(8,128)(2,1)S(1)}, bf16[1,1,2,4,512,128]{5,4,3,2,1,0:T(8,128)(2,1)}, u32[]{:S(2)}) copy-start(bf16[1,1,2,4,512,128]{5,4,3,2,1,0:T(8,128)(2,1)} %param.19) | copy-start | bytes 3145732
  4.6 40.2 %all-to-all-start = ((bf16[32,136,128]{2,1,0:T(8,128)(2,1)}), bf16[32,136,128]{2,1,0:T(8,128)(2,1)}, u32[]{:S(2)}, u32[]{:S(2)}) async-start(bf16[32,136,128]{2,1,0:T(8,128)(2,1)} %pack.1), calls=%async_computation | async-start | bytes 2228224 | tf_op jit(solution)/shard_map/all_to_all | solution.py:597
  11.8 13.0 %copy-start.6 = (bf16[9,128,256]{2,1,0:T(8,128)(2,1)S(1)}, bf16[9,128,256]{2,1,0:T(8,128)(2,1)}, u32[]{:S(2)}) copy-start(bf16[9,128,256]{2,1,0:T(8,128)(2,1)} %k1_in.1) | copy-start | bytes 1769476
  11.8 13.0 %copy-start.8 = (bf16[9,256,128]{2,1,0:T(8,128)(2,1)S(1)}, bf16[9,256,128]{2,1,0:T(8,128)(2,1)}, u32[]{:S(2)}) copy-start(bf16[9,256,128]{2,1,0:T(8,128)(2,1)} %k2_ref.5) | copy-start | bytes 1769476
  11.9 13.0 %copy-start.10 = (f32[256]{0:T(256)S(1)}, f32[256]{0:T(256)}, u32[]{:S(2)}) copy-start(f32[256]{0:T(256)} %param.16) | copy-start | bytes 3076
  11.9 21.5 %collective-permute-start.2 = (bf16[4,32,128]{2,1,0:T(8,128)(2,1)S(1)}, bf16[4,32,128]{2,1,0:T(8,128)(2,1)S(1)}, u32[]{:S(2)}, u32[]{:S(2)}) collective-permute-start(bf16[4,32,128]{2,1,0:T(8,128)(2,1)S(1)} %pad_maximum_fusion.2), channel_id=1, source_target_pairs={{0,1},{1,2},{2,3},{3,4},{4,5},{5,6},{6,7},{8,9},{9,10},{10,11},{11... | collective-permute-start | bytes 98312 | tf_op jit(solution)/shard_map/ppermute | solution.py:566
  16.5 28.3 %collective-permute-start.1 = (bf16[4,512,128]{2,1,0:T(8,128)(2,1)}, bf16[4,512,128]{2,1,0:T(8,128)(2,1)}, u32[]{:S(2)}, u32[]{:S(2)}) collective-permute-start(bf16[4,512,128]{2,1,0:T(8,128)(2,1)} %pad_maximum_fusion.1), channel_id=1, source_target_pairs={{1,0},{2,1},{3,2},{4,3},{5,4},{6,5},{7,6},{9,8},{10,9},{11,10},{12... | collective-permute-start | bytes 1572872 | tf_op jit(solution)/shard_map/ppermute | solution.py:560
  19.2 25.6 %collective-permute-start = (bf16[4,512,128]{2,1,0:T(8,128)(2,1)}, bf16[4,512,128]{2,1,0:T(8,128)(2,1)}, u32[]{:S(2)}, u32[]{:S(2)}) collective-permute-start(bf16[4,512,128]{2,1,0:T(8,128)(2,1)} %pad_maximum_fusion), channel_id=1, source_target_pairs={{0,1},{1,2},{2,3},{3,4},{4,5},{5,6},{6,7},{8,9},{9,10},{10,11},{11... | collective-permute-start | bytes 1572872 | tf_op jit(solution)/shard_map/ppermute | solution.py:559
  22.9 12.1 %collective-permute-start.3 = (bf16[4,32,128]{2,1,0:T(8,128)(2,1)S(1)}, bf16[4,32,128]{2,1,0:T(8,128)(2,1)S(1)}, u32[]{:S(2)}, u32[]{:S(2)}) collective-permute-start(bf16[4,32,128]{2,1,0:T(8,128)(2,1)S(1)} %pad_maximum_fusion.3), channel_id=1, source_target_pairs={{1,0},{2,1},{3,2},{4,3},{5,4},{6,5},{7,6},{9,8},{10,9},{11,10},{12... | collective-permute-start | bytes 98312 | tf_op jit(solution)/shard_map/ppermute | solution.py:567
  36.0 5.6 %copy-start.12 = (s32[4,2,3]{0,1,2:T(2,128)S(1)}, s32[4,2,3]{0,1,2:T(2,128)}, u32[]{:S(2)}) copy-start(s32[4,2,3]{0,1,2:T(2,128)} %param.14) | copy-start | bytes 292
  36.0 7.9 %copy-start.7 = (bf16[9,128,256]{2,1,0:T(8,128)(2,1)S(1)}, bf16[9,128,256]{2,1,0:T(8,128)(2,1)}, u32[]{:S(2)}) copy-start(bf16[9,128,256]{2,1,0:T(8,128)(2,1)} %get-tuple-element.26.k2t_ref.k2t_in) | copy-start | bytes 1769476
  36.1 6.2 %collective-permute-start.6 = (f32[2,2,16,128]{3,2,1,0:T(8,128)S(1)}, f32[2,2,16,128]{3,2,1,0:T(8,128)S(1)}, u32[]{:S(2)}, u32[]{:S(2)}) collective-permute-start(f32[2,2,16,128]{3,2,1,0:T(8,128)S(1)} %edges.1.rest_0_), channel_id=1, source_target_pairs={{24,0},{0,8},{8,16},{16,24},{25,1},{1,9},{9,17},{17,25},{26,2},{2,... | collective-permute-start | bytes 98312 | tf_op jit(solution)/shard_map/ppermute | solution.py:576
  37.6 5.4 %collective-permute-start.5 = (f32[2,2,16,128]{3,2,1,0:T(8,128)S(1)}, f32[2,2,16,128]{3,2,1,0:T(8,128)S(1)}, u32[]{:S(2)}, u32[]{:S(2)}) collective-permute-start(f32[2,2,16,128]{3,2,1,0:T(8,128)S(1)} %edges.1.rest_0_), channel_id=1, source_target_pairs={{16,0},{24,8},{0,16},{8,24},{17,1},{25,9},{1,17},{9,25},{18,2},{26... | collective-permute-start | bytes 98312 | tf_op jit(solution)/shard_map/ppermute | solution.py:576
  41.2 2.8 %collective-permute-start.4 = (f32[2,2,16,128]{3,2,1,0:T(8,128)S(1)}, f32[2,2,16,128]{3,2,1,0:T(8,128)S(1)}, u32[]{:S(2)}, u32[]{:S(2)}) collective-permute-start(f32[2,2,16,128]{3,2,1,0:T(8,128)S(1)} %edges.1.rest_0_), channel_id=1, source_target_pairs={{8,0},{16,8},{24,16},{0,24},{9,1},{17,9},{25,17},{1,25},{10,2},{18... | collective-permute-start | bytes 98312 | tf_op jit(solution)/shard_map/ppermute | solution.py:576
  44.8 15.4 %copy-start.5 = (bf16[9,256,128]{2,1,0:T(8,128)(2,1)S(1)}, bf16[9,256,128]{2,1,0:T(8,128)(2,1)}, u32[]{:S(2)}) copy-start(bf16[9,256,128]{2,1,0:T(8,128)(2,1)} %get-tuple-element.27._.k1t_ref) | copy-start | bytes 1769476
  44.9 15.4 %copy-start.9 = (bf16[9,256,128]{2,1,0:T(8,128)(2,1)S(1)}, bf16[9,256,128]{2,1,0:T(8,128)(2,1)}, u32[]{:S(2)}) copy-start(bf16[9,256,128]{2,1,0:T(8,128)(2,1)} %k2_ref.5) | copy-start | bytes 1769476
  53.1 5.2 %collective-permute-start.9 = (f32[2,2,16,256]{3,2,1,0:T(8,128)S(1)}, f32[2,2,16,256]{3,2,1,0:T(8,128)S(1)}, u32[]{:S(2)}, u32[]{:S(2)}) collective-permute-start(f32[2,2,16,256]{3,2,1,0:T(8,128)S(1)} %get-tuple-element.32.rest_0_), channel_id=1, source_target_pairs={{24,0},{0,8},{8,16},{16,24},{25,1},{1,9},{9,17},{17,25},{26,2},{2,... | collective-permute-start | bytes 196616 | tf_op jit(solution)/shard_map/ppermute | solution.py:576
  53.2 6.3 %collective-permute-start.8 = (f32[2,2,16,256]{3,2,1,0:T(8,128)S(1)}, f32[2,2,16,256]{3,2,1,0:T(8,128)S(1)}, u32[]{:S(2)}, u32[]{:S(2)}) collective-permute-start(f32[2,2,16,256]{3,2,1,0:T(8,128)S(1)} %get-tuple-element.32.rest_0_), channel_id=1, source_target_pairs={{16,0},{24,8},{0,16},{8,24},{17,1},{25,9},{1,17},{9,25},{18,2},{26... | collective-permute-start | bytes 196616 | tf_op jit(solution)/shard_map/ppermute | solution.py:576
  55.6 4.6 %collective-permute-start.7 = (f32[2,2,16,256]{3,2,1,0:T(8,128)S(1)}, f32[2,2,16,256]{3,2,1,0:T(8,128)S(1)}, u32[]{:S(2)}, u32[]{:S(2)}) collective-permute-start(f32[2,2,16,256]{3,2,1,0:T(8,128)S(1)} %get-tuple-element.32.rest_0_), channel_id=1, source_target_pairs={{8,0},{16,8},{24,16},{0,24},{9,1},{17,9},{25,17},{1,25},{10,2},{18... | collective-permute-start | bytes 196616 | tf_op jit(solution)/shard_map/ppermute | solution.py:576
  62.2 21.3 %collective-permute-start.11 = (bf16[4,512,128]{2,1,0:T(8,128)(2,1)S(1)}, bf16[4,512,128]{2,1,0:T(8,128)(2,1)S(1)}, u32[]{:S(2)}, u32[]{:S(2)}) collective-permute-start(bf16[4,512,128]{2,1,0:T(8,128)(2,1)S(1)} %get-tuple-element.33._), channel_id=1, source_target_pairs={{1,0},{2,1},{3,2},{4,3},{5,4},{6,5},{7,6},{9,8},{10,9},{11,10},{12... | collective-permute-start | bytes 1572872 | tf_op jit(solution)/shard_map/ppermute | solution.py:703
  64.5 18.9 %collective-permute-start.10 = (bf16[4,512,128]{2,1,0:T(8,128)(2,1)S(1)}, bf16[4,512,128]{2,1,0:T(8,128)(2,1)S(1)}, u32[]{:S(2)}, u32[]{:S(2)}) collective-permute-start(bf16[4,512,128]{2,1,0:T(8,128)(2,1)S(1)} %get-tuple-element.43.up_ref), channel_id=1, source_target_pairs={{0,1},{1,2},{2,3},{3,4},{4,5},{5,6},{6,7},{8,9},{9,10},{10,11},{11... | collective-permute-start | bytes 1572872 | tf_op jit(solution)/shard_map/ppermute | solution.py:702
  69.7 5.2 %copy-start.1 = (bf16[1,1,2,4,512,128]{5,4,3,2,1,0:T(8,128)(2,1)S(1)}, bf16[1,1,2,4,512,128]{5,4,3,2,1,0:T(8,128)(2,1)}, u32[]{:S(2)}) copy-start(bf16[1,1,2,4,512,128]{5,4,3,2,1,0:T(8,128)(2,1)} %param.10) | copy-start | bytes 3145732
  69.7 5.2 %copy-start.3 = (bf16[1,1,2,4,512,128]{5,4,3,2,1,0:T(8,128)(2,1)S(1)}, bf16[1,1,2,4,512,128]{5,4,3,2,1,0:T(8,128)(2,1)}, u32[]{:S(2)}) copy-start(bf16[1,1,2,4,512,128]{5,4,3,2,1,0:T(8,128)(2,1)} %param.19) | copy-start | bytes 3145732
  (2 other events, 6.3 us)

commit v2 on v1

v2 whole, which is shorter than its diff:
```python
import functools
import math

import jax
import jax.numpy as jnp
from jax import lax
from jax.experimental import pallas as pl
from jax.experimental.pallas import tpu as pltpu
from jax.sharding import PartitionSpec as P

F32 = jnp.float32
BF16 = jnp.bfloat16
GROUP = 8
HIGH = 64
PIXEL_ROWS = 8
ROOT = math.sqrt(2.0 / math.pi)
CUBIC = 0.044715


def params(mib=24):
    return pltpu.CompilerParams(vmem_limit_bytes=mib << 20)


def cost(flops, nbytes):
    return pl.CostEstimate(flops=int(flops), bytes_accessed=int(nbytes), transcendentals=0)


def hold(shape, kind):
    return pltpu.VMEM(shape, kind)


def held(array):
    return pltpu.with_memory_space_constraint(array, pltpu.VMEM)


def far(array):
    return pltpu.with_memory_space_constraint(array, pltpu.HBM)


def fixed(shape):
    return pl.BlockSpec(shape, lambda *_: (0,) * len(shape))


def dot(a, b):
    return jnp.dot(a, b, preferred_element_type=F32)


def matched(matching_ref, side, faces):
    face = lax.axis_index("face")
    partner = matching_ref[face, side, 0]
    return lax.rem(partner - face + faces, faces), matching_ref[face, side, 1], matching_ref[face, side, 2]


def is_even():
    return lax.rem(lax.axis_index("tile"), 2) == 0


def is_last():
    return lax.axis_index("tile") == lax.axis_size("tile") - 1


def partner_rows(part_refs, array, hop, their_side, flipped):
    rows = None
    for k, ref in enumerate(part_refs):
        mine = jnp.where(their_side == 1, ref[array, 1], ref[array, 0])
        rows = mine if rows is None else jnp.where(hop == k, mine, rows)
    swapped = jnp.concatenate([rows[GROUP:], rows[:GROUP]], axis=0)
    return jnp.where(flipped == 1, swapped, rows)


def rolled_rows(rows, step):
    first, second = rows[:GROUP], rows[GROUP:]
    if step:
        first = pltpu.roll(first, (-step) % GROUP, 0)
        second = pltpu.roll(second, step % GROUP, 0)
    return jnp.concatenate([first, second], axis=0).astype(BF16)


def side_forward(rows, side, taps_ref):
    lhs = jnp.concatenate([rolled_rows(rows, dy) for dy in (-1, 0, 1)], axis=1)
    taps = jnp.concatenate([taps_ref[3 * row + 2 * side] for row in range(3)], axis=0)
    return dot(lhs, taps)


def side_adjoint(rows, their_side, flipped, taps_ref):
    lhs = jnp.concatenate([rolled_rows(rows, -dy) for dy in (-1, 0, 1)], axis=1)
    order = [jnp.where(flipped == 1, 2 - row, row) for row in range(3)]
    taps = jnp.concatenate([taps_ref[3 * row + 2 * their_side] for row in order], axis=0)
    return dot(lhs, taps)


def shift_columns(values, step):
    count = values.shape[0]
    at = lax.broadcasted_iota(jnp.int32, values.shape, 0)
    moved = pltpu.roll(values, (-step) % count, 0)
    edge = count - 1 if step == 1 else 0
    return jnp.where(at == edge, 0.0, moved)


def spread_columns(row, order):
    wide = row.astype(F32)
    return jnp.concatenate(
        [row if s == 0 else shift_columns(wide, s).astype(BF16) for s in order], axis=1
    )


def add_edges(values, left, right):
    count = values.shape[0]
    at = lax.broadcasted_iota(jnp.int32, (GROUP, values.shape[1]), 0)
    first = values[:GROUP] + jnp.where(at == 0, left, 0.0)
    tail = values[count - GROUP :] + jnp.where(at == GROUP - 1, right, 0.0)
    return jnp.concatenate([first, values[GROUP : count - GROUP], tail], axis=0)


def pack_body(
    capacity, dest_in, pixel_in, values_in, out_hbm, dest_ref, pixel_ref, values_ref, out_ref, in_sem,
    out_sem,
):
    count = values_ref.shape[0]
    devices = out_ref.shape[0]
    block = 128
    loads = [
        pltpu.make_async_copy(source, target, in_sem.at[k])
        for k, (source, target) in enumerate(
            ((dest_in, dest_ref), (pixel_in, pixel_ref), (values_in, values_ref))
        )
    ]
    for load in loads:
        load.start()
    loads[0].wait()
    loads[1].wait()
    dest_row = dest_ref[...].astype(F32)
    pixel_row = pixel_ref[...]
    eye = lax.broadcasted_iota(jnp.int32, (block, block), 0) == lax.broadcasted_iota(
        jnp.int32, (block, block), 1
    )

    def column(row, start):
        piece = row[:, start : start + block]
        return jnp.sum(jnp.where(eye, piece, 0.0), axis=1, keepdims=True)

    high_row = lax.shift_right_logical(pixel_row, 6).astype(F32) + 1.0
    low_row = (pixel_row & (HIGH - 1)).astype(F32)
    own = lax.broadcasted_iota(jnp.int32, (block, count), 0)
    other = lax.broadcasted_iota(jnp.int32, (block, count), 1)
    lane = lax.broadcasted_iota(jnp.int32, (block, 128), 1)
    lane_rank = (lane & (HIGH - 1)).astype(F32)
    rank_row = jnp.zeros((1, count), F32)
    coded = []
    for start in range(0, count, block):
        same = column(dest_row, start) == dest_row
        later = (own + start) < other
        earlier = (own + start) > other
        rank_row = rank_row + jnp.sum(
            jnp.where(same & later, 1.0, 0.0), axis=0, keepdims=True
        )
        rank = jnp.sum(jnp.where(same & earlier, 1.0, 0.0), axis=1, keepdims=True)
        code = jnp.where(lane < HIGH, column(high_row, start), column(low_row, start))
        coded.append(jnp.where(rank == lane_rank, code, 0.0).astype(BF16))
    to_device = (
        lax.broadcasted_iota(jnp.int32, (devices, count), 0).astype(F32) == dest_row
    )
    pixels = dot(
        jnp.where(to_device, 1.0, 0.0).astype(BF16), jnp.concatenate(coded, axis=0)
    )
    out_ref[:, 2 * capacity :, :] = jnp.broadcast_to(
        pixels[:, None, :], (devices, PIXEL_ROWS, 128)
    ).astype(BF16)
    slot_row = dest_row * capacity + rank_row
    slots = 512
    per_block = slots // capacity
    loads[2].wait()
    values = values_ref[...]
    stores = []
    slot_at = lax.broadcasted_iota(jnp.int32, (slots, count), 0).astype(F32)
    for start in range(0, devices * capacity, slots):
        onehot = jnp.where(slot_at == slot_row - start, 1.0, 0.0).astype(BF16)
        rows = dot(onehot, values).astype(BF16)
        first = start // capacity
        for half in range(2):
            out_ref[first : first + per_block, half * capacity : (half + 1) * capacity, :] = (
                rows[:, half * 128 : (half + 1) * 128].reshape(per_block, capacity, 128)
            )
        store = pltpu.make_async_copy(
            out_ref.at[first : first + per_block],
            out_hbm.at[first : first + per_block],
            out_sem.at[len(stores)],
        )
        store.start()
        stores.append(store)
    for store in stores:
        store.wait()


def end_rows(rows, x_ends, c_ends, pair_ends, cross_ends):
    prev, after = [], []
    even = is_even()
    for side in range(2):
        pair, cross = pair_ends[side], cross_ends[side]
        prev.append(jnp.where(even, cross, pair))
        after.append(jnp.where(even, pair, cross))
    outside = {}
    for array, own in enumerate((x_ends, c_ends)):
        for side in range(2):
            for band in range(2):
                plane = 2 * array + band
                fold = own[side][(1 - band) * rows + rows - 1]
                outside[array, side, 2 * band] = prev[side][plane]
                outside[array, side, 2 * band + 1] = jnp.where(is_last(), fold, after[side][plane])
    return outside


def edge_body(rows, x_lo, x_hi, c_lo, c_hi, a_lo, a_hi, b_lo, b_hi, out_ref):
    out_ref[...] = jnp.zeros_like(out_ref)
    wide = lambda refs: [ref[...].astype(F32) for ref in refs]
    x_ends, c_ends = wide((x_lo, x_hi)), wide((c_lo, c_hi))
    outside = end_rows(rows, x_ends, c_ends, wide((a_lo, a_hi)), wide((b_lo, b_hi)))
    for array, own in enumerate((x_ends, c_ends)):
        for side in range(2):
            at = 0 if side == 0 else own[side].shape[1] - 1
            for band in range(2):
                base = band * GROUP
                out_ref[array, side, base, :] = outside[array, side, 2 * band][at]
                for r in range(rows):
                    out_ref[array, side, base + 1 + r, :] = own[side][band * rows + r, at]
                out_ref[array, side, base + 1 + rows, :] = outside[array, side, 2 * band + 1][at]


def row_groups(rows, way):
    first, last = ((0, 0), (1, rows - 1)), ((0, rows - 1), (1, 0))
    if way < 0:
        first, last = last, first
    inner = tuple((b, r) for b in range(2) for r in range(1, rows - 1))
    return ((inner, (-1, 0, 1)), (first, (0, 1)), (last, (-1, 0)))


def border_index(j, rows):
    return (j // 2) * rows + (j % 2) * (rows - 1)


def border_row(j, rows):
    return (j // 2) * rows + lax.rem(j, 2) * (rows - 1)


def lift_body(
    rows, x_in, c_in, k1_in, k2_in, b1_ref, pre_out, grad_out, k1t_ref, k2t_ref, x_ref, c_ref, k1_ref,
    k2_ref, cat, held_rows, sem,
):
    width, channels = x_ref.shape[1], x_ref.shape[2]
    lifted = k1_ref.shape[2]
    used = [0]

    def slot():
        used[0] += 1
        return sem.at[used[0] - 1]

    loads = [
        pltpu.make_async_copy(source, target, slot())
        for source, target in ((x_in, x_ref), (k1_in, k1_ref), (k2_in, k2_ref), (c_in, c_ref))
    ]
    for load in loads:
        load.start()
    stores = []
    for array, (source, weights, order, out) in enumerate(
        ((x_ref, k1_ref, (-1, 0, 1), pre_out), (c_ref, k2t_ref, (1, 0, -1), grad_out))
    ):
        way = 1 - 2 * array
        loads[2 * array].wait()
        loads[2 * array + 1].wait()
        if array == 1:
            for t in range(k2_ref.shape[0]):
                k2t_ref[t] = k2_ref[t].astype(F32).T.astype(BF16)
        for i in range(2 * rows):
            cat[array, i] = spread_columns(source[i], order)
        members, steps = row_groups(rows, way)[0]
        lhs = jnp.concatenate(
            [
                jnp.concatenate(
                    [cat[array, b * rows + r + way * (1 - 2 * b) * dy] for dy in steps], axis=1
                )
                for b, r in members
            ],
            axis=0,
        )
        taps = weights[...].reshape(3 * len(steps) * channels, lifted)
        half = len(members) // 2
        for first in (0, half):
            total = dot(lhs[first * width : (first + half) * width], taps)
            if array == 0:
                total = total + b1_ref[...]
            for k in range(half):
                held_rows[array, first + k] = total[k * width : (k + 1) * width]
                store = pltpu.make_async_copy(
                    held_rows.at[array, first + k], out.at[first + k], slot()
                )
                store.start()
                stores.append(store)
    for t in range(k1_ref.shape[0]):
        k1t_ref[t] = k1_ref[t].astype(F32).T.astype(BF16)
    for store in stores:
        store.wait()


def border_pieces(array, pair, outside, own, inside):
    first = (pair[0] == 0) == (array == 0)
    return [outside, own, inside] if first else [inside, own, outside]


def rim_in_body(
    rows, matching_ref, k1_in, b1_ref, k2t_in, pre_lo, pre_hi, grad_lo, grad_hi, x_lo, x_hi, c_lo, c_hi,
    a_lo, a_hi, b_lo, b_hi, base_ref, taps_ref, k1_ref, k2t_ref, sem,
):
    loads = [
        pltpu.make_async_copy(k1_in, k1_ref, sem.at[0]),
        pltpu.make_async_copy(k2t_in, k2t_ref, sem.at[1]),
    ]
    for load in loads:
        load.start()
    for load in loads:
        load.wait()
    face = lax.axis_index("face")
    for side in range(2):
        their_side, flipped = matching_ref[face, side, 1], matching_ref[face, side, 2]
        for row in range(3):
            taps_ref[0, side, row] = k1_ref[3 * row + 2 * side]
            turned = jnp.where(flipped == 1, 2 - row, row)
            taps_ref[1, side, row] = k2t_ref[3 * turned + 2 * their_side]
    whole = lambda refs: [ref[...] for ref in refs]
    x_ends, c_ends = whole((x_lo, x_hi)), whole((c_lo, c_hi))
    outside = end_rows(rows, x_ends, c_ends, whole((a_lo, a_hi)), whole((b_lo, b_hi)))
    channels, lifted = k1_ref.shape[1], k1_ref.shape[2]
    base_ref[...] = jnp.zeros_like(base_ref)
    for array, (strips, own, weights, order) in enumerate(
        (
            ((pre_lo, pre_hi), x_ends, k1_ref, (-1, 0, 1)),
            ((grad_lo, grad_hi), c_ends, k2t_ref, (1, 0, -1)),
        )
    ):
        for side in range(2):
            spot = 0 if side == 0 else GROUP - 1
            for b in range(2):
                for r in range(1, rows - 1):
                    at = 2 * GROUP * side + GROUP * b + r + 1
                    base_ref[array, at : at + 1, :] = strips[side][
                        b * (rows - 2) + r - 1, spot : spot + 1, :
                    ]
        for pair in ((0, 3), (1, 2)):
            spots = [(side, j) for side in range(2) for j in pair]
            lhs = []
            for side, j in spots:
                i = border_index(j, rows)
                planes = border_pieces(
                    array, pair, outside[array, side, j], own[side][i], own[side][i + 1 - 2 * (j % 2)]
                )
                lhs.append(
                    jnp.concatenate([spread_columns(plane, order) for plane in planes], axis=1)
                )
            found = dot(
                jnp.concatenate(lhs, axis=0),
                weights[...].reshape(weights.shape[0] * channels, lifted),
            )
            if array == 0:
                found = found + b1_ref[...]
            strip = found.shape[0] // len(spots)
            for k, (side, j) in enumerate(spots):
                at = 2 * GROUP * side + GROUP * (j // 2) + 1 + (rows - 1) * (j % 2)
                spot = k * strip + (0 if side == 0 else strip - 1)
                base_ref[array, at : at + 1, :] = found[spot : spot + 1]


def side_in_body(faces, matching_ref, taps_ref, base_ref, *rest):
    parts = rest[:faces]
    x_side, c_side, sums_ref = rest[faces:]
    taps = taps_ref[...].reshape(2, 2, 3 * taps_ref.shape[3], taps_ref.shape[4])
    for side in range(2):
        hop, their_side, flipped = matched(matching_ref, side, faces)
        for array, out in enumerate((x_side, c_side)):
            near = partner_rows(parts, array, hop, their_side, flipped)
            way = 1 - 2 * array
            lhs = jnp.concatenate([rolled_rows(near, way * dy) for dy in (-1, 0, 1)], axis=1)
            out[side] = dot(lhs, taps[array, side])
    for array, out in enumerate((x_side, c_side)):
        sums_ref[array] = base_ref[array] + out[...].reshape(sums_ref.shape[1:])


def gelu_pair(v, grad):
    square = v * v
    t = jnp.tanh(v * (ROOT + (ROOT * CUBIC) * square))
    half = 0.5 + 0.5 * t
    slope = half + (0.5 * v) * (1.0 - t * t) * (ROOT + (3.0 * ROOT * CUBIC) * square)
    return (v * half).astype(BF16), (grad * slope).astype(BF16)


def unpack_received(capacity, recv_ref, values, keys):
    devices = recv_ref.shape[0]
    slots = devices * capacity
    per_lane = 128 // capacity
    for half in range(2):
        values[:, half * 128 : (half + 1) * 128] = recv_ref[
            :, half * capacity : (half + 1) * capacity, :
        ].reshape(slots, 128)
    owner = lax.broadcasted_iota(jnp.int32, (PIXEL_ROWS, 128), 1) // capacity
    for start in range(0, devices, per_lane):
        key = jnp.zeros((PIXEL_ROWS, 128), F32)
        for k in range(per_lane):
            code = recv_ref[start + k, 2 * capacity :, :].astype(F32)
            mine = (code - 1.0) * HIGH + pltpu.roll(code, HIGH, 1)
            if k:
                mine = pltpu.roll(mine, k * capacity, 1)
            key = jnp.where(owner == k, mine, key)
        keys[:, start * capacity : start * capacity + 128] = key


def row_taps(taps_ref, row):
    return jnp.concatenate([taps_ref[3 * row + dx] for dx in range(3)], axis=1)


def merge_shifts(wide, forward):
    channels = wide.shape[1] // 3
    left, mid, right = (wide[:, k * channels : (k + 1) * channels] for k in range(3))
    step = -1 if forward else 1
    return mid + shift_columns(left, step) + shift_columns(right, -step)


def rim_body(rows, width, capacity, recv_ref, base_ref, edge_ref, values, keys):
    unpack_received(capacity, recv_ref, values, keys)
    at = lax.broadcasted_iota(jnp.int32, (4 * GROUP, 1), 0)
    e = at & (GROUP - 1)
    b = (at // GROUP) & 1
    side = at // (2 * GROUP)
    inside = (e >= 1) & (e <= rows)
    pixel = (b * rows + e - 1) * width + side * (width - 1)
    wanted = jnp.where(inside, pixel, -1).astype(F32)
    onehot = jnp.where(keys[0:1, :] == wanted, 1.0, 0.0).astype(BF16)
    v = base_ref[0] + dot(onehot, values[...])
    inner, gp = gelu_pair(v, base_ref[1])
    shape = (2, 2 * GROUP, v.shape[1])
    edge_ref[0] = jnp.where(inside, inner.astype(F32), 0.0).reshape(shape)
    edge_ref[1] = jnp.where(inside, gp.astype(F32), 0.0).reshape(shape)


def border_body(
    rows, values, keys, x_side, c_side, b1_ref, a_in, b_in, x_in, c_in, k1_in, k2t_in, inner_ref, gp_ref,
    x_ref, c_ref, outside, k1_ref, k2t_ref, sem,
):
    width, lifted = inner_ref.shape[1], inner_ref.shape[2]
    channels = outside.shape[3]
    even, last = is_even(), is_last()
    waits = []

    def load(target, *sources):
        slot = sem.at[len(waits)]
        for condition, source in sources:
            copy = pltpu.make_async_copy(source, target, slot)
            if condition is None:
                copy.start()
            else:
                pl.when(condition)(copy.start)
        waits.append(copy)

    for array, (source, target, weights, held_weights) in enumerate(
        ((x_in, x_ref, k1_in, k1_ref), (c_in, c_ref, k2t_in, k2t_ref))
    ):
        load(target, (None, source))
        load(held_weights, (None, weights))
        for j in range(4):
            band = j // 2
            plane = 2 * array + band
            if j % 2 == 0:
                choices = ((even, b_in.at[plane]), (jnp.logical_not(even), a_in.at[plane]))
            else:
                fold = source.at[(1 - band) * rows + rows - 1]
                middle = jnp.logical_not(even) & jnp.logical_not(last)
                choices = ((last, fold), (even, a_in.at[plane]), (middle, b_in.at[plane]))
            load(outside.at[array, j], *choices)

    column = lax.broadcasted_iota(jnp.int32, (width, keys.shape[1]), 0).astype(F32)
    for pair in ((0, 3), (1, 2)):
        onehot = jnp.concatenate(
            [
                jnp.where(
                    column == keys[0:1, :] - float(border_index(j, rows) * width), 1.0, 0.0
                ).astype(BF16)
                for j in pair
            ],
            axis=0,
        )
        found = dot(onehot, values[...]) + b1_ref[...]
        totals = []
        for array, (own, weights, order) in enumerate(
            ((x_ref, k1_ref, (-1, 0, 1)), (c_ref, k2t_ref, (1, 0, -1)))
        ):
            if pair[0] == 0:
                for copy in waits[6 * array : 6 * array + 6]:
                    copy.wait()
            lhs = []
            for j in pair:
                i = border_index(j, rows)
                planes = border_pieces(
                    array, pair, outside[array, j], own[i], own[i + 1 - 2 * (j % 2)]
                )
                lhs.append(
                    jnp.concatenate([spread_columns(plane, order) for plane in planes], axis=1)
                )
            totals.append(
                dot(
                    jnp.concatenate(lhs, axis=0),
                    weights[...].reshape(weights.shape[0] * channels, lifted),
                )
            )
        v = found + totals[0]
        for k, j in enumerate(pair):
            at = GROUP * (j // 2) + 1 + (rows - 1) * (j % 2)
            piece = slice(k * width, (k + 1) * width)
            inner, gp = gelu_pair(
                add_edges(v[piece], x_side[0, at : at + 1, :], x_side[1, at : at + 1, :]),
                add_edges(totals[1][piece], c_side[0, at : at + 1, :], c_side[1, at : at + 1, :]),
            )
            inner_ref[j] = inner
            gp_ref[j] = gp


def send_body(rows, faces, matching_ref, inner_ref, gp_ref, k2_ref, k1t_ref, *rest):
    parts = rest[:faces]
    pair_ref, cross_ref, side_ref = rest[faces:]
    even = is_even()
    width = inner_ref.shape[1]
    for side in range(2):
        hop, their_side, flipped = matched(matching_ref, side, faces)
        near = partner_rows(parts, 0, hop, their_side, flipped)
        side_ref[0, side] = side_forward(near, side, k2_ref)
        near = partner_rows(parts, 1, hop, their_side, flipped)
        side_ref[1, side] = side_adjoint(near, their_side, flipped, k1t_ref)
    up = jnp.where(even, 1, 0)
    for array, (source, taps) in enumerate(((inner_ref, k2_ref), (gp_ref, k1t_ref))):
        for group in range(2):
            members = ((pair_ref, group, up), (cross_ref, 1 - group, 1 - up))
            tap = jnp.where((group == up) == (array == 0), 2, 0)
            lhs = jnp.concatenate([source[2 * band + bottom] for _, band, bottom in members], axis=0)
            wide = dot(lhs, row_taps(taps, tap))
            for k, (target, band, bottom) in enumerate(members):
                part = merge_shifts(wide[k * width : (k + 1) * width], array == 0)
                corner = GROUP * band + (rows + 1) * bottom
                part = add_edges(
                    part,
                    side_ref[array, 0, pl.ds(corner, 1), :],
                    side_ref[array, 1, pl.ds(corner, 1), :],
                )
                target[2 * array + band] = part.astype(BF16)


def middle_body(rows, _, values, keys, *rest):
    middle = rows - 2
    pre_refs, grad_refs = rest[:middle], rest[middle : 2 * middle]
    x_side, c_side, inner_ref, gp_ref = rest[2 * middle :]
    band = pl.program_id(0)
    width, lifted = pre_refs[0].shape[1], pre_refs[0].shape[2]
    column = lax.broadcasted_iota(jnp.int32, (width, keys.shape[1]), 0).astype(F32)
    onehots = []
    for k in range(middle):
        local = keys[0:1, :] - ((band * rows + k + 1) * width).astype(F32)
        onehots.append(jnp.where(column == local, 1.0, 0.0).astype(BF16))
    found = dot(jnp.concatenate(onehots, axis=0), values[...])
    for k in range(middle):
        at = band * GROUP + k + 2
        inner, gp = gelu_pair(
            add_edges(
                pre_refs[k][0] + found[k * width : (k + 1) * width],
                x_side[0, pl.ds(at, 1), :],
                x_side[1, pl.ds(at, 1), :],
            ),
            add_edges(grad_refs[k][0], c_side[0, pl.ds(at, 1), :], c_side[1, pl.ds(at, 1), :]),
        )
        inner_ref[k] = inner
        gp_ref[k] = gp


def inside_body(
    rows, inner_b, gp_b, inner_m, gp_m, side_ref, k2_ref, k1t_ref, b2_ref, x_in, c_in, ana_out, ana_b,
    grad_out, grad_b, own_rows, ana_rows, grad_rows, sem,
):
    width, channels = own_rows.shape[2], own_rows.shape[3]
    middle = rows - 2
    loads = [
        pltpu.make_async_copy(x_in, own_rows.at[0], sem.at[0]),
        pltpu.make_async_copy(c_in, own_rows.at[1], sem.at[1]),
    ]
    for load in loads:
        load.start()
    stores = []
    for array, (border, inner, taps) in enumerate(
        ((inner_b, inner_m, k2_ref), (gp_b, gp_m, k1t_ref))
    ):
        way = 1 - 2 * array

        def plane(b, r):
            if r == 0 or r == rows - 1:
                return border[2 * b + r // (rows - 1)]
            return inner[middle * b + r - 1]

        for members, steps in row_groups(rows, way):
            lhs = jnp.concatenate(
                [
                    jnp.concatenate(
                        [plane(b, r + way * (1 - 2 * b) * dy) for dy in steps], axis=1
                    )
                    for b, r in members
                ],
                axis=0,
            )
            wide = dot(lhs, jnp.concatenate([row_taps(taps, dy + 1) for dy in steps], axis=0))
            if len(steps) == 3:
                loads[array].wait()
            for k, (b, r) in enumerate(members):
                i = b * rows + r
                at = b * GROUP + r + 1
                total = merge_shifts(wide[k * width : (k + 1) * width], array == 0)
                total = add_edges(
                    total + own_rows[array, i].astype(F32),
                    side_ref[array, 0, at : at + 1, :],
                    side_ref[array, 1, at : at + 1, :],
                )
                if array == 0:
                    total = total + b2_ref[...]
                if len(steps) == 2:
                    (ana_b, grad_b)[array][2 * b + r // (rows - 1)] = total
                    continue
                held_rows, out = ((ana_rows, ana_out), (grad_rows, grad_out))[array]
                held_rows[k] = total.astype(held_rows.dtype)
                store = pltpu.make_async_copy(held_rows.at[k], out.at[i], sem.at[2 + len(stores)])
                store.start()
                stores.append(store)
    for store in stores:
        store.wait()


def final_body(
    rows, ana_b, grad_b, own_ref, pair_ref, cross_ref, _, __, ana_out, grad_out, ana_rows, grad_rows, sem
):
    even, last = is_even(), is_last()
    stores = []
    for array, (acc, held_rows, out) in enumerate(
        ((ana_b, ana_rows, ana_out), (grad_b, grad_rows, grad_out))
    ):
        for j in range(4):
            band = j // 2
            plane = 2 * array + band
            if j % 2:
                add = jnp.where(even, pair_ref[plane], cross_ref[plane])
                add = jnp.where(last, own_ref[2 * array + 1 - band], add)
            else:
                add = jnp.where(even, cross_ref[plane], pair_ref[plane])
            held_rows[j] = (acc[j] + add.astype(F32)).astype(held_rows.dtype)
            store = pltpu.make_async_copy(
                held_rows.at[j], out.at[border_index(j, rows)], sem.at[len(stores)]
            )
            store.start()
            stores.append(store)
    for store in stores:
        store.wait()


def per_device(
    state,
    obs_values,
    obs_dest,
    obs_pixel,
    matching,
    kernel_one,
    bias_one,
    kernel_two,
    bias_two,
    cotangent,
):
    rows, width, channels = state.shape[3], state.shape[4], state.shape[5]
    lifted = kernel_one.shape[2]
    tiles, faces = lax.axis_size("tile"), lax.axis_size("face")
    devices = tiles * faces
    count = obs_values.shape[0]
    capacity = 2 * count // devices
    all_rows = 2 * rows
    middle = rows - 2
    chunk = 2 * capacity + PIXEL_ROWS
    x = state.reshape(all_rows, width, channels)
    c = cotangent.reshape(all_rows, width, channels)
    even = is_even()
    pairs = [(i, i ^ 1) for i in range(tiles)]
    crosses = [(i, i + 1 if i % 2 else i - 1) for i in range(1, tiles - 1)]
    strip = 16

    def ends(at):
        fields = [field.reshape(2, rows, width, channels) for field in (x, c)]
        picked = [
            jnp.concatenate(
                [
                    lax.dynamic_slice(field, (0, at, start, 0), (2, 1, strip, channels))[:, 0]
                    for start in (0, width - strip)
                ],
                axis=1,
            )
            for field in fields
        ]
        return jnp.concatenate(picked, axis=0)

    pair_ends = lax.ppermute(ends(jnp.where(even, rows - 1, 0)), "tile", pairs)
    cross_ends = lax.ppermute(ends(jnp.where(even, 0, rows - 1)), "tile", crosses)
    low_row = lambda field, at: lax.dynamic_index_in_dim(
        field.reshape(2, rows, width, channels), at, 1, keepdims=False
    )
    border_rows = lambda at: jnp.concatenate([low_row(x, at), low_row(c, at)], axis=0)
    pair_out = border_rows(jnp.where(even, rows - 1, 0))
    cross_out = border_rows(jnp.where(even, 0, rows - 1))
    cross_out, pair_ends, cross_ends = lax.optimization_barrier(
        (cross_out, pair_ends, cross_ends)
    )
    pair_rows = lax.ppermute(pair_out, "tile", pairs)
    cross_rows = lax.ppermute(cross_out, "tile", crosses)
    smem = pl.BlockSpec(memory_space=pltpu.SMEM)
    vmem = pl.BlockSpec(memory_space=pltpu.VMEM)
    hbm = pl.BlockSpec(memory_space=pl.ANY)

    def exchange(own):
        parts = [own]
        for k in range(1, faces):
            parts.append(
                lax.ppermute(own, "face", [((i + k) % faces, i) for i in range(faces)])
            )
        return parts

    packed = pl.pallas_call(
        functools.partial(pack_body, capacity),
        in_specs=[hbm] * 3,
        out_specs=hbm,
        out_shape=pltpu.HBM((devices, chunk, 128), BF16),
        scratch_shapes=[
            pltpu.VMEM((1, count), jnp.int32),
            pltpu.VMEM((1, count), jnp.int32),
            pltpu.VMEM((count, lifted), BF16),
            pltpu.VMEM((devices, chunk, 128), BF16),
            pltpu.SemaphoreType.DMA((3,)),
            pltpu.SemaphoreType.DMA((devices * capacity // 512,)),
        ],
        compiler_params=params(16),
        cost_estimate=cost(2 * devices * capacity * count * lifted, 2 << 20),
        name="pack",
    )(far(obs_dest.reshape(1, count)), far(obs_pixel.reshape(1, count)), far(obs_values))
    received = lax.all_to_all(packed, ("face", "tile"), 0, 0, tiled=True)

    b1 = bias_one.reshape(1, lifted)
    b2 = bias_two.reshape(1, channels)
    row_block = lambda n: pl.BlockSpec((1, width, n), lambda i: (i, 0, 0))
    edge_block = lambda n: pl.BlockSpec((1, width, n), lambda i: (border_row(i, rows), 0, 0))
    conv_flops = 2 * 9 * all_rows * width * channels * lifted
    plane = (4, width, channels)
    pre, grad_inner, k1t, k2t = pl.pallas_call(
        functools.partial(lift_body, rows),
        in_specs=[hbm] * 4 + [vmem],
        out_specs=[hbm] * 2 + [vmem] * 2,
        out_shape=[pltpu.HBM((2 * middle, width, lifted), F32)] * 2
        + [pltpu.HBM(kernel_two.shape, BF16), pltpu.HBM(kernel_one.shape, BF16)],
        scratch_shapes=[
            pltpu.VMEM(x.shape, BF16),
            pltpu.VMEM(c.shape, BF16),
            pltpu.VMEM(kernel_one.shape, BF16),
            pltpu.VMEM(kernel_two.shape, BF16),
            pltpu.VMEM((2, all_rows, width, 3 * channels), BF16),
            pltpu.VMEM((2, 2 * middle, width, lifted), F32),
            pltpu.SemaphoreType.DMA((4 + 4 * middle,)),
        ],
        compiler_params=params(40),
        cost_estimate=cost(conv_flops, 8 << 20),
        name="lift",
    )(far(x), far(c), far(kernel_one), far(kernel_two), b1)
    pre, grad_inner = far(pre), far(grad_inner)
    low = lambda n: pl.BlockSpec((n, strip, channels), lambda *_: (0, 0, 0))
    high = lambda n, at: pl.BlockSpec((n, strip, channels), lambda *_: (0, at, 0))
    tail = width // strip - 1
    edge_shape = (2, 2, 2 * GROUP, channels)
    edges = pl.pallas_call(
        functools.partial(edge_body, rows),
        grid=(1,),
        in_specs=[low(all_rows), high(all_rows, tail)] * 2 + [low(4), high(4, 1)] * 2,
        out_specs=fixed(edge_shape),
        out_shape=jax.ShapeDtypeStruct(edge_shape, F32),
        compiler_params=params(8),
        cost_estimate=cost(0, 1 << 18),
        name="edges",
    )(x, x, c, c, pair_ends, pair_ends, cross_ends, cross_ends)
    parts = exchange(edges)

    side_in = (2, 2 * GROUP, lifted)
    end = width // GROUP - 1
    edge_strip = lambda at: pl.BlockSpec((2 * middle, GROUP, lifted), lambda *_: (0, at, 0))
    rim_shape = (2, 4 * GROUP, lifted)
    taps_shape = (2, 2, 3, channels, lifted)
    rim_base, side_taps = pl.pallas_call(
        functools.partial(rim_in_body, rows),
        grid=(1,),
        in_specs=[smem, hbm, fixed(b1.shape), hbm]
        + [edge_strip(0), edge_strip(end)] * 2
        + [low(all_rows), high(all_rows, tail)] * 2
        + [low(4), high(4, 1)] * 2,
        out_specs=[fixed(rim_shape), fixed(taps_shape)],
        out_shape=[jax.ShapeDtypeStruct(rim_shape, F32), jax.ShapeDtypeStruct(taps_shape, BF16)],
        scratch_shapes=[
            pltpu.VMEM(kernel_one.shape, BF16),
            pltpu.VMEM(k2t.shape, BF16),
            pltpu.SemaphoreType.DMA((2,)),
        ],
        compiler_params=params(8),
        cost_estimate=cost(0, 2 << 20),
        name="rim_in",
    )(
        matching, far(kernel_one), b1, far(k2t), pre, pre, grad_inner, grad_inner, x, x, c, c, pair_ends,
        pair_ends, cross_ends, cross_ends,
    )
    x_side, c_side, rim_sums = pl.pallas_call(
        functools.partial(side_in_body, faces),
        in_specs=[smem] + [vmem] * (2 + faces),
        out_specs=[vmem] * 3,
        out_shape=[
            jax.ShapeDtypeStruct(side_in, F32),
            jax.ShapeDtypeStruct(side_in, F32),
            jax.ShapeDtypeStruct(rim_shape, F32),
        ],
        compiler_params=params(8),
        cost_estimate=cost(0, 1 << 20),
        name="sides_in",
    )(matching, side_taps, rim_base, *parts)

    side_two = (2, 2, 2 * GROUP, lifted)
    slots = devices * capacity
    onehot_flops = 2 * width * slots * lifted
    other_block = pl.BlockSpec(
        (1, width, channels), lambda j: ((1 - j // 2) * rows + rows - 1, 0, 0)
    )
    edges_two, values, keys = pl.pallas_call(
        functools.partial(rim_body, rows, width, capacity),
        in_specs=[vmem] * 2,
        out_specs=[vmem] * 3,
        out_shape=[
            jax.ShapeDtypeStruct(side_two, F32),
            hold((slots, lifted), BF16),
            hold((PIXEL_ROWS, slots), F32),
        ],
        compiler_params=params(8),
        cost_estimate=cost(0, 3 << 20),
        name="rim",
    )(received, rim_sums)
    values, keys = held(values), held(keys)
    parts_two = exchange(edges_two)

    border_shape = hold((4, width, lifted), BF16)
    inner_b, gp_b = pl.pallas_call(
        functools.partial(border_body, rows),
        in_specs=[vmem] * 5 + [hbm] * 6,
        out_specs=[vmem] * 2,
        out_shape=[border_shape] * 2,
        scratch_shapes=[
            pltpu.VMEM(x.shape, BF16),
            pltpu.VMEM(c.shape, BF16),
            pltpu.VMEM((2, 4, width, channels), BF16),
            pltpu.VMEM(kernel_one.shape, BF16),
            pltpu.VMEM(k2t.shape, BF16),
            pltpu.SemaphoreType.DMA((12,)),
        ],
        compiler_params=params(32),
        cost_estimate=cost(4 * onehot_flops + conv_flops // 6, 10 << 20),
        name="border",
    )(
        values, keys, x_side, c_side, b1, far(pair_rows), far(cross_rows), far(x), far(c),
        far(kernel_one), far(k2t),
    )
    inner_b, gp_b = held(inner_b), held(gp_b)

    side_out = (2, 2, 2 * GROUP, channels)
    to_pair, to_cross, sides = pl.pallas_call(
        functools.partial(send_body, rows, faces),
        in_specs=[smem] + [vmem] * (4 + faces),
        out_specs=[vmem] * 3,
        out_shape=[
            jax.ShapeDtypeStruct(plane, BF16),
            jax.ShapeDtypeStruct(plane, BF16),
            jax.ShapeDtypeStruct(side_out, F32),
        ],
        compiler_params=params(16),
        cost_estimate=cost(conv_flops // 6, 4 << 20),
        name="send",
    )(matching, inner_b, gp_b, kernel_two, k1t, *parts_two)
    from_pair = lax.ppermute(to_pair, "tile", pairs)
    from_cross = lax.ppermute(to_cross, "tile", crosses)

    middle_block = lambda k: pl.BlockSpec((1, width, lifted), lambda i: (i * middle + k, 0, 0))
    inner_m, gp_m = pl.pallas_call(
        functools.partial(middle_body, rows),
        grid=(2,),
        in_specs=[hbm, fixed(values.shape), fixed(keys.shape)]
        + [middle_block(k) for k in range(middle)] * 2
        + [fixed(side_in)] * 2,
        out_specs=[pl.BlockSpec((middle, width, lifted), lambda i: (i, 0, 0))] * 2,
        out_shape=[hold((2 * middle, width, lifted), BF16)] * 2,
        compiler_params=params(),
        cost_estimate=cost(2 * middle * onehot_flops, 10 << 20),
        name="middle",
    )(to_cross, values, keys, *[pre] * middle, *[grad_inner] * middle, x_side, c_side)
    inner_m, gp_m = held(inner_m), held(gp_m)

    analysis, ana_b, grad_state, grad_b = pl.pallas_call(
        functools.partial(inside_body, rows),
        in_specs=[vmem] * 8 + [hbm] * 2,
        out_specs=[hbm, vmem, hbm, vmem],
        out_shape=[
            pltpu.HBM((all_rows, width, channels), BF16),
            hold(plane, F32),
            pltpu.HBM((all_rows, width, channels), F32),
            hold(plane, F32),
        ],
        scratch_shapes=[
            pltpu.VMEM((2, all_rows, width, channels), BF16),
            pltpu.VMEM((2 * middle, width, channels), BF16),
            pltpu.VMEM((2 * middle, width, channels), F32),
            pltpu.SemaphoreType.DMA((2 + 4 * middle,)),
        ],
        compiler_params=params(),
        cost_estimate=cost(2 * conv_flops, 14 << 20),
        name="inside",
    )(inner_b, gp_b, inner_m, gp_m, sides, kernel_two, k1t, b2, far(x), far(c))
    ana_b, grad_b = held(ana_b), held(grad_b)

    analysis, grad_state = pl.pallas_call(
        functools.partial(final_body, rows),
        in_specs=[vmem] * 5 + [hbm] * 2,
        out_specs=[hbm] * 2,
        out_shape=[
            pltpu.HBM((all_rows, width, channels), BF16),
            pltpu.HBM((all_rows, width, channels), F32),
        ],
        scratch_shapes=[
            pltpu.VMEM(plane, BF16),
            pltpu.VMEM(plane, F32),
            pltpu.SemaphoreType.DMA((8,)),
        ],
        input_output_aliases={5: 0, 6: 1},
        compiler_params=params(16),
        cost_estimate=cost(0, 6 << 20),
        name="final",
    )(ana_b, grad_b, to_cross, from_pair, from_cross, far(analysis), far(grad_state))
    return analysis.reshape(state.shape), grad_state.reshape(cotangent.shape)


def solution(mesh):
    return jax.shard_map(
        per_device,
        mesh=mesh,
        in_specs=(
            P("face", "tile", None, None, None, None),
            P(("face", "tile"), None),
            P(("face", "tile"), None),
            P(("face", "tile")),
            P(),
            P(),
            P(),
            P(),
            P(),
            P("face", "tile", None, None, None, None),
        ),
        out_specs=(
            P("face", "tile", None, None, None, None),
            P("face", "tile", None, None, None, None),
        ),
        check_vma=False,
    )
```

time: 86 us -> 76.9 us (0.89)
  starting transfers between devices: 34.6 us -> 26 us
  Pallas kernels: 39.1 us -> 40.6 us
  local copies, waits for them, and re-layouts: 1.31 us -> 0.24 us
    ppermute x6, starting transfers between devices: 18.6 us -> 10.7 us  [the longest x1 3.42 us: per_device(): lax.ppermute(ends(jnp.where(even, 0, rows - 1)), 'tile', crosses)]
    ppermute x6, waiting for transfers between devices: 6.11 us -> 2.88 us  [exchange(): lax.ppermute(own, 'face', [((i + k) % faces, i) for i in range(faces)])]
    ppermute x6, waiting for transfers between devices: 1.52 us -> 4.22 us  [the longest x1 3.95 us: per_device(): lax.ppermute(ends(jnp.where(even, 0, rows - 1)), 'tile', crosses)]
    pallas_call x5 -> x7, Pallas kernels: 27.2 us -> 28.7 us  [the longest x1 9.57 us: per_device(): pl.pallas_call(functools.partial(border_body, rows), in_specs=[vmem] * 5...]
    unnamed x27 -> x19, local copies, waits for them, and re-layouts: 1.23 us -> 0.14 us
  transfers between devices with their start and end apart: 13 -> 13, of which waited for: 7 -> 3; matrix products, arithmetic and copies ran while one was open for 2% -> 2% of each run, Pallas kernels for 27% -> 43%
where the time goes in v2:
time: 76.9 us; the launch traced here: 76.6 us
  Pallas kernels  40.6 us (53%)
  starting transfers between devices  26 us (34%)
  waiting for transfers between devices  7.11 us (9%)
  other arithmetic  1.68 us (2%)
  between operations  1.09 us (1%)
    pallas_call x1, Pallas kernels, per_device(): pl.pallas_call(functools.partial(border_body, rows), in_specs=[vmem] * 5...  9.57 us
    ppermute x6, starting transfers between devices, exchange(): lax.ppermute(own, 'face', [((i + k) % faces, i) for i in range(faces)])  8.13 us
    pallas_call x1, Pallas kernels, per_device(): pl.pallas_call(functools.partial(inside_body, rows), in_specs=[vmem] * 8...  7.57 us
    pallas_call x1, Pallas kernels, per_device(): pl.pallas_call(functools.partial(lift_body, rows), in_specs=[hbm] * 4 + [...  7.14 us
    all_to_all x1, starting transfers between devices, per_device(): received = lax.all_to_all(packed, ('face', 'tile'), 0, 0, tiled=True)  7.1 us
    pallas_call x1, Pallas kernels, per_device(): pl.pallas_call(functools.partial(middle_body, rows), grid=(2,), in_specs=...  5.01 us
    pallas_call x1, Pallas kernels, per_device(): pl.pallas_call(functools.partial(pack_body, capacity), in_specs=[hbm] * 3...  4.03 us
    ppermute x1, waiting for transfers between devices, per_device(): lax.ppermute(ends(jnp.where(even, 0, rows - 1)), 'tile', crosses)  3.95 us
  transfers between devices with their start and end apart: 13, of which 3 were waited for; matrix products, arithmetic and copies ran while one was open for 2% of the time, Pallas kernels for 43%

profile of v2, /device:TPU:1, one launch (start us, length us, event | category | flops | bytes accessed | tf_op | source)
XLA Modules:
  0.0 76.6 jit_solution(11378622489362822938)
XLA Ops:
  0.6 4.0 %pack.1 = bf16[32,136,128]{2,1,0:T(8,128)(2,1)} custom-call(s32[1,1024]{1,0:T(1,128)} %bitcast.52, s32[1,1024]{1,0:T(1,128)} %bitcast.53, bf16[1024,256]{1,0:T(8,128)(2,1)} %values_in.1), custom_call_target="tpu_custom_call" | custom-call | flops 1073741824 | bytes 2097152 | tf_op jit(solution)/shard_map/pack/pallas_call | solution.py:730
  4.7 7.1 %all-to-all-start = ((bf16[32,136,128]{2,1,0:T(8,128)(2,1)}), bf16[32,136,128]{2,1,0:T(8,128)(2,1)S(1)}, u32[]{:S(2)}, u32[]{:S(2)}) async-start(bf16[32,136,128]{2,1,0:T(8,128)(2,1)} %pack.1), calls=%async_computation | async-start | bytes 2228224 | tf_op jit(solution)/shard_map/all_to_all | solution.py:747
  12.2 3.4 %collective-permute-start.1 = (bf16[4,32,128]{2,1,0:T(8,128)(2,1)S(1)}, bf16[4,32,128]{2,1,0:T(8,128)(2,1)S(1)}, u32[]{:S(2)}, u32[]{:S(2)}) collective-permute-start(bf16[4,32,128]{2,1,0:T(8,128)(2,1)S(1)} %maximum_maximum_fusion.1), channel_id=1, source_target_pairs={{1,2},{2,1},{3,4},{4,3},{5,6},{6,5},{9,10},{10,9},{11,12},{12,11},... | collective-permute-start | bytes 98312 | tf_op jit(solution)/shard_map/ppermute | solution.py:706
  15.7 0.8 %pad_maximum_fusion.1 = bf16[4,512,128]{2,1,0:T(8,128)(2,1)} fusion(bf16[2,512,128]{2,1,0:T(8,128)(2,1)S(1)} %get-tuple-element.60, bf16[2,512,128]{2,1,0:T(8,128)(2,1)S(1)} %get-tuple-element.71), kind=kLoop, calls=%fused_computation.1 | loop fusion | flops 262144 | bytes 1048576 | tf_op jit(solution)/shard_map/concatenate | solution.py:710
  16.6 0.8 %pad_maximum_fusion = bf16[4,512,128]{2,1,0:T(8,128)(2,1)} fusion(bf16[2,512,128]{2,1,0:T(8,128)(2,1)S(1)} %get-tuple-element.61, bf16[2,512,128]{2,1,0:T(8,128)(2,1)S(1)} %get-tuple-element.70), kind=kLoop, calls=%fused_computation | loop fusion | flops 262144 | bytes 1048576 | tf_op jit(solution)/shard_map/concatenate | solution.py:710
  17.4 4.0 %collective-permute-done.1.b_lo.b_hi = bf16[4,32,128]{2,1,0:T(8,128)(2,1)S(1)} collective-permute-done((bf16[4,32,128]{2,1,0:T(8,128)(2,1)S(1)}, bf16[4,32,128]{2,1,0:T(8,128)(2,1)S(1)}, u32[]{:S(2)}, u32[]{:S(2)}) %collective-permute-start.1) | collective-permute-done | bytes 32800 | tf_op jit(solution)/shard_map/ppermute | solution.py:706
  21.3 1.9 %collective-permute-start.6 = (bf16[4,512,128]{2,1,0:T(8,128)(2,1)}, bf16[4,512,128]{2,1,0:T(8,128)(2,1)}, u32[]{:S(2)}, u32[]{:S(2)}) collective-permute-start(bf16[4,512,128]{2,1,0:T(8,128)(2,1)} %pad_maximum_fusion), channel_id=1, source_target_pairs={{1,2},{2,1},{3,4},{4,3},{5,6},{6,5},{9,10},{10,9},{11,12},{12,11},... | collective-permute-start | bytes 1572872 | tf_op jit(solution)/shard_map/ppermute | solution.py:717
  23.7 2.6 %collective-permute-start.3 = (f32[2,2,16,128]{3,2,1,0:T(8,128)S(1)}, f32[2,2,16,128]{3,2,1,0:T(8,128)S(1)}, u32[]{:S(2)}, u32[]{:S(2)}) collective-permute-start(f32[2,2,16,128]{3,2,1,0:T(8,128)S(1)} %edges.1.rest_0_), channel_id=1, source_target_pairs={{16,0},{24,8},{0,16},{8,24},{17,1},{25,9},{1,17},{9,25},{18,2},{26... | collective-permute-start | bytes 98312 | tf_op jit(solution)/shard_map/ppermute | solution.py:726
  26.4 1.7 %collective-permute-start.2 = (f32[2,2,16,128]{3,2,1,0:T(8,128)S(1)}, f32[2,2,16,128]{3,2,1,0:T(8,128)S(1)}, u32[]{:S(2)}, u32[]{:S(2)}) collective-permute-start(f32[2,2,16,128]{3,2,1,0:T(8,128)S(1)} %edges.1.rest_0_), channel_id=1, source_target_pairs={{8,0},{16,8},{24,16},{0,24},{9,1},{17,9},{25,17},{1,25},{10,2},{18... | collective-permute-start | bytes 98312 | tf_op jit(solution)/shard_map/ppermute | solution.py:726
  28.1 7.1 %lift.1 = (f32[4,512,256]{2,1,0:T(8,128)}, f32[4,512,256]{2,1,0:T(8,128)}, bf16[9,256,128]{2,1,0:T(8,128)(2,1)}, bf16[9,128,256]{2,1,0:T(8,128)(2,1)}) custom-call(bf16[8,512,128]{2,1,0:T(8,128)(2,1)} %bitcast.32, bf16[8,512,128]{2,1,0:T(8,128)(2,1)} %bitcast.39, bf16[9,128,256]{2,1,0:T(8,128)(2,1)} %k1_in.5, bf16[9,256,128]{2,1,0:T(8,128)(2,1)} %k2_ref.3, ...), custom_call_target="tpu_custom_call" | custom-call | flops 2415919104 | bytes 8388608 | tf_op jit(solution)/shard_map/lift/pallas_call | solution.py:755
  35.4 2.6 %rim_in.1 = (f32[2,32,256]{2,1,0:T(8,128)S(1)}, bf16[2,2,3,128,256]{4,3,2,1,0:T(8,128)(2,1)S(1)}) custom-call(s32[4,2,3]{2,1,0:T(2,128)S(1)} %copy.15.matching_ref, bf16[9,128,256]{2,1,0:T(8,128)(2,1)} %k1_in.5, f32[1,256]{1,0:T(1,128)S(1)} %bitcast.47, bf16[9,128,256]{2,1,0:T(8,128)(2,1)} %get-tuple-element.30.k2t_in, ...), custom_call_target="tpu_custom_call" | custom-call | bytes 2097152 | tf_op jit(solution)/shard_map/rim_in/pallas_call | solution.py:796
  38.1 2.9 %collective-permute-done.3.rest_2_ = f32[2,2,16,128]{3,2,1,0:T(8,128)S(1)} collective-permute-done((f32[2,2,16,128]{3,2,1,0:T(8,128)S(1)}, f32[2,2,16,128]{3,2,1,0:T(8,128)S(1)}, u32[]{:S(2)}, u32[]{:S(2)}) %collective-permute-start.3) | collective-permute-done | bytes 32800 | tf_op jit(solution)/shard_map/ppermute | solution.py:726
  40.9 0.8 %sides_in.1 = (f32[2,16,256]{2,1,0:T(8,128)S(1)}, f32[2,16,256]{2,1,0:T(8,128)S(1)}, f32[2,32,256]{2,1,0:T(8,128)S(1)}) custom-call(s32[4,2,3]{2,1,0:T(2,128)S(1)} %copy.15.matching_ref, bf16[2,2,3,128,256]{4,3,2,1,0:T(8,128)(2,1)S(1)} %get-tuple-element.35.taps_ref, f32[2,32,256]{2,1,0:T(8,128)S(1)} %get-tuple-element.36.base_ref, ...), custom_call_target="tpu_custom_call" | custom-call | bytes 1048576 | tf_op jit(solution)/shard_map/sides_in/pallas_call | solution.py:817
  41.8 0.5 rim.1
  42.2 0.7 collective-permute-start.9
  43.0 1.6 %collective-permute-start.8 = (f32[2,2,16,256]{3,2,1,0:T(8,128)S(1)}, f32[2,2,16,256]{3,2,1,0:T(8,128)S(1)}, u32[]{:S(2)}, u32[]{:S(2)}) collective-permute-start(f32[2,2,16,256]{3,2,1,0:T(8,128)S(1)} %get-tuple-element.46.rest_0_), channel_id=1, source_target_pairs={{16,0},{24,8},{0,16},{8,24},{17,1},{25,9},{1,17},{9,25},{18,2},{26... | collective-permute-start | bytes 196616 | tf_op jit(solution)/shard_map/ppermute | solution.py:726
  44.6 0.9 %collective-permute-start.7 = (f32[2,2,16,256]{3,2,1,0:T(8,128)S(1)}, f32[2,2,16,256]{3,2,1,0:T(8,128)S(1)}, u32[]{:S(2)}, u32[]{:S(2)}) collective-permute-start(f32[2,2,16,256]{3,2,1,0:T(8,128)S(1)} %get-tuple-element.46.rest_0_), channel_id=1, source_target_pairs={{8,0},{16,8},{24,16},{0,24},{9,1},{17,9},{25,17},{1,25},{10,2},{18... | collective-permute-start | bytes 196616 | tf_op jit(solution)/shard_map/ppermute | solution.py:726
  45.6 9.6 %border.1 = (bf16[4,512,256]{2,1,0:T(8,128)(2,1)S(1)}, bf16[4,512,256]{2,1,0:T(8,128)(2,1)S(1)}) custom-call(bf16[2048,256]{1,0:T(8,128)(2,1)S(1)} %get-tuple-element.38.values, f32[8,2048]{1,0:T(8,128)S(1)} %get-tuple-element.39.keys, f32[2,16,256]{2,1,0:T(8,128)S(1)} %get-tuple-element.40.x_side.rest_4_, ...), custom_call_target="tpu_custom_call" | custom-call | flops 2550136832 | bytes 10485760 | tf_op jit(solution)/shard_map/border/pallas_call | solution.py:854
  55.2 2.0 %send.1 = (bf16[4,512,128]{2,1,0:T(8,128)(2,1)S(1)}, bf16[4,512,128]{2,1,0:T(8,128)(2,1)S(1)}, f32[2,2,16,128]{3,2,1,0:T(8,128)S(1)}) custom-call(s32[4,2,3]{2,1,0:T(2,128)S(1)} %copy.15.matching_ref, bf16[4,512,256]{2,1,0:T(8,128)(2,1)S(1)} %get-tuple-element.43.inner_ref.inner_b, bf16[4,512,256]{2,1,0:T(8,128)(2,1)S(1)} %get-tuple-element.44.gp_ref.gp_b, ...), custom_call_target="tpu_custom_call" | custom-call | flops 402653184 | bytes 4194304 | tf_op jit(solution)/shard_map/send/pallas_call | solution.py:877
  57.2 1.8 %collective-permute-start.10 = (bf16[4,512,128]{2,1,0:T(8,128)(2,1)S(1)}, bf16[4,512,128]{2,1,0:T(8,128)(2,1)S(1)}, u32[]{:S(2)}, u32[]{:S(2)}) collective-permute-start(bf16[4,512,128]{2,1,0:T(8,128)(2,1)S(1)} %get-tuple-element.53), channel_id=1, source_target_pairs={{0,1},{1,0},{2,3},{3,2},{4,5},{5,4},{6,7},{7,6},{8,9},{9,8},{10,11... | collective-permute-start | bytes 1572872 | tf_op jit(solution)/shard_map/ppermute | solution.py:890
  59.0 3.2 %collective-permute-start.11 = (bf16[4,512,128]{2,1,0:T(8,128)(2,1)S(1)}, bf16[4,512,128]{2,1,0:T(8,128)(2,1)S(1)}, u32[]{:S(2)}, u32[]{:S(2)}) collective-permute-start(bf16[4,512,128]{2,1,0:T(8,128)(2,1)S(1)} %get-tuple-element.47._.own_ref), channel_id=1, source_target_pairs={{1,2},{2,1},{3,4},{4,3},{5,6},{6,5},{9,10},{10,9},{11,12},{12,11},... | collective-permute-start | bytes 1572872 | tf_op jit(solution)/shard_map/ppermute | solution.py:891
  62.3 5.0 %middle.1 = (bf16[4,512,256]{2,1,0:T(8,128)(2,1)S(1)}, bf16[4,512,256]{2,1,0:T(8,128)(2,1)S(1)}) custom-call(bf16[4,512,128]{2,1,0:T(8,128)(2,1)S(1)} %get-tuple-element.47._.own_ref, bf16[2048,256]{1,0:T(8,128)(2,1)S(1)} %get-tuple-element.38.values, f32[8,2048]{1,0:T(8,128)S(1)} %get-tuple-element.39.keys, ...), custom_call_target="tpu_custom_call" | custom-call | flops 2147483648 | bytes 10485760 | tf_op jit(solution)/shard_map/middle/pallas_call | solution.py:894
  67.3 7.6 %inside.1 = (bf16[8,512,128]{2,1,0:T(8,128)(2,1)}, f32[4,512,128]{2,1,0:T(8,128)S(1)}, f32[8,512,128]{2,1,0:T(8,128)}, f32[4,512,128]{2,1,0:T(8,128)S(1)}) custom-call(bf16[4,512,256]{2,1,0:T(8,128)(2,1)S(1)} %get-tuple-element.43.inner_ref.inner_b, bf16[4,512,256]{2,1,0:T(8,128)(2,1)S(1)} %get-tuple-element.44.gp_ref.gp_b, ...), custom_call_target="tpu_custom_call" | custom-call | flops 4831838208 | bytes 14680064 | tf_op jit(solution)/shard_map/inside/pallas_call | solution.py:908
  75.1 1.3 %final.1 = (bf16[8,512,128]{2,1,0:T(8,128)(2,1)}, f32[8,512,128]{2,1,0:T(8,128)}) custom-call(f32[4,512,128]{2,1,0:T(8,128)S(1)} %get-tuple-element.51.ana_b, f32[4,512,128]{2,1,0:T(8,128)S(1)} %get-tuple-element.52.grad_b, bf16[4,512,128]{2,1,0:T(8,128)(2,1)S(1)} %get-tuple-element.47._.own_ref, ...), custom_call_target="tpu_custom_call", output_to_operand_aliasing={{0}: (5, {}), {1}: (6, {})} | custom-call | bytes 6291456 | tf_op jit(solution)/shard_map/final/pallas_call | solution.py:930
  (38 shorter events, 1.3 us)
Async XLA Ops:
  4.7 7.1 %copy-start = (bf16[1,1,2,4,512,128]{5,4,3,2,1,0:T(8,128)(2,1)S(1)}, bf16[1,1,2,4,512,128]{5,4,3,2,1,0:T(8,128)(2,1)}, u32[]{:S(2)}) copy-start(bf16[1,1,2,4,512,128]{5,4,3,2,1,0:T(8,128)(2,1)} %param.10) | copy-start | bytes 3145732
  4.7 7.1 %copy-start.2 = (bf16[1,1,2,4,512,128]{5,4,3,2,1,0:T(8,128)(2,1)S(1)}, bf16[1,1,2,4,512,128]{5,4,3,2,1,0:T(8,128)(2,1)}, u32[]{:S(2)}) copy-start(bf16[1,1,2,4,512,128]{5,4,3,2,1,0:T(8,128)(2,1)} %param.19) | copy-start | bytes 3145732
  4.7 37.1 %all-to-all-start = ((bf16[32,136,128]{2,1,0:T(8,128)(2,1)}), bf16[32,136,128]{2,1,0:T(8,128)(2,1)S(1)}, u32[]{:S(2)}, u32[]{:S(2)}) async-start(bf16[32,136,128]{2,1,0:T(8,128)(2,1)} %pack.1), calls=%async_computation | async-start | bytes 2228224 | tf_op jit(solution)/shard_map/all_to_all | solution.py:747
  11.9 5.5 %collective-permute-start = (bf16[4,32,128]{2,1,0:T(8,128)(2,1)S(1)}, bf16[4,32,128]{2,1,0:T(8,128)(2,1)S(1)}, u32[]{:S(2)}, u32[]{:S(2)}) collective-permute-start(bf16[4,32,128]{2,1,0:T(8,128)(2,1)S(1)} %maximum_maximum_fusion), channel_id=1, source_target_pairs={{0,1},{1,0},{2,3},{3,2},{4,5},{5,4},{6,7},{7,6},{8,9},{9,8},{10,11... | collective-permute-start | bytes 98312 | tf_op jit(solution)/shard_map/ppermute | solution.py:705
  12.2 9.1 %collective-permute-start.1 = (bf16[4,32,128]{2,1,0:T(8,128)(2,1)S(1)}, bf16[4,32,128]{2,1,0:T(8,128)(2,1)S(1)}, u32[]{:S(2)}, u32[]{:S(2)}) collective-permute-start(bf16[4,32,128]{2,1,0:T(8,128)(2,1)S(1)} %maximum_maximum_fusion.1), channel_id=1, source_target_pairs={{1,2},{2,1},{3,4},{4,3},{5,6},{6,5},{9,10},{10,9},{11,12},{12,11},... | collective-permute-start | bytes 98312 | tf_op jit(solution)/shard_map/ppermute | solution.py:706
  16.6 29.0 %collective-permute-start.5 = (bf16[4,512,128]{2,1,0:T(8,128)(2,1)}, bf16[4,512,128]{2,1,0:T(8,128)(2,1)}, u32[]{:S(2)}, u32[]{:S(2)}) collective-permute-start(bf16[4,512,128]{2,1,0:T(8,128)(2,1)} %pad_maximum_fusion.1), channel_id=1, source_target_pairs={{0,1},{1,0},{2,3},{3,2},{4,5},{5,4},{6,7},{7,6},{8,9},{9,8},{10,11... | collective-permute-start | bytes 1572872 | tf_op jit(solution)/shard_map/ppermute | solution.py:716
  21.3 24.2 %collective-permute-start.6 = (bf16[4,512,128]{2,1,0:T(8,128)(2,1)}, bf16[4,512,128]{2,1,0:T(8,128)(2,1)}, u32[]{:S(2)}, u32[]{:S(2)}) collective-permute-start(bf16[4,512,128]{2,1,0:T(8,128)(2,1)} %pad_maximum_fusion), channel_id=1, source_target_pairs={{1,2},{2,1},{3,4},{4,3},{5,6},{6,5},{9,10},{10,9},{11,12},{12,11},... | collective-permute-start | bytes 1572872 | tf_op jit(solution)/shard_map/ppermute | solution.py:717
  23.3 4.9 %copy-start.6 = (f32[256]{0:T(256)S(1)}, f32[256]{0:T(256)}, u32[]{:S(2)}) copy-start(f32[256]{0:T(256)} %param.16) | copy-start | bytes 3076
  23.3 14.7 %collective-permute-start.4 = (f32[2,2,16,128]{3,2,1,0:T(8,128)S(1)}, f32[2,2,16,128]{3,2,1,0:T(8,128)S(1)}, u32[]{:S(2)}, u32[]{:S(2)}) collective-permute-start(f32[2,2,16,128]{3,2,1,0:T(8,128)S(1)} %edges.1.rest_0_), channel_id=1, source_target_pairs={{24,0},{0,8},{8,16},{16,24},{25,1},{1,9},{9,17},{17,25},{26,2},{2,... | collective-permute-start | bytes 98312 | tf_op jit(solution)/shard_map/ppermute | solution.py:726
  23.7 17.2 %collective-permute-start.3 = (f32[2,2,16,128]{3,2,1,0:T(8,128)S(1)}, f32[2,2,16,128]{3,2,1,0:T(8,128)S(1)}, u32[]{:S(2)}, u32[]{:S(2)}) collective-permute-start(f32[2,2,16,128]{3,2,1,0:T(8,128)S(1)} %edges.1.rest_0_), channel_id=1, source_target_pairs={{16,0},{24,8},{0,16},{8,24},{17,1},{25,9},{1,17},{9,25},{18,2},{26... | collective-permute-start | bytes 98312 | tf_op jit(solution)/shard_map/ppermute | solution.py:726
  26.4 14.6 %collective-permute-start.2 = (f32[2,2,16,128]{3,2,1,0:T(8,128)S(1)}, f32[2,2,16,128]{3,2,1,0:T(8,128)S(1)}, u32[]{:S(2)}, u32[]{:S(2)}) collective-permute-start(f32[2,2,16,128]{3,2,1,0:T(8,128)S(1)} %edges.1.rest_0_), channel_id=1, source_target_pairs={{8,0},{16,8},{24,16},{0,24},{9,1},{17,9},{25,17},{1,25},{10,2},{18... | collective-permute-start | bytes 98312 | tf_op jit(solution)/shard_map/ppermute | solution.py:726
  28.1 7.2 %copy-start.8 = (s32[4,2,3]{0,1,2:T(2,128)S(1)}, s32[4,2,3]{0,1,2:T(2,128)}, u32[]{:S(2)}) copy-start(s32[4,2,3]{0,1,2:T(2,128)} %param.14) | copy-start | bytes 292
  28.1 7.3 %copy-start.1 = (bf16[1,1,2,4,512,128]{5,4,3,2,1,0:T(8,128)(2,1)S(1)}, bf16[1,1,2,4,512,128]{5,4,3,2,1,0:T(8,128)(2,1)}, u32[]{:S(2)}) copy-start(bf16[1,1,2,4,512,128]{5,4,3,2,1,0:T(8,128)(2,1)} %param.10) | copy-start | bytes 3145732
  28.1 7.3 %copy-start.3 = (bf16[1,1,2,4,512,128]{5,4,3,2,1,0:T(8,128)(2,1)S(1)}, bf16[1,1,2,4,512,128]{5,4,3,2,1,0:T(8,128)(2,1)}, u32[]{:S(2)}) copy-start(bf16[1,1,2,4,512,128]{5,4,3,2,1,0:T(8,128)(2,1)} %param.19) | copy-start | bytes 3145732
  42.2 12.9 %collective-permute-start.9 = (f32[2,2,16,256]{3,2,1,0:T(8,128)S(1)}, f32[2,2,16,256]{3,2,1,0:T(8,128)S(1)}, u32[]{:S(2)}, u32[]{:S(2)}) collective-permute-start(f32[2,2,16,256]{3,2,1,0:T(8,128)S(1)} %get-tuple-element.46.rest_0_), channel_id=1, source_target_pairs={{24,0},{0,8},{8,16},{16,24},{25,1},{1,9},{9,17},{17,25},{26,2},{2,... | collective-permute-start | bytes 196616 | tf_op jit(solution)/shard_map/ppermute | solution.py:726
  43.0 12.2 %collective-permute-start.8 = (f32[2,2,16,256]{3,2,1,0:T(8,128)S(1)}, f32[2,2,16,256]{3,2,1,0:T(8,128)S(1)}, u32[]{:S(2)}, u32[]{:S(2)}) collective-permute-start(f32[2,2,16,256]{3,2,1,0:T(8,128)S(1)} %get-tuple-element.46.rest_0_), channel_id=1, source_target_pairs={{16,0},{24,8},{0,16},{8,24},{17,1},{25,9},{1,17},{9,25},{18,2},{26... | collective-permute-start | bytes 196616 | tf_op jit(solution)/shard_map/ppermute | solution.py:726
  44.6 10.6 %collective-permute-start.7 = (f32[2,2,16,256]{3,2,1,0:T(8,128)S(1)}, f32[2,2,16,256]{3,2,1,0:T(8,128)S(1)}, u32[]{:S(2)}, u32[]{:S(2)}) collective-permute-start(f32[2,2,16,256]{3,2,1,0:T(8,128)S(1)} %get-tuple-element.46.rest_0_), channel_id=1, source_target_pairs={{8,0},{16,8},{24,16},{0,24},{9,1},{17,9},{25,17},{1,25},{10,2},{18... | collective-permute-start | bytes 196616 | tf_op jit(solution)/shard_map/ppermute | solution.py:726
  45.6 9.6 %copy-start.4 = (bf16[9,256,128]{2,1,0:T(8,128)(2,1)S(1)}, bf16[9,256,128]{2,1,0:T(8,128)(2,1)}, u32[]{:S(2)}) copy-start(bf16[9,256,128]{2,1,0:T(8,128)(2,1)} %k2_ref.3) | copy-start | bytes 1769476
  45.6 9.6 %copy-start.5 = (bf16[9,256,128]{2,1,0:T(8,128)(2,1)S(1)}, bf16[9,256,128]{2,1,0:T(8,128)(2,1)}, u32[]{:S(2)}) copy-start(bf16[9,256,128]{2,1,0:T(8,128)(2,1)} %get-tuple-element.45.k1t_ref) | copy-start | bytes 1769476
  57.2 17.7 %collective-permute-start.10 = (bf16[4,512,128]{2,1,0:T(8,128)(2,1)S(1)}, bf16[4,512,128]{2,1,0:T(8,128)(2,1)S(1)}, u32[]{:S(2)}, u32[]{:S(2)}) collective-permute-start(bf16[4,512,128]{2,1,0:T(8,128)(2,1)S(1)} %get-tuple-element.53), channel_id=1, source_target_pairs={{0,1},{1,0},{2,3},{3,2},{4,5},{5,4},{6,7},{7,6},{8,9},{9,8},{10,11... | collective-permute-start | bytes 1572872 | tf_op jit(solution)/shard_map/ppermute | solution.py:890
  59.0 8.3 %copy-start.7 = (f32[128]{0:T(128)S(1)}, f32[128]{0:T(128)}, u32[]{:S(2)}) copy-start(f32[128]{0:T(128)} %param.18) | copy-start | bytes 1540
  59.0 16.1 %collective-permute-start.11 = (bf16[4,512,128]{2,1,0:T(8,128)(2,1)S(1)}, bf16[4,512,128]{2,1,0:T(8,128)(2,1)S(1)}, u32[]{:S(2)}, u32[]{:S(2)}) collective-permute-start(bf16[4,512,128]{2,1,0:T(8,128)(2,1)S(1)} %get-tuple-element.47._.own_ref), channel_id=1, source_target_pairs={{1,2},{2,1},{3,4},{4,3},{5,6},{6,5},{9,10},{10,9},{11,12},{12,11},... | collective-permute-start | bytes 1572872 | tf_op jit(solution)/shard_map/ppermute | solution.py:891

commit v3 on v2

--- a/solution.py
+++ b/solution.py
@@ -150,13 +150,12 @@
     for start in range(0, count, block):
         same = column(dest_row, start) == dest_row
         later = (own + start) < other
-        earlier = (own + start) > other
         rank_row = rank_row + jnp.sum(
             jnp.where(same & later, 1.0, 0.0), axis=0, keepdims=True
         )
-        rank = jnp.sum(jnp.where(same & earlier, 1.0, 0.0), axis=1, keepdims=True)
+    for start in range(0, count, block):
         code = jnp.where(lane < HIGH, column(high_row, start), column(low_row, start))
-        coded.append(jnp.where(rank == lane_rank, code, 0.0).astype(BF16))
+        coded.append(jnp.where(column(rank_row, start) == lane_rank, code, 0.0).astype(BF16))
     to_device = (
         lax.broadcasted_iota(jnp.int32, (devices, count), 0).astype(F32) == dest_row
     )
@@ -272,27 +271,27 @@
                 k2t_ref[t] = k2_ref[t].astype(F32).T.astype(BF16)
         for i in range(2 * rows):
             cat[array, i] = spread_columns(source[i], order)
-        members, steps = row_groups(rows, way)[0]
-        lhs = jnp.concatenate(
-            [
-                jnp.concatenate(
-                    [cat[array, b * rows + r + way * (1 - 2 * b) * dy] for dy in steps], axis=1
-                )
-                for b, r in members
-            ],
-            axis=0,
-        )
-        taps = weights[...].reshape(3 * len(steps) * channels, lifted)
-        half = len(members) // 2
-        for first in (0, half):
-            total = dot(lhs[first * width : (first + half) * width], taps)
+        inner, first, last = row_groups(rows, way)
+        half = len(inner[0]) // 2
+        groups = ((inner[0][:half], inner[1]), (inner[0][half:], inner[1]), first, last)
+        for members, steps in groups:
+            lhs = jnp.concatenate(
+                [
+                    jnp.concatenate(
+                        [cat[array, b * rows + r + way * (1 - 2 * b) * dy] for dy in steps], axis=1
+                    )
+                    for b, r in members
+                ],
+                axis=0,
+            )
+            taps = weights[3 * (steps[0] + 1) : 3 * (steps[-1] + 2)]
+            total = dot(lhs, taps.reshape(3 * len(steps) * channels, lifted))
             if array == 0:
                 total = total + b1_ref[...]
-            for k in range(half):
-                held_rows[array, first + k] = total[k * width : (k + 1) * width]
-                store = pltpu.make_async_copy(
-                    held_rows.at[array, first + k], out.at[first + k], slot()
-                )
+            for k, (b, r) in enumerate(members):
+                i = b * rows + r
+                held_rows[array, i] = total[k * width : (k + 1) * width]
+                store = pltpu.make_async_copy(held_rows.at[array, i], out.at[i], slot())
                 store.start()
                 stores.append(store)
     for t in range(k1_ref.shape[0]):
@@ -301,13 +300,13 @@
         store.wait()
 
 
-def border_pieces(array, pair, outside, own, inside):
-    first = (pair[0] == 0) == (array == 0)
-    return [outside, own, inside] if first else [inside, own, outside]
+def row_onehot(keys, row, width):
+    column = lax.broadcasted_iota(jnp.int32, (width, keys.shape[1]), 0).astype(F32)
+    return jnp.where(column == keys[0:1, :] - float(row * width), 1.0, 0.0).astype(BF16)
 
 
 def rim_in_body(
-    rows, matching_ref, k1_in, b1_ref, k2t_in, pre_lo, pre_hi, grad_lo, grad_hi, x_lo, x_hi, c_lo, c_hi,
+    rows, matching_ref, k1_in, k2t_in, pre_lo, pre_hi, grad_lo, grad_hi, x_lo, x_hi, c_lo, c_hi,
     a_lo, a_hi, b_lo, b_hi, base_ref, taps_ref, k1_ref, k2t_ref, sem,
 ):
     loads = [
@@ -330,47 +329,34 @@
     outside = end_rows(rows, x_ends, c_ends, whole((a_lo, a_hi)), whole((b_lo, b_hi)))
     channels, lifted = k1_ref.shape[1], k1_ref.shape[2]
     base_ref[...] = jnp.zeros_like(base_ref)
-    for array, (strips, own, weights, order) in enumerate(
-        (
-            ((pre_lo, pre_hi), x_ends, k1_ref, (-1, 0, 1)),
-            ((grad_lo, grad_hi), c_ends, k2t_ref, (1, 0, -1)),
-        )
+    for array, (strips, weights, order) in enumerate(
+        (((pre_lo, pre_hi), k1_ref, (-1, 0, 1)), ((grad_lo, grad_hi), k2t_ref, (1, 0, -1)))
     ):
         for side in range(2):
             spot = 0 if side == 0 else GROUP - 1
             for b in range(2):
-                for r in range(1, rows - 1):
+                for r in range(rows):
                     at = 2 * GROUP * side + GROUP * b + r + 1
                     base_ref[array, at : at + 1, :] = strips[side][
-                        b * (rows - 2) + r - 1, spot : spot + 1, :
+                        b * rows + r, spot : spot + 1, :
                     ]
         for pair in ((0, 3), (1, 2)):
             spots = [(side, j) for side in range(2) for j in pair]
-            lhs = []
-            for side, j in spots:
-                i = border_index(j, rows)
-                planes = border_pieces(
-                    array, pair, outside[array, side, j], own[side][i], own[side][i + 1 - 2 * (j % 2)]
-                )
-                lhs.append(
-                    jnp.concatenate([spread_columns(plane, order) for plane in planes], axis=1)
-                )
+            lhs = [spread_columns(outside[array, side, j], order) for side, j in spots]
+            row = 0 if (pair[0] == 0) == (array == 0) else 6
             found = dot(
-                jnp.concatenate(lhs, axis=0),
-                weights[...].reshape(weights.shape[0] * channels, lifted),
+                jnp.concatenate(lhs, axis=0), weights[row : row + 3].reshape(3 * channels, lifted)
             )
-            if array == 0:
-                found = found + b1_ref[...]
             strip = found.shape[0] // len(spots)
             for k, (side, j) in enumerate(spots):
                 at = 2 * GROUP * side + GROUP * (j // 2) + 1 + (rows - 1) * (j % 2)
                 spot = k * strip + (0 if side == 0 else strip - 1)
-                base_ref[array, at : at + 1, :] = found[spot : spot + 1]
-
-
-def side_in_body(faces, matching_ref, taps_ref, base_ref, *rest):
+                base_ref[array, at : at + 1, :] += found[spot : spot + 1]
+
+
+def rim_body(rows, faces, matching_ref, taps_ref, base_ref, found_ref, *rest):
     parts = rest[:faces]
-    x_side, c_side, sums_ref = rest[faces:]
+    x_side, c_side, edge_ref = rest[faces:]
     taps = taps_ref[...].reshape(2, 2, 3 * taps_ref.shape[3], taps_ref.shape[4])
     for side in range(2):
         hop, their_side, flipped = matched(matching_ref, side, faces)
@@ -379,8 +365,13 @@
             way = 1 - 2 * array
             lhs = jnp.concatenate([rolled_rows(near, way * dy) for dy in (-1, 0, 1)], axis=1)
             out[side] = dot(lhs, taps[array, side])
-    for array, out in enumerate((x_side, c_side)):
-        sums_ref[array] = base_ref[array] + out[...].reshape(sums_ref.shape[1:])
+    e = lax.broadcasted_iota(jnp.int32, (4 * GROUP, 1), 0) & (GROUP - 1)
+    inside = (e >= 1) & (e <= rows)
+    shape = base_ref.shape[1:]
+    v = base_ref[0] + x_side[...].reshape(shape) + found_ref[...]
+    inner, gp = gelu_pair(v, base_ref[1] + c_side[...].reshape(shape))
+    edge_ref[0] = jnp.where(inside, inner.astype(F32), 0.0).reshape(edge_ref.shape[1:])
+    edge_ref[1] = jnp.where(inside, gp.astype(F32), 0.0).reshape(edge_ref.shape[1:])
 
 
 def gelu_pair(v, grad):
@@ -422,7 +413,28 @@
     return mid + shift_columns(left, step) + shift_columns(right, -step)
 
 
-def rim_body(rows, width, capacity, recv_ref, base_ref, edge_ref, values, keys):
+def found_body(
+    rows, capacity, recv_in, pre_in, grad_in, k1_in, k2t_in, values, keys, pre_b, grad_b, found_b, rim_ref,
+    taps, recv_ref, sem,
+):
+    width = pre_b.shape[1]
+    loads = [pltpu.make_async_copy(recv_in, recv_ref, sem.at[0])]
+    for j in range(4):
+        row = border_index(j, rows)
+        loads.append(pltpu.make_async_copy(pre_in.at[row], pre_b.at[j], sem.at[1 + j]))
+    for j in range(4):
+        row = border_index(j, rows)
+        loads.append(pltpu.make_async_copy(grad_in.at[row], grad_b.at[j], sem.at[5 + j]))
+    for array, source in enumerate((k1_in, k2t_in)):
+        for k in range(2):
+            loads.append(
+                pltpu.make_async_copy(
+                    source.at[6 * k : 6 * k + 3], taps.at[array, k], sem.at[9 + 2 * array + k]
+                )
+            )
+    for load in loads:
+        load.start()
+    loads[0].wait()
     unpack_received(capacity, recv_ref, values, keys)
     at = lax.broadcasted_iota(jnp.int32, (4 * GROUP, 1), 0)
     e = at & (GROUP - 1)
@@ -432,37 +444,40 @@
     pixel = (b * rows + e - 1) * width + side * (width - 1)
     wanted = jnp.where(inside, pixel, -1).astype(F32)
     onehot = jnp.where(keys[0:1, :] == wanted, 1.0, 0.0).astype(BF16)
-    v = base_ref[0] + dot(onehot, values[...])
-    inner, gp = gelu_pair(v, base_ref[1])
-    shape = (2, 2 * GROUP, v.shape[1])
-    edge_ref[0] = jnp.where(inside, inner.astype(F32), 0.0).reshape(shape)
-    edge_ref[1] = jnp.where(inside, gp.astype(F32), 0.0).reshape(shape)
+    rim_ref[...] = dot(onehot, values[...])
+    for half in range(2):
+        members = (2 * half, 2 * half + 1)
+        found = dot(
+            jnp.concatenate(
+                [row_onehot(keys, border_index(j, rows), width) for j in members], axis=0
+            ),
+            values[...],
+        )
+        for k, j in enumerate(members):
+            found_b[j] = found[k * width : (k + 1) * width]
+    for load in loads[1:]:
+        load.wait()
 
 
 def border_body(
-    rows, values, keys, x_side, c_side, b1_ref, a_in, b_in, x_in, c_in, k1_in, k2t_in, inner_ref, gp_ref,
-    x_ref, c_ref, outside, k1_ref, k2t_ref, sem,
+    rows, pre_b, grad_b, found_b, taps, x_side, c_side, a_in, b_in, x_in, c_in, inner_ref, gp_ref, outside,
+    sem,
 ):
     width, lifted = inner_ref.shape[1], inner_ref.shape[2]
     channels = outside.shape[3]
     even, last = is_even(), is_last()
-    waits = []
-
-    def load(target, *sources):
-        slot = sem.at[len(waits)]
+    waits = [[], []]
+    used = [0]
+
+    def load(array, target, *sources):
+        slot = sem.at[used[0]]
+        used[0] += 1
         for condition, source in sources:
             copy = pltpu.make_async_copy(source, target, slot)
-            if condition is None:
-                copy.start()
-            else:
-                pl.when(condition)(copy.start)
-        waits.append(copy)
-
-    for array, (source, target, weights, held_weights) in enumerate(
-        ((x_in, x_ref, k1_in, k1_ref), (c_in, c_ref, k2t_in, k2t_ref))
-    ):
-        load(target, (None, source))
-        load(held_weights, (None, weights))
+            pl.when(condition)(copy.start)
+        waits[array].append(copy)
+
+    for array, source in enumerate((x_in, c_in)):
         for j in range(4):
             band = j // 2
             plane = 2 * array + band
@@ -472,49 +487,28 @@
                 fold = source.at[(1 - band) * rows + rows - 1]
                 middle = jnp.logical_not(even) & jnp.logical_not(last)
                 choices = ((last, fold), (even, a_in.at[plane]), (middle, b_in.at[plane]))
-            load(outside.at[array, j], *choices)
-
-    column = lax.broadcasted_iota(jnp.int32, (width, keys.shape[1]), 0).astype(F32)
+            load(array, outside.at[array, j], *choices)
+
+    for copy in waits[0] + waits[1]:
+        copy.wait()
     for pair in ((0, 3), (1, 2)):
-        onehot = jnp.concatenate(
-            [
-                jnp.where(
-                    column == keys[0:1, :] - float(border_index(j, rows) * width), 1.0, 0.0
-                ).astype(BF16)
-                for j in pair
-            ],
-            axis=0,
-        )
-        found = dot(onehot, values[...]) + b1_ref[...]
         totals = []
-        for array, (own, weights, order) in enumerate(
-            ((x_ref, k1_ref, (-1, 0, 1)), (c_ref, k2t_ref, (1, 0, -1)))
-        ):
-            if pair[0] == 0:
-                for copy in waits[6 * array : 6 * array + 6]:
-                    copy.wait()
-            lhs = []
-            for j in pair:
-                i = border_index(j, rows)
-                planes = border_pieces(
-                    array, pair, outside[array, j], own[i], own[i + 1 - 2 * (j % 2)]
-                )
-                lhs.append(
-                    jnp.concatenate([spread_columns(plane, order) for plane in planes], axis=1)
-                )
-            totals.append(
-                dot(
-                    jnp.concatenate(lhs, axis=0),
-                    weights[...].reshape(weights.shape[0] * channels, lifted),
-                )
-            )
-        v = found + totals[0]
+        for array, order in enumerate(((-1, 0, 1), (1, 0, -1))):
+            lhs = [spread_columns(outside[array, j], order) for j in pair]
+            tap = taps[array, 0 if (pair[0] == 0) == (array == 0) else 1]
+            totals.append(dot(jnp.concatenate(lhs, axis=0), tap.reshape(3 * channels, lifted)))
         for k, j in enumerate(pair):
             at = GROUP * (j // 2) + 1 + (rows - 1) * (j % 2)
             piece = slice(k * width, (k + 1) * width)
             inner, gp = gelu_pair(
-                add_edges(v[piece], x_side[0, at : at + 1, :], x_side[1, at : at + 1, :]),
-                add_edges(totals[1][piece], c_side[0, at : at + 1, :], c_side[1, at : at + 1, :]),
+                add_edges(
+                    totals[0][piece] + (pre_b[j] + found_b[j]),
+                    x_side[0, at : at + 1, :],
+                    x_side[1, at : at + 1, :],
+                ),
+                add_edges(
+                    totals[1][piece] + grad_b[j], c_side[0, at : at + 1, :], c_side[1, at : at + 1, :]
+                ),
             )
             inner_ref[j] = inner
             gp_ref[j] = gp
@@ -549,27 +543,34 @@
                 target[2 * array + band] = part.astype(BF16)
 
 
-def middle_body(rows, _, values, keys, *rest):
+def middle_body(
+    rows, _, values, keys, pre_in, grad_in, x_side, c_side, inner_ref, gp_ref, base, sem
+):
     middle = rows - 2
-    pre_refs, grad_refs = rest[:middle], rest[middle : 2 * middle]
-    x_side, c_side, inner_ref, gp_ref = rest[2 * middle :]
-    band = pl.program_id(0)
-    width, lifted = pre_refs[0].shape[1], pre_refs[0].shape[2]
-    column = lax.broadcasted_iota(jnp.int32, (width, keys.shape[1]), 0).astype(F32)
-    onehots = []
-    for k in range(middle):
-        local = keys[0:1, :] - ((band * rows + k + 1) * width).astype(F32)
-        onehots.append(jnp.where(column == local, 1.0, 0.0).astype(BF16))
-    found = dot(jnp.concatenate(onehots, axis=0), values[...])
-    for k in range(middle):
-        at = band * GROUP + k + 2
+    width = base.shape[2]
+    members = [(b, r) for b in range(2) for r in range(1, rows - 1)]
+    loads = []
+    for k in range(len(members)):
+        for array, source in enumerate((pre_in, grad_in)):
+            row = members[k][0] * rows + members[k][1]
+            load = pltpu.make_async_copy(source.at[row], base.at[array, k], sem.at[2 * k + array])
+            load.start()
+            loads.append(load)
+    found = dot(
+        jnp.concatenate([row_onehot(keys, b * rows + r, width) for b, r in members], axis=0),
+        values[...],
+    )
+    for k, (b, r) in enumerate(members):
+        at = b * GROUP + r + 1
+        loads[2 * k].wait()
+        loads[2 * k + 1].wait()
         inner, gp = gelu_pair(
             add_edges(
-                pre_refs[k][0] + found[k * width : (k + 1) * width],
-                x_side[0, pl.ds(at, 1), :],
-                x_side[1, pl.ds(at, 1), :],
+                base[0, k] + found[k * width : (k + 1) * width],
+                x_side[0, at : at + 1, :],
+                x_side[1, at : at + 1, :],
             ),
-            add_edges(grad_refs[k][0], c_side[0, pl.ds(at, 1), :], c_side[1, pl.ds(at, 1), :]),
+            add_edges(base[1, k], c_side[0, at : at + 1, :], c_side[1, at : at + 1, :]),
         )
         inner_ref[k] = inner
         gp_ref[k] = gp
@@ -710,11 +711,6 @@
     border_rows = lambda at: jnp.concatenate([low_row(x, at), low_row(c, at)], axis=0)
     pair_out = border_rows(jnp.where(even, rows - 1, 0))
     cross_out = border_rows(jnp.where(even, 0, rows - 1))
-    cross_out, pair_ends, cross_ends = lax.optimization_barrier(
-        (cross_out, pair_ends, cross_ends)
-    )
-    pair_rows = lax.ppermute(pair_out, "tile", pairs)
-    cross_rows = lax.ppermute(cross_out, "tile", crosses)
     smem = pl.BlockSpec(memory_space=pltpu.SMEM)
     vmem = pl.BlockSpec(memory_space=pltpu.VMEM)
     hbm = pl.BlockSpec(memory_space=pl.ANY)
@@ -756,7 +752,7 @@
         functools.partial(lift_body, rows),
         in_specs=[hbm] * 4 + [vmem],
         out_specs=[hbm] * 2 + [vmem] * 2,
-        out_shape=[pltpu.HBM((2 * middle, width, lifted), F32)] * 2
+        out_shape=[pltpu.HBM((all_rows, width, lifted), F32)] * 2
         + [pltpu.HBM(kernel_two.shape, BF16), pltpu.HBM(kernel_one.shape, BF16)],
         scratch_shapes=[
             pltpu.VMEM(x.shape, BF16),
@@ -764,14 +760,19 @@
             pltpu.VMEM(kernel_one.shape, BF16),
             pltpu.VMEM(kernel_two.shape, BF16),
             pltpu.VMEM((2, all_rows, width, 3 * channels), BF16),
-            pltpu.VMEM((2, 2 * middle, width, lifted), F32),
-            pltpu.SemaphoreType.DMA((4 + 4 * middle,)),
+            pltpu.VMEM((2, all_rows, width, lifted), F32),
+            pltpu.SemaphoreType.DMA((4 + 2 * all_rows,)),
         ],
         compiler_params=params(40),
         cost_estimate=cost(conv_flops, 8 << 20),
         name="lift",
     )(far(x), far(c), far(kernel_one), far(kernel_two), b1)
     pre, grad_inner = far(pre), far(grad_inner)
+    pair_out, cross_out, pair_ends, cross_ends, k1t = lax.optimization_barrier(
+        (pair_out, cross_out, pair_ends, cross_ends, k1t)
+    )
+    pair_rows = lax.ppermute(pair_out, "tile", pairs)
+    cross_rows = lax.ppermute(cross_out, "tile", crosses)
     low = lambda n: pl.BlockSpec((n, strip, channels), lambda *_: (0, 0, 0))
     high = lambda n, at: pl.BlockSpec((n, strip, channels), lambda *_: (0, at, 0))
     tail = width // strip - 1
@@ -790,13 +791,13 @@
 
     side_in = (2, 2 * GROUP, lifted)
     end = width // GROUP - 1
-    edge_strip = lambda at: pl.BlockSpec((2 * middle, GROUP, lifted), lambda *_: (0, at, 0))
+    edge_strip = lambda at: pl.BlockSpec((all_rows, GROUP, lifted), lambda *_: (0, at, 0))
     rim_shape = (2, 4 * GROUP, lifted)
     taps_shape = (2, 2, 3, channels, lifted)
     rim_base, side_taps = pl.pallas_call(
         functools.partial(rim_in_body, rows),
         grid=(1,),
-        in_specs=[smem, hbm, fixed(b1.shape), hbm]
+        in_specs=[smem, hbm, hbm]
         + [edge_strip(0), edge_strip(end)] * 2
         + [low(all_rows), high(all_rows, tail)] * 2
         + [low(4), high(4, 1)] * 2,
@@ -811,65 +812,70 @@
         cost_estimate=cost(0, 2 << 20),
         name="rim_in",
     )(
-        matching, far(kernel_one), b1, far(k2t), pre, pre, grad_inner, grad_inner, x, x, c, c, pair_ends,
+        matching, far(kernel_one), far(k2t), pre, pre, grad_inner, grad_inner, x, x, c, c, pair_ends,
         pair_ends, cross_ends, cross_ends,
     )
-    x_side, c_side, rim_sums = pl.pallas_call(
-        functools.partial(side_in_body, faces),
-        in_specs=[smem] + [vmem] * (2 + faces),
-        out_specs=[vmem] * 3,
-        out_shape=[
-            jax.ShapeDtypeStruct(side_in, F32),
-            jax.ShapeDtypeStruct(side_in, F32),
-            jax.ShapeDtypeStruct(rim_shape, F32),
-        ],
-        compiler_params=params(8),
-        cost_estimate=cost(0, 1 << 20),
-        name="sides_in",
-    )(matching, side_taps, rim_base, *parts)
-
     side_two = (2, 2, 2 * GROUP, lifted)
     slots = devices * capacity
     onehot_flops = 2 * width * slots * lifted
     other_block = pl.BlockSpec(
         (1, width, channels), lambda j: ((1 - j // 2) * rows + rows - 1, 0, 0)
     )
-    edges_two, values, keys = pl.pallas_call(
-        functools.partial(rim_body, rows, width, capacity),
-        in_specs=[vmem] * 2,
+    values, keys, pre_b, grad_b, found_b, rim_found, rim_taps = pl.pallas_call(
+        functools.partial(found_body, rows, capacity),
+        in_specs=[hbm] * 5,
+        out_specs=[vmem] * 7,
+        out_shape=[
+            hold((slots, lifted), BF16),
+            hold((PIXEL_ROWS, slots), F32),
+            hold((4, width, lifted), F32),
+            hold((4, width, lifted), F32),
+            hold((4, width, lifted), F32),
+            hold(rim_shape[1:], F32),
+            hold((2, 2, 3, channels, lifted), BF16),
+        ],
+        scratch_shapes=[
+            pltpu.VMEM(received.shape, BF16),
+            pltpu.SemaphoreType.DMA((13,)),
+        ],
+        compiler_params=params(),
+        cost_estimate=cost(4 * onehot_flops, 6 << 20),
+        name="found",
+    )(far(received), pre, grad_inner, far(kernel_one), far(k2t))
+    values, keys, pre_b, grad_b = held(values), held(keys), held(pre_b), held(grad_b)
+    found_b = held(found_b)
+    x_side, c_side, edges_two = pl.pallas_call(
+        functools.partial(rim_body, rows, faces),
+        in_specs=[smem] + [vmem] * (3 + faces),
         out_specs=[vmem] * 3,
         out_shape=[
+            hold(side_in, F32),
+            hold(side_in, F32),
             jax.ShapeDtypeStruct(side_two, F32),
-            hold((slots, lifted), BF16),
-            hold((PIXEL_ROWS, slots), F32),
         ],
         compiler_params=params(8),
-        cost_estimate=cost(0, 3 << 20),
+        cost_estimate=cost(0, 1 << 20),
         name="rim",
-    )(received, rim_sums)
-    values, keys = held(values), held(keys)
+    )(matching, side_taps, rim_base, held(rim_found), *parts)
+    x_side, c_side = held(x_side), held(c_side)
     parts_two = exchange(edges_two)
 
     border_shape = hold((4, width, lifted), BF16)
     inner_b, gp_b = pl.pallas_call(
         functools.partial(border_body, rows),
-        in_specs=[vmem] * 5 + [hbm] * 6,
+        in_specs=[vmem] * 6 + [hbm] * 4,
         out_specs=[vmem] * 2,
         out_shape=[border_shape] * 2,
         scratch_shapes=[
-            pltpu.VMEM(x.shape, BF16),
-            pltpu.VMEM(c.shape, BF16),
             pltpu.VMEM((2, 4, width, channels), BF16),
-            pltpu.VMEM(kernel_one.shape, BF16),
-            pltpu.VMEM(k2t.shape, BF16),
-            pltpu.SemaphoreType.DMA((12,)),
-        ],
-        compiler_params=params(32),
-        cost_estimate=cost(4 * onehot_flops + conv_flops // 6, 10 << 20),
+            pltpu.SemaphoreType.DMA((8,)),
+        ],
+        compiler_params=params(),
+        cost_estimate=cost(conv_flops // 6, 4 << 20),
         name="border",
     )(
-        values, keys, x_side, c_side, b1, far(pair_rows), far(cross_rows), far(x), far(c),
-        far(kernel_one), far(k2t),
+        pre_b, grad_b, found_b, held(rim_taps), x_side, c_side, far(pair_rows), far(cross_rows), far(x),
+        far(c),
     )
     inner_b, gp_b = held(inner_b), held(gp_b)
 
@@ -890,19 +896,19 @@
     from_pair = lax.ppermute(to_pair, "tile", pairs)
     from_cross = lax.ppermute(to_cross, "tile", crosses)
 
-    middle_block = lambda k: pl.BlockSpec((1, width, lifted), lambda i: (i * middle + k, 0, 0))
     inner_m, gp_m = pl.pallas_call(
         functools.partial(middle_body, rows),
-        grid=(2,),
-        in_specs=[hbm, fixed(values.shape), fixed(keys.shape)]
-        + [middle_block(k) for k in range(middle)] * 2
-        + [fixed(side_in)] * 2,
-        out_specs=[pl.BlockSpec((middle, width, lifted), lambda i: (i, 0, 0))] * 2,
+        in_specs=[hbm, vmem, vmem, hbm, hbm, vmem, vmem],
+        out_specs=[vmem] * 2,
         out_shape=[hold((2 * middle, width, lifted), BF16)] * 2,
-        compiler_params=params(),
+        scratch_shapes=[
+            pltpu.VMEM((2, 2 * middle, width, lifted), F32),
+            pltpu.SemaphoreType.DMA((4 * middle,)),
+        ],
+        compiler_params=params(32),
         cost_estimate=cost(2 * middle * onehot_flops, 10 << 20),
         name="middle",
-    )(to_cross, values, keys, *[pre] * middle, *[grad_inner] * middle, x_side, c_side)
+    )(to_cross, values, keys, pre, grad_inner, x_side, c_side)
     inner_m, gp_m = held(inner_m), held(gp_m)
 
     analysis, ana_b, grad_state, grad_b = pl.pallas_call(

time: 76.9 us -> 74.5 us (0.969)
  Pallas kernels: 40.6 us -> 38.8 us
  waiting for transfers between devices: 7.11 us -> 5.74 us
    ppermute x1, waiting for transfers between devices: 3.95 us -> 0.01 us  [per_device(): lax.ppermute(ends(jnp.where(even, 0, rows - 1)), 'tile', crosses)]
    all_to_all x1, waiting for transfers between devices: 0.01 us -> 3.79 us  [per_device(): received = lax.all_to_all(packed, ('face', 'tile'), 0, 0, tiled=True)]
    pallas_call x4, Pallas kernels: 15.9 us -> 12.8 us  [the longest x1 4.19 us: per_device(): pl.pallas_call(functools.partial(middle_body, rows), in_specs=[hbm, vmem,...]
    pallas_call x1, Pallas kernels: 7.14 us -> 9 us  [per_device(): pl.pallas_call(functools.partial(lift_body, rows), in_specs=[hbm] * 4 + [...]
    ppermute x6, waiting for transfers between devices: 2.88 us -> 1.08 us  [exchange(): lax.ppermute(own, 'face', [((i + k) % faces, i) for i in range(faces)])]
    ppermute x1, starting transfers between devices: 1.91 us -> 3.47 us  [per_device(): cross_rows = lax.ppermute(cross_out, 'tile', crosses)]
    ppermute x6, starting transfers between devices: 8.13 us -> 7.01 us  [exchange(): lax.ppermute(own, 'face', [((i + k) % faces, i) for i in range(faces)])]
  transfers between devices with their start and end apart: 13 -> 13, of which waited for: 3 -> 3; matrix products, arithmetic and copies ran while one was open for 2% -> 3% of each run, Pallas kernels for 43% -> 43%
where the time goes in v3:
time: 74.5 us; the launch traced here: 74.1 us
  Pallas kernels  38.8 us (52%)
  starting transfers between devices  26.5 us (36%)
  waiting for transfers between devices  5.74 us (8%)
  other arithmetic  1.71 us (2%)
  between operations  1.08 us (1%)
    pallas_call x1, Pallas kernels, per_device(): pl.pallas_call(functools.partial(lift_body, rows), in_specs=[hbm] * 4 + [...  9 us
    pallas_call x1, Pallas kernels, per_device(): pl.pallas_call(functools.partial(inside_body, rows), in_specs=[vmem] * 8...  7.52 us
    all_to_all x1, starting transfers between devices, per_device(): received = lax.all_to_all(packed, ('face', 'tile'), 0, 0, tiled=True)  7.15 us
    ppermute x6, starting transfers between devices, exchange(): lax.ppermute(own, 'face', [((i + k) % faces, i) for i in range(faces)])  7.01 us
    pallas_call x1, Pallas kernels, per_device(): pl.pallas_call(functools.partial(middle_body, rows), in_specs=[hbm, vmem,...  4.19 us
    pallas_call x1, Pallas kernels, per_device(): pl.pallas_call(functools.partial(found_body, rows, capacity), in_specs=[h...  3.96 us
    pallas_call x1, Pallas kernels, per_device(): pl.pallas_call(functools.partial(pack_body, capacity), in_specs=[hbm] * 3...  3.81 us
    all_to_all x1, waiting for transfers between devices, per_device(): received = lax.all_to_all(packed, ('face', 'tile'), 0, 0, tiled=True)  3.79 us
  transfers between devices with their start and end apart: 13, of which 3 were waited for; matrix products, arithmetic and copies ran while one was open for 3% of the time, Pallas kernels for 43%

profile of v3, /device:TPU:1, one launch (start us, length us, event | category | flops | bytes accessed | tf_op | source)
XLA Modules:
  0.0 74.1 jit_solution(9387519709200688211)
XLA Ops:
  0.6 3.8 %pack.1 = bf16[32,136,128]{2,1,0:T(8,128)(2,1)} custom-call(s32[1,1024]{1,0:T(1,128)} %bitcast.50, s32[1,1024]{1,0:T(1,128)} %bitcast.51, bf16[1024,256]{1,0:T(8,128)(2,1)} %values_in.1), custom_call_target="tpu_custom_call" | custom-call | flops 1073741824 | bytes 2097152 | tf_op jit(solution)/shard_map/pack/pallas_call | solution.py:726
  4.5 7.2 %all-to-all-start = ((bf16[32,136,128]{2,1,0:T(8,128)(2,1)}), bf16[32,136,128]{2,1,0:T(8,128)(2,1)}, u32[]{:S(2)}, u32[]{:S(2)}) async-start(bf16[32,136,128]{2,1,0:T(8,128)(2,1)} %pack.1), calls=%async_computation | async-start | bytes 2228224 | tf_op jit(solution)/shard_map/all_to_all | solution.py:743
  12.1 3.4 %collective-permute-start.1 = (bf16[4,32,128]{2,1,0:T(8,128)(2,1)S(1)}, bf16[4,32,128]{2,1,0:T(8,128)(2,1)S(1)}, u32[]{:S(2)}, u32[]{:S(2)}) collective-permute-start(bf16[4,32,128]{2,1,0:T(8,128)(2,1)S(1)} %maximum_maximum_fusion.1), channel_id=1, source_target_pairs={{1,2},{2,1},{3,4},{4,3},{5,6},{6,5},{9,10},{10,9},{11,12},{12,11},... | collective-permute-start | bytes 98312 | tf_op jit(solution)/shard_map/ppermute | solution.py:707
  15.6 0.9 %pad_maximum_fusion = bf16[4,512,128]{2,1,0:T(8,128)(2,1)} fusion(bf16[2,512,128]{2,1,0:T(8,128)(2,1)S(1)} %get-tuple-element.81, bf16[2,512,128]{2,1,0:T(8,128)(2,1)S(1)} %get-tuple-element.82), kind=kLoop, calls=%fused_computation | loop fusion | flops 262144 | bytes 1048576 | tf_op jit(solution)/shard_map/concatenate | solution.py:711
  16.4 9.0 %lift.1 = (f32[8,512,256]{2,1,0:T(8,128)}, f32[8,512,256]{2,1,0:T(8,128)}, bf16[9,256,128]{2,1,0:T(8,128)(2,1)}, bf16[9,128,256]{2,1,0:T(8,128)(2,1)}) custom-call(bf16[8,512,128]{2,1,0:T(8,128)(2,1)} %bitcast.32, bf16[8,512,128]{2,1,0:T(8,128)(2,1)} %bitcast.39, bf16[9,128,256]{2,1,0:T(8,128)(2,1)} %k1_in.5, bf16[9,256,128]{2,1,0:T(8,128)(2,1)} %k2_ref.3, ...), custom_call_target="tpu_custom_call" | custom-call | flops 2415919104 | bytes 8388608 | tf_op jit(solution)/shard_map/lift/pallas_call | solution.py:751
  25.4 0.8 %pad_maximum_fusion.1 = bf16[4,512,128]{2,1,0:T(8,128)(2,1)} fusion(bf16[2,512,128]{2,1,0:T(8,128)(2,1)S(1)} %get-tuple-element.80, bf16[2,512,128]{2,1,0:T(8,128)(2,1)S(1)} %get-tuple-element.83), kind=kLoop, calls=%fused_computation.1 | loop fusion | flops 262144 | bytes 1048576 | tf_op jit(solution)/shard_map/concatenate | solution.py:711
  26.3 3.5 %collective-permute-start.6 = (bf16[4,512,128]{2,1,0:T(8,128)(2,1)}, bf16[4,512,128]{2,1,0:T(8,128)(2,1)}, u32[]{:S(2)}, u32[]{:S(2)}) collective-permute-start(bf16[4,512,128]{2,1,0:T(8,128)(2,1)} %pad_maximum_fusion.1), channel_id=1, source_target_pairs={{1,2},{2,1},{3,4},{4,3},{5,6},{6,5},{9,10},{10,9},{11,12},{12,11},... | collective-permute-start | bytes 1572872 | tf_op jit(solution)/shard_map/ppermute | solution.py:775
  29.9 3.1 %collective-permute-start.2 = (f32[2,2,16,128]{3,2,1,0:T(8,128)S(1)}, f32[2,2,16,128]{3,2,1,0:T(8,128)S(1)}, u32[]{:S(2)}, u32[]{:S(2)}) collective-permute-start(f32[2,2,16,128]{3,2,1,0:T(8,128)S(1)} %edges.1.rest_0_), channel_id=1, source_target_pairs={{8,0},{16,8},{24,16},{0,24},{9,1},{17,9},{25,17},{1,25},{10,2},{18... | collective-permute-start | bytes 98312 | tf_op jit(solution)/shard_map/ppermute | solution.py:722
  33.5 2.5 %rim_in.1 = (f32[2,32,256]{2,1,0:T(8,128)S(1)}, bf16[2,2,3,128,256]{4,3,2,1,0:T(8,128)(2,1)S(1)}) custom-call(s32[4,2,3]{2,1,0:T(2,128)S(1)} %copy.15.matching_ref, bf16[9,128,256]{2,1,0:T(8,128)(2,1)} %k1_in.5, bf16[9,128,256]{2,1,0:T(8,128)(2,1)} %get-tuple-element.38.k2t_in, f32[8,512,256]{2,1,0:T(8,128)} %get-tuple-element.36.pre_in.pre_lo.pre_hi, ...), custom_call_target="tpu_custom_call" | custom-call | bytes 2097152 | tf_op jit(solution)/shard_map/rim_in/pallas_call | solution.py:797
  36.0 3.8 %all-to-all-done.recv_in = bf16[32,136,128]{2,1,0:T(8,128)(2,1)} async-done(((bf16[32,136,128]{2,1,0:T(8,128)(2,1)}), bf16[32,136,128]{2,1,0:T(8,128)(2,1)}, u32[]{:S(2)}, u32[]{:S(2)}) %all-to-all-start) | async-done | bytes 1114144 | tf_op jit(solution)/shard_map/all_to_all | solution.py:743
  39.8 4.0 %found.1 = (bf16[2048,256]{1,0:T(8,128)(2,1)S(1)}, f32[8,2048]{1,0:T(8,128)S(1)}, f32[4,512,256]{2,1,0:T(8,128)S(1)}, f32[4,512,256]{2,1,0:T(8,128)S(1)}, f32[4,...) custom-call(bf16[32,136,128]{2,1,0:T(8,128)(2,1)} %all-to-all-done.recv_in, ...), custom_call_target="tpu_custom_call" | custom-call | flops 2147483648 | bytes 6291456 | tf_op jit(solution)/shard_map/found/pallas_call | solution.py:824
  43.8 0.8 %rim.1 = (f32[2,16,256]{2,1,0:T(8,128)S(1)}, f32[2,16,256]{2,1,0:T(8,128)S(1)}, f32[2,2,16,256]{3,2,1,0:T(8,128)S(1)}) custom-call(s32[4,2,3]{2,1,0:T(2,128)S(1)} %copy.15.matching_ref, bf16[2,2,3,128,256]{4,3,2,1,0:T(8,128)(2,1)S(1)} %get-tuple-element.46.taps_ref, f32[2,32,256]{2,1,0:T(8,128)S(1)} %get-tuple-element.47.base_ref, ...), custom_call_target="tpu_custom_call" | custom-call | bytes 1048576 | tf_op jit(solution)/shard_map/rim/pallas_call | solution.py:847
  44.7 1.7 %collective-permute-start.7 = (f32[2,2,16,256]{3,2,1,0:T(8,128)S(1)}, f32[2,2,16,256]{3,2,1,0:T(8,128)S(1)}, u32[]{:S(2)}, u32[]{:S(2)}) collective-permute-start(f32[2,2,16,256]{3,2,1,0:T(8,128)S(1)} %get-tuple-element.56.rest_0_), channel_id=1, source_target_pairs={{8,0},{16,8},{24,16},{0,24},{9,1},{17,9},{25,17},{1,25},{10,2},{18... | collective-permute-start | bytes 196616 | tf_op jit(solution)/shard_map/ppermute | solution.py:722
  46.4 0.9 %collective-permute-start.8 = (f32[2,2,16,256]{3,2,1,0:T(8,128)S(1)}, f32[2,2,16,256]{3,2,1,0:T(8,128)S(1)}, u32[]{:S(2)}, u32[]{:S(2)}) collective-permute-start(f32[2,2,16,256]{3,2,1,0:T(8,128)S(1)} %get-tuple-element.56.rest_0_), channel_id=1, source_target_pairs={{16,0},{24,8},{0,16},{8,24},{17,1},{25,9},{1,17},{9,25},{18,2},{26... | collective-permute-start | bytes 196616 | tf_op jit(solution)/shard_map/ppermute | solution.py:722
  47.3 0.8 %collective-permute-start.9 = (f32[2,2,16,256]{3,2,1,0:T(8,128)S(1)}, f32[2,2,16,256]{3,2,1,0:T(8,128)S(1)}, u32[]{:S(2)}, u32[]{:S(2)}) collective-permute-start(f32[2,2,16,256]{3,2,1,0:T(8,128)S(1)} %get-tuple-element.56.rest_0_), channel_id=1, source_target_pairs={{24,0},{0,8},{8,16},{16,24},{25,1},{1,9},{9,17},{17,25},{26,2},{2,... | collective-permute-start | bytes 196616 | tf_op jit(solution)/shard_map/ppermute | solution.py:722
  48.1 3.8 %border.1 = (bf16[4,512,256]{2,1,0:T(8,128)(2,1)S(1)}, bf16[4,512,256]{2,1,0:T(8,128)(2,1)S(1)}) custom-call(f32[4,512,256]{2,1,0:T(8,128)S(1)} %get-tuple-element.39.pre_b, f32[4,512,256]{2,1,0:T(8,128)S(1)} %get-tuple-element.40.grad_b, f32[4,512,256]{2,1,0:T(8,128)S(1)} %get-tuple-element.41.found_b, ...), custom_call_target="tpu_custom_call" | custom-call | flops 402653184 | bytes 4194304 | tf_op jit(solution)/shard_map/border/pallas_call | solution.py:864
  51.9 1.1 %collective-permute-done.9.rest_3_ = f32[2,2,16,256]{3,2,1,0:T(8,128)S(1)} collective-permute-done((f32[2,2,16,256]{3,2,1,0:T(8,128)S(1)}, f32[2,2,16,256]{3,2,1,0:T(8,128)S(1)}, u32[]{:S(2)}, u32[]{:S(2)}) %collective-permute-start.9) | collective-permute-done | bytes 65568 | tf_op jit(solution)/shard_map/ppermute | solution.py:722
  52.9 2.0 %send.1 = (bf16[4,512,128]{2,1,0:T(8,128)(2,1)S(1)}, bf16[4,512,128]{2,1,0:T(8,128)(2,1)S(1)}, f32[2,2,16,128]{3,2,1,0:T(8,128)S(1)}) custom-call(s32[4,2,3]{2,1,0:T(2,128)S(1)} %copy.15.matching_ref, bf16[4,512,256]{2,1,0:T(8,128)(2,1)S(1)} %get-tuple-element.53.inner_ref.inner_b, bf16[4,512,256]{2,1,0:T(8,128)(2,1)S(1)} %get-tuple-element.54.gp_ref.gp_b, ...), custom_call_target="tpu_custom_call" | custom-call | flops 402653184 | bytes 4194304 | tf_op jit(solution)/shard_map/send/pallas_call | solution.py:883
  54.9 1.8 %collective-permute-start.10 = (bf16[4,512,128]{2,1,0:T(8,128)(2,1)S(1)}, bf16[4,512,128]{2,1,0:T(8,128)(2,1)S(1)}, u32[]{:S(2)}, u32[]{:S(2)}) collective-permute-start(bf16[4,512,128]{2,1,0:T(8,128)(2,1)S(1)} %get-tuple-element.65), channel_id=1, source_target_pairs={{0,1},{1,0},{2,3},{3,2},{4,5},{5,4},{6,7},{7,6},{8,9},{9,8},{10,11... | collective-permute-start | bytes 1572872 | tf_op jit(solution)/shard_map/ppermute | solution.py:896
  56.7 3.4 %collective-permute-start.11 = (bf16[4,512,128]{2,1,0:T(8,128)(2,1)S(1)}, bf16[4,512,128]{2,1,0:T(8,128)(2,1)S(1)}, u32[]{:S(2)}, u32[]{:S(2)}) collective-permute-start(bf16[4,512,128]{2,1,0:T(8,128)(2,1)S(1)} %get-tuple-element.57._.own_ref), channel_id=1, source_target_pairs={{1,2},{2,1},{3,4},{4,3},{5,6},{6,5},{9,10},{10,9},{11,12},{12,11},... | collective-permute-start | bytes 1572872 | tf_op jit(solution)/shard_map/ppermute | solution.py:897
  60.1 4.2 %middle.1 = (bf16[4,512,256]{2,1,0:T(8,128)(2,1)S(1)}, bf16[4,512,256]{2,1,0:T(8,128)(2,1)S(1)}) custom-call(bf16[4,512,128]{2,1,0:T(8,128)(2,1)S(1)} %get-tuple-element.57._.own_ref, bf16[2048,256]{1,0:T(8,128)(2,1)S(1)} %get-tuple-element.58.values, f32[8,2048]{1,0:T(8,128)S(1)} %get-tuple-element.59.keys, ...), custom_call_target="tpu_custom_call" | custom-call | flops 2147483648 | bytes 10485760 | tf_op jit(solution)/shard_map/middle/pallas_call | solution.py:899
  64.3 7.5 %inside.1 = (bf16[8,512,128]{2,1,0:T(8,128)(2,1)}, f32[4,512,128]{2,1,0:T(8,128)S(1)}, f32[8,512,128]{2,1,0:T(8,128)}, f32[4,512,128]{2,1,0:T(8,128)S(1)}) custom-call(bf16[4,512,256]{2,1,0:T(8,128)(2,1)S(1)} %get-tuple-element.53.inner_ref.inner_b, bf16[4,512,256]{2,1,0:T(8,128)(2,1)S(1)} %get-tuple-element.54.gp_ref.gp_b, ...), custom_call_target="tpu_custom_call" | custom-call | flops 4831838208 | bytes 14680064 | tf_op jit(solution)/shard_map/inside/pallas_call | solution.py:914
  71.9 0.9 %collective-permute-done.11.cross_ref = bf16[4,512,128]{2,1,0:T(8,128)(2,1)S(1)} collective-permute-done((bf16[4,512,128]{2,1,0:T(8,128)(2,1)S(1)}, bf16[4,512,128]{2,1,0:T(8,128)(2,1)S(1)}, u32[]{:S(2)}, u32[]{:S(2)}) %collective-permute-start.11) | collective-permute-done | bytes 524320 | tf_op jit(solution)/shard_map/ppermute | solution.py:897
  72.7 1.2 %final.1 = (bf16[8,512,128]{2,1,0:T(8,128)(2,1)}, f32[8,512,128]{2,1,0:T(8,128)}) custom-call(f32[4,512,128]{2,1,0:T(8,128)S(1)} %get-tuple-element.63.ana_b, f32[4,512,128]{2,1,0:T(8,128)S(1)} %get-tuple-element.64.grad_b, bf16[4,512,128]{2,1,0:T(8,128)(2,1)S(1)} %get-tuple-element.57._.own_ref, ...), custom_call_target="tpu_custom_call", output_to_operand_aliasing={{0}: (5, {}), {1}: (6, {})} | custom-call | bytes 6291456 | tf_op jit(solution)/shard_map/final/pallas_call | solution.py:936
  (38 shorter events, 1.2 us)
Async XLA Ops:
  4.4 7.2 %copy-start = (bf16[1,1,2,4,512,128]{5,4,3,2,1,0:T(8,128)(2,1)S(1)}, bf16[1,1,2,4,512,128]{5,4,3,2,1,0:T(8,128)(2,1)}, u32[]{:S(2)}) copy-start(bf16[1,1,2,4,512,128]{5,4,3,2,1,0:T(8,128)(2,1)} %param.10) | copy-start | bytes 3145732
  4.5 7.2 %copy-start.2 = (bf16[1,1,2,4,512,128]{5,4,3,2,1,0:T(8,128)(2,1)S(1)}, bf16[1,1,2,4,512,128]{5,4,3,2,1,0:T(8,128)(2,1)}, u32[]{:S(2)}) copy-start(bf16[1,1,2,4,512,128]{5,4,3,2,1,0:T(8,128)(2,1)} %param.19) | copy-start | bytes 3145732
  4.5 35.4 %all-to-all-start = ((bf16[32,136,128]{2,1,0:T(8,128)(2,1)}), bf16[32,136,128]{2,1,0:T(8,128)(2,1)}, u32[]{:S(2)}, u32[]{:S(2)}) async-start(bf16[32,136,128]{2,1,0:T(8,128)(2,1)} %pack.1), calls=%async_computation | async-start | bytes 2228224 | tf_op jit(solution)/shard_map/all_to_all | solution.py:743
  11.6 4.8 %copy-start.6 = (f32[256]{0:T(256)S(1)}, f32[256]{0:T(256)}, u32[]{:S(2)}) copy-start(f32[256]{0:T(256)} %param.16) | copy-start | bytes 3076
  11.7 14.6 %collective-permute-start = (bf16[4,32,128]{2,1,0:T(8,128)(2,1)S(1)}, bf16[4,32,128]{2,1,0:T(8,128)(2,1)S(1)}, u32[]{:S(2)}, u32[]{:S(2)}) collective-permute-start(bf16[4,32,128]{2,1,0:T(8,128)(2,1)S(1)} %maximum_maximum_fusion), channel_id=1, source_target_pairs={{0,1},{1,0},{2,3},{3,2},{4,5},{5,4},{6,7},{7,6},{8,9},{9,8},{10,11... | collective-permute-start | bytes 98312 | tf_op jit(solution)/shard_map/ppermute | solution.py:706
  12.1 14.2 %collective-permute-start.1 = (bf16[4,32,128]{2,1,0:T(8,128)(2,1)S(1)}, bf16[4,32,128]{2,1,0:T(8,128)(2,1)S(1)}, u32[]{:S(2)}, u32[]{:S(2)}) collective-permute-start(bf16[4,32,128]{2,1,0:T(8,128)(2,1)S(1)} %maximum_maximum_fusion.1), channel_id=1, source_target_pairs={{1,2},{2,1},{3,4},{4,3},{5,6},{6,5},{9,10},{10,9},{11,12},{12,11},... | collective-permute-start | bytes 98312 | tf_op jit(solution)/shard_map/ppermute | solution.py:707
  16.4 13.3 %copy-start.8 = (s32[4,2,3]{0,1,2:T(2,128)S(1)}, s32[4,2,3]{0,1,2:T(2,128)}, u32[]{:S(2)}) copy-start(s32[4,2,3]{0,1,2:T(2,128)} %param.14) | copy-start | bytes 292
  16.4 13.5 %copy-start.1 = (bf16[1,1,2,4,512,128]{5,4,3,2,1,0:T(8,128)(2,1)S(1)}, bf16[1,1,2,4,512,128]{5,4,3,2,1,0:T(8,128)(2,1)}, u32[]{:S(2)}) copy-start(bf16[1,1,2,4,512,128]{5,4,3,2,1,0:T(8,128)(2,1)} %param.10) | copy-start | bytes 3145732
  16.4 13.5 %copy-start.3 = (bf16[1,1,2,4,512,128]{5,4,3,2,1,0:T(8,128)(2,1)S(1)}, bf16[1,1,2,4,512,128]{5,4,3,2,1,0:T(8,128)(2,1)}, u32[]{:S(2)}) copy-start(bf16[1,1,2,4,512,128]{5,4,3,2,1,0:T(8,128)(2,1)} %param.19) | copy-start | bytes 3145732
  26.3 21.8 %collective-permute-start.5 = (bf16[4,512,128]{2,1,0:T(8,128)(2,1)}, bf16[4,512,128]{2,1,0:T(8,128)(2,1)}, u32[]{:S(2)}, u32[]{:S(2)}) collective-permute-start(bf16[4,512,128]{2,1,0:T(8,128)(2,1)} %pad_maximum_fusion), channel_id=1, source_target_pairs={{0,1},{1,0},{2,3},{3,2},{4,5},{5,4},{6,7},{7,6},{8,9},{9,8},{10,11... | collective-permute-start | bytes 1572872 | tf_op jit(solution)/shard_map/ppermute | solution.py:774
  26.3 21.8 %collective-permute-start.6 = (bf16[4,512,128]{2,1,0:T(8,128)(2,1)}, bf16[4,512,128]{2,1,0:T(8,128)(2,1)}, u32[]{:S(2)}, u32[]{:S(2)}) collective-permute-start(bf16[4,512,128]{2,1,0:T(8,128)(2,1)} %pad_maximum_fusion.1), channel_id=1, source_target_pairs={{1,2},{2,1},{3,4},{4,3},{5,6},{6,5},{9,10},{10,9},{11,12},{12,11},... | collective-permute-start | bytes 1572872 | tf_op jit(solution)/shard_map/ppermute | solution.py:775
  29.9 13.9 %collective-permute-start.2 = (f32[2,2,16,128]{3,2,1,0:T(8,128)S(1)}, f32[2,2,16,128]{3,2,1,0:T(8,128)S(1)}, u32[]{:S(2)}, u32[]{:S(2)}) collective-permute-start(f32[2,2,16,128]{3,2,1,0:T(8,128)S(1)} %edges.1.rest_0_), channel_id=1, source_target_pairs={{8,0},{16,8},{24,16},{0,24},{9,1},{17,9},{25,17},{1,25},{10,2},{18... | collective-permute-start | bytes 98312 | tf_op jit(solution)/shard_map/ppermute | solution.py:722
  33.0 10.8 %collective-permute-start.3 = (f32[2,2,16,128]{3,2,1,0:T(8,128)S(1)}, f32[2,2,16,128]{3,2,1,0:T(8,128)S(1)}, u32[]{:S(2)}, u32[]{:S(2)}) collective-permute-start(f32[2,2,16,128]{3,2,1,0:T(8,128)S(1)} %edges.1.rest_0_), channel_id=1, source_target_pairs={{16,0},{24,8},{0,16},{8,24},{17,1},{25,9},{1,17},{9,25},{18,2},{26... | collective-permute-start | bytes 98312 | tf_op jit(solution)/shard_map/ppermute | solution.py:722
  33.0 10.8 %collective-permute-start.4 = (f32[2,2,16,128]{3,2,1,0:T(8,128)S(1)}, f32[2,2,16,128]{3,2,1,0:T(8,128)S(1)}, u32[]{:S(2)}, u32[]{:S(2)}) collective-permute-start(f32[2,2,16,128]{3,2,1,0:T(8,128)S(1)} %edges.1.rest_0_), channel_id=1, source_target_pairs={{24,0},{0,8},{8,16},{16,24},{25,1},{1,9},{9,17},{17,25},{26,2},{2,... | collective-permute-start | bytes 98312 | tf_op jit(solution)/shard_map/ppermute | solution.py:722
  44.7 7.2 %collective-permute-start.7 = (f32[2,2,16,256]{3,2,1,0:T(8,128)S(1)}, f32[2,2,16,256]{3,2,1,0:T(8,128)S(1)}, u32[]{:S(2)}, u32[]{:S(2)}) collective-permute-start(f32[2,2,16,256]{3,2,1,0:T(8,128)S(1)} %get-tuple-element.56.rest_0_), channel_id=1, source_target_pairs={{8,0},{16,8},{24,16},{0,24},{9,1},{17,9},{25,17},{1,25},{10,2},{18... | collective-permute-start | bytes 196616 | tf_op jit(solution)/shard_map/ppermute | solution.py:722
  46.4 5.5 %collective-permute-start.8 = (f32[2,2,16,256]{3,2,1,0:T(8,128)S(1)}, f32[2,2,16,256]{3,2,1,0:T(8,128)S(1)}, u32[]{:S(2)}, u32[]{:S(2)}) collective-permute-start(f32[2,2,16,256]{3,2,1,0:T(8,128)S(1)} %get-tuple-element.56.rest_0_), channel_id=1, source_target_pairs={{16,0},{24,8},{0,16},{8,24},{17,1},{25,9},{1,17},{9,25},{18,2},{26... | collective-permute-start | bytes 196616 | tf_op jit(solution)/shard_map/ppermute | solution.py:722
  47.3 5.6 %collective-permute-start.9 = (f32[2,2,16,256]{3,2,1,0:T(8,128)S(1)}, f32[2,2,16,256]{3,2,1,0:T(8,128)S(1)}, u32[]{:S(2)}, u32[]{:S(2)}) collective-permute-start(f32[2,2,16,256]{3,2,1,0:T(8,128)S(1)} %get-tuple-element.56.rest_0_), channel_id=1, source_target_pairs={{24,0},{0,8},{8,16},{16,24},{25,1},{1,9},{9,17},{17,25},{26,2},{2,... | collective-permute-start | bytes 196616 | tf_op jit(solution)/shard_map/ppermute | solution.py:722
  48.1 4.9 %copy-start.4 = (bf16[9,256,128]{2,1,0:T(8,128)(2,1)S(1)}, bf16[9,256,128]{2,1,0:T(8,128)(2,1)}, u32[]{:S(2)}) copy-start(bf16[9,256,128]{2,1,0:T(8,128)(2,1)} %k2_ref.3) | copy-start | bytes 1769476
  48.1 4.9 %copy-start.5 = (bf16[9,256,128]{2,1,0:T(8,128)(2,1)S(1)}, bf16[9,256,128]{2,1,0:T(8,128)(2,1)}, u32[]{:S(2)}) copy-start(bf16[9,256,128]{2,1,0:T(8,128)(2,1)} %get-tuple-element.55.k1t_ref) | copy-start | bytes 1769476
  54.9 16.9 %collective-permute-start.10 = (bf16[4,512,128]{2,1,0:T(8,128)(2,1)S(1)}, bf16[4,512,128]{2,1,0:T(8,128)(2,1)S(1)}, u32[]{:S(2)}, u32[]{:S(2)}) collective-permute-start(bf16[4,512,128]{2,1,0:T(8,128)(2,1)S(1)} %get-tuple-element.65), channel_id=1, source_target_pairs={{0,1},{1,0},{2,3},{3,2},{4,5},{5,4},{6,7},{7,6},{8,9},{9,8},{10,11... | collective-permute-start | bytes 1572872 | tf_op jit(solution)/shard_map/ppermute | solution.py:896
  56.7 16.0 %collective-permute-start.11 = (bf16[4,512,128]{2,1,0:T(8,128)(2,1)S(1)}, bf16[4,512,128]{2,1,0:T(8,128)(2,1)S(1)}, u32[]{:S(2)}, u32[]{:S(2)}) collective-permute-start(bf16[4,512,128]{2,1,0:T(8,128)(2,1)S(1)} %get-tuple-element.57._.own_ref), channel_id=1, source_target_pairs={{1,2},{2,1},{3,4},{4,3},{5,6},{6,5},{9,10},{10,9},{11,12},{12,11},... | collective-permute-start | bytes 1572872 | tf_op jit(solution)/shard_map/ppermute | solution.py:897
  60.1 4.2 %copy-start.7 = (f32[128]{0:T(128)S(1)}, f32[128]{0:T(128)}, u32[]{:S(2)}) copy-start(f32[128]{0:T(128)} %param.18) | copy-start | bytes 1540

commit v4 on v3

--- a/solution.py
+++ b/solution.py
@@ -514,33 +514,37 @@
             gp_ref[j] = gp
 
 
-def send_body(rows, faces, matching_ref, inner_ref, gp_ref, k2_ref, k1t_ref, *rest):
+def send_rows(rows, inner_ref, gp_ref, k2_ref, k1t_ref, side_ref, out_ref, bottom):
+    width = inner_ref.shape[1]
+    for array, (source, taps) in enumerate(((inner_ref, k2_ref), (gp_ref, k1t_ref))):
+        for band in range(2):
+            tap = jnp.where((bottom == band) == (array == 0), 2, 0)
+            wide = dot(source[2 * band + bottom], row_taps(taps, tap))
+            corner = GROUP * band + (rows + 1) * bottom
+            part = add_edges(
+                merge_shifts(wide, array == 0),
+                side_ref[array, 0, pl.ds(corner, 1), :],
+                side_ref[array, 1, pl.ds(corner, 1), :],
+            )
+            out_ref[2 * array + band] = part.astype(BF16)
+
+
+def cross_body(rows, faces, matching_ref, inner_ref, gp_ref, k2_ref, k1t_ref, *rest):
     parts = rest[:faces]
-    pair_ref, cross_ref, side_ref = rest[faces:]
-    even = is_even()
-    width = inner_ref.shape[1]
+    cross_ref, side_ref = rest[faces:]
     for side in range(2):
         hop, their_side, flipped = matched(matching_ref, side, faces)
         near = partner_rows(parts, 0, hop, their_side, flipped)
         side_ref[0, side] = side_forward(near, side, k2_ref)
         near = partner_rows(parts, 1, hop, their_side, flipped)
         side_ref[1, side] = side_adjoint(near, their_side, flipped, k1t_ref)
-    up = jnp.where(even, 1, 0)
-    for array, (source, taps) in enumerate(((inner_ref, k2_ref), (gp_ref, k1t_ref))):
-        for group in range(2):
-            members = ((pair_ref, group, up), (cross_ref, 1 - group, 1 - up))
-            tap = jnp.where((group == up) == (array == 0), 2, 0)
-            lhs = jnp.concatenate([source[2 * band + bottom] for _, band, bottom in members], axis=0)
-            wide = dot(lhs, row_taps(taps, tap))
-            for k, (target, band, bottom) in enumerate(members):
-                part = merge_shifts(wide[k * width : (k + 1) * width], array == 0)
-                corner = GROUP * band + (rows + 1) * bottom
-                part = add_edges(
-                    part,
-                    side_ref[array, 0, pl.ds(corner, 1), :],
-                    side_ref[array, 1, pl.ds(corner, 1), :],
-                )
-                target[2 * array + band] = part.astype(BF16)
+    bottom = jnp.where(is_even(), 0, 1)
+    send_rows(rows, inner_ref, gp_ref, k2_ref, k1t_ref, side_ref, cross_ref, bottom)
+
+
+def pair_body(rows, _, inner_ref, gp_ref, k2_ref, k1t_ref, side_ref, pair_ref):
+    bottom = jnp.where(is_even(), 1, 0)
+    send_rows(rows, inner_ref, gp_ref, k2_ref, k1t_ref, side_ref, pair_ref, bottom)
 
 
 def middle_body(
@@ -577,17 +581,11 @@
 
 
 def inside_body(
-    rows, inner_b, gp_b, inner_m, gp_m, side_ref, k2_ref, k1t_ref, b2_ref, x_in, c_in, ana_out, ana_b,
-    grad_out, grad_b, own_rows, ana_rows, grad_rows, sem,
+    rows, inner_b, gp_b, inner_m, gp_m, side_ref, k2_ref, k1t_ref, b2_ref, x_ref, c_ref, ana_out, ana_b,
+    grad_out, grad_b, ana_rows, grad_rows, sem,
 ):
-    width, channels = own_rows.shape[2], own_rows.shape[3]
+    width, channels = x_ref.shape[1], x_ref.shape[2]
     middle = rows - 2
-    loads = [
-        pltpu.make_async_copy(x_in, own_rows.at[0], sem.at[0]),
-        pltpu.make_async_copy(c_in, own_rows.at[1], sem.at[1]),
-    ]
-    for load in loads:
-        load.start()
     stores = []
     for array, (border, inner, taps) in enumerate(
         ((inner_b, inner_m, k2_ref), (gp_b, gp_m, k1t_ref))
@@ -610,14 +608,12 @@
                 axis=0,
             )
             wide = dot(lhs, jnp.concatenate([row_taps(taps, dy + 1) for dy in steps], axis=0))
-            if len(steps) == 3:
-                loads[array].wait()
             for k, (b, r) in enumerate(members):
                 i = b * rows + r
                 at = b * GROUP + r + 1
                 total = merge_shifts(wide[k * width : (k + 1) * width], array == 0)
                 total = add_edges(
-                    total + own_rows[array, i].astype(F32),
+                    total + (x_ref, c_ref)[array][i].astype(F32),
                     side_ref[array, 0, at : at + 1, :],
                     side_ref[array, 1, at : at + 1, :],
                 )
@@ -628,7 +624,7 @@
                     continue
                 held_rows, out = ((ana_rows, ana_out), (grad_rows, grad_out))[array]
                 held_rows[k] = total.astype(held_rows.dtype)
-                store = pltpu.make_async_copy(held_rows.at[k], out.at[i], sem.at[2 + len(stores)])
+                store = pltpu.make_async_copy(held_rows.at[k], out.at[i], sem.at[len(stores)])
                 store.start()
                 stores.append(store)
     for store in stores:
@@ -880,21 +876,26 @@
     inner_b, gp_b = held(inner_b), held(gp_b)
 
     side_out = (2, 2, 2 * GROUP, channels)
-    to_pair, to_cross, sides = pl.pallas_call(
-        functools.partial(send_body, rows, faces),
+    to_cross, sides = pl.pallas_call(
+        functools.partial(cross_body, rows, faces),
         in_specs=[smem] + [vmem] * (4 + faces),
-        out_specs=[vmem] * 3,
-        out_shape=[
-            jax.ShapeDtypeStruct(plane, BF16),
-            jax.ShapeDtypeStruct(plane, BF16),
-            jax.ShapeDtypeStruct(side_out, F32),
-        ],
+        out_specs=[vmem] * 2,
+        out_shape=[jax.ShapeDtypeStruct(plane, BF16), jax.ShapeDtypeStruct(side_out, F32)],
         compiler_params=params(16),
-        cost_estimate=cost(conv_flops // 6, 4 << 20),
-        name="send",
+        cost_estimate=cost(conv_flops // 12, 3 << 20),
+        name="send_cross",
     )(matching, inner_b, gp_b, kernel_two, k1t, *parts_two)
+    from_cross = lax.ppermute(to_cross, "tile", crosses)
+    to_pair = pl.pallas_call(
+        functools.partial(pair_body, rows),
+        in_specs=[hbm] + [vmem] * 5,
+        out_specs=vmem,
+        out_shape=jax.ShapeDtypeStruct(plane, BF16),
+        compiler_params=params(16),
+        cost_estimate=cost(conv_flops // 12, 3 << 20),
+        name="send_pair",
+    )(to_cross, inner_b, gp_b, kernel_two, k1t, sides)
     from_pair = lax.ppermute(to_pair, "tile", pairs)
-    from_cross = lax.ppermute(to_cross, "tile", crosses)
 
     inner_m, gp_m = pl.pallas_call(
         functools.partial(middle_body, rows),
@@ -908,12 +909,12 @@
         compiler_params=params(32),
         cost_estimate=cost(2 * middle * onehot_flops, 10 << 20),
         name="middle",
-    )(to_cross, values, keys, pre, grad_inner, x_side, c_side)
+    )(to_pair, values, keys, pre, grad_inner, x_side, c_side)
     inner_m, gp_m = held(inner_m), held(gp_m)
 
     analysis, ana_b, grad_state, grad_b = pl.pallas_call(
         functools.partial(inside_body, rows),
-        in_specs=[vmem] * 8 + [hbm] * 2,
+        in_specs=[vmem] * 10,
         out_specs=[hbm, vmem, hbm, vmem],
         out_shape=[
             pltpu.HBM((all_rows, width, channels), BF16),
@@ -922,15 +923,14 @@
             hold(plane, F32),
         ],
         scratch_shapes=[
-            pltpu.VMEM((2, all_rows, width, channels), BF16),
             pltpu.VMEM((2 * middle, width, channels), BF16),
             pltpu.VMEM((2 * middle, width, channels), F32),
-            pltpu.SemaphoreType.DMA((2 + 4 * middle,)),
+            pltpu.SemaphoreType.DMA((4 * middle,)),
         ],
         compiler_params=params(),
         cost_estimate=cost(2 * conv_flops, 14 << 20),
         name="inside",
-    )(inner_b, gp_b, inner_m, gp_m, sides, kernel_two, k1t, b2, far(x), far(c))
+    )(inner_b, gp_b, inner_m, gp_m, sides, kernel_two, k1t, b2, x, c)
     ana_b, grad_b = held(ana_b), held(grad_b)
 
     analysis, grad_state = pl.pallas_call(

time: 74.5 us -> 73.4 us (0.985)
  Pallas kernels: 38.8 us -> 37.2 us
    ppermute x1, starting transfers between devices: 1.75 us -> 0.07 us  [per_device(): from_pair = lax.ppermute(to_pair, 'tile', pairs)]
    ppermute x1, starting transfers between devices: 3.4 us -> 5.07 us  [per_device(): from_cross = lax.ppermute(to_cross, 'tile', crosses)]
    pallas_call x2 -> x3, Pallas kernels: 9.5 us -> 7.87 us  [the longest x1 5.71 us: per_device(): pl.pallas_call(functools.partial(inside_body, rows), in_specs=[vmem] * 10...]
  transfers between devices with their start and end apart: 13 -> 13, of which waited for: 3 -> 3; matrix products, arithmetic and copies ran while one was open for 3% -> 3% of each run, Pallas kernels for 43% -> 42%
where the time goes in v4:
time: 73.4 us; the launch traced here: 73.1 us
  Pallas kernels  37.2 us (51%)
  starting transfers between devices  26.5 us (36%)
  waiting for transfers between devices  6.23 us (8%)
  other arithmetic  1.7 us (2%)
  between operations  1.12 us (2%)
    pallas_call x1, Pallas kernels, per_device(): pl.pallas_call(functools.partial(lift_body, rows), in_specs=[hbm] * 4 + [...  9.01 us
    all_to_all x1, starting transfers between devices, per_device(): received = lax.all_to_all(packed, ('face', 'tile'), 0, 0, tiled=True)  7.15 us
    ppermute x6, starting transfers between devices, exchange(): lax.ppermute(own, 'face', [((i + k) % faces, i) for i in range(faces)])  7 us
    pallas_call x1, Pallas kernels, per_device(): pl.pallas_call(functools.partial(inside_body, rows), in_specs=[vmem] * 10...  5.71 us
    ppermute x1, starting transfers between devices, per_device(): from_cross = lax.ppermute(to_cross, 'tile', crosses)  5.07 us
    pallas_call x1, Pallas kernels, per_device(): pl.pallas_call(functools.partial(middle_body, rows), in_specs=[hbm, vmem,...  4.2 us
    pallas_call x1, Pallas kernels, per_device(): pl.pallas_call(functools.partial(found_body, rows, capacity), in_specs=[h...  3.96 us
    pallas_call x1, Pallas kernels, per_device(): pl.pallas_call(functools.partial(pack_body, capacity), in_specs=[hbm] * 3...  3.81 us
  transfers between devices with their start and end apart: 13, of which 3 were waited for; matrix products, arithmetic and copies ran while one was open for 3% of the time, Pallas kernels for 42%

profile of v4, /device:TPU:1, one launch (start us, length us, event | category | flops | bytes accessed | tf_op | source)
XLA Modules:
  0.0 73.1 jit_solution(6151515621155104534)
XLA Ops:
  0.6 3.8 %pack.1 = bf16[32,136,128]{2,1,0:T(8,128)(2,1)} custom-call(s32[1,1024]{1,0:T(1,128)} %bitcast.50, s32[1,1024]{1,0:T(1,128)} %bitcast.51, bf16[1024,256]{1,0:T(8,128)(2,1)} %values_in.1), custom_call_target="tpu_custom_call" | custom-call | flops 1073741824 | bytes 2097152 | tf_op jit(solution)/shard_map/pack/pallas_call | solution.py:722
  4.5 7.2 %all-to-all-start = ((bf16[32,136,128]{2,1,0:T(8,128)(2,1)}), bf16[32,136,128]{2,1,0:T(8,128)(2,1)}, u32[]{:S(2)}, u32[]{:S(2)}) async-start(bf16[32,136,128]{2,1,0:T(8,128)(2,1)} %pack.1), calls=%async_computation | async-start | bytes 2228224 | tf_op jit(solution)/shard_map/all_to_all | solution.py:739
  12.1 3.4 %collective-permute-start.1 = (bf16[4,32,128]{2,1,0:T(8,128)(2,1)S(1)}, bf16[4,32,128]{2,1,0:T(8,128)(2,1)S(1)}, u32[]{:S(2)}, u32[]{:S(2)}) collective-permute-start(bf16[4,32,128]{2,1,0:T(8,128)(2,1)S(1)} %maximum_maximum_fusion.1), channel_id=1, source_target_pairs={{1,2},{2,1},{3,4},{4,3},{5,6},{6,5},{9,10},{10,9},{11,12},{12,11},... | collective-permute-start | bytes 98312 | tf_op jit(solution)/shard_map/ppermute | solution.py:703
  15.6 0.9 %pad_maximum_fusion = bf16[4,512,128]{2,1,0:T(8,128)(2,1)} fusion(bf16[2,512,128]{2,1,0:T(8,128)(2,1)S(1)} %get-tuple-element.79, bf16[2,512,128]{2,1,0:T(8,128)(2,1)S(1)} %get-tuple-element.80), kind=kLoop, calls=%fused_computation | loop fusion | flops 262144 | bytes 1048576 | tf_op jit(solution)/shard_map/concatenate | solution.py:707
  16.4 9.0 %lift.1 = (f32[8,512,256]{2,1,0:T(8,128)}, f32[8,512,256]{2,1,0:T(8,128)}, bf16[9,256,128]{2,1,0:T(8,128)(2,1)}, bf16[9,128,256]{2,1,0:T(8,128)(2,1)}) custom-call(bf16[8,512,128]{2,1,0:T(8,128)(2,1)} %bitcast.32, bf16[8,512,128]{2,1,0:T(8,128)(2,1)} %bitcast.39, bf16[9,128,256]{2,1,0:T(8,128)(2,1)} %k1_in.5, bf16[9,256,128]{2,1,0:T(8,128)(2,1)} %k2_ref.5, ...), custom_call_target="tpu_custom_call" | custom-call | flops 2415919104 | bytes 8388608 | tf_op jit(solution)/shard_map/lift/pallas_call | solution.py:747
  25.4 0.8 %pad_maximum_fusion.1 = bf16[4,512,128]{2,1,0:T(8,128)(2,1)} fusion(bf16[2,512,128]{2,1,0:T(8,128)(2,1)S(1)} %get-tuple-element.78, bf16[2,512,128]{2,1,0:T(8,128)(2,1)S(1)} %get-tuple-element.81), kind=kLoop, calls=%fused_computation.1 | loop fusion | flops 262144 | bytes 1048576 | tf_op jit(solution)/shard_map/concatenate | solution.py:707
  26.3 3.5 %collective-permute-start.6 = (bf16[4,512,128]{2,1,0:T(8,128)(2,1)}, bf16[4,512,128]{2,1,0:T(8,128)(2,1)}, u32[]{:S(2)}, u32[]{:S(2)}) collective-permute-start(bf16[4,512,128]{2,1,0:T(8,128)(2,1)} %pad_maximum_fusion.1), channel_id=1, source_target_pairs={{1,2},{2,1},{3,4},{4,3},{5,6},{6,5},{9,10},{10,9},{11,12},{12,11},... | collective-permute-start | bytes 1572872 | tf_op jit(solution)/shard_map/ppermute | solution.py:771
  29.9 3.1 %collective-permute-start.2 = (f32[2,2,16,128]{3,2,1,0:T(8,128)S(1)}, f32[2,2,16,128]{3,2,1,0:T(8,128)S(1)}, u32[]{:S(2)}, u32[]{:S(2)}) collective-permute-start(f32[2,2,16,128]{3,2,1,0:T(8,128)S(1)} %edges.1.rest_0_), channel_id=1, source_target_pairs={{8,0},{16,8},{24,16},{0,24},{9,1},{17,9},{25,17},{1,25},{10,2},{18... | collective-permute-start | bytes 98312 | tf_op jit(solution)/shard_map/ppermute | solution.py:718
  33.5 2.5 %rim_in.1 = (f32[2,32,256]{2,1,0:T(8,128)S(1)}, bf16[2,2,3,128,256]{4,3,2,1,0:T(8,128)(2,1)S(1)}) custom-call(s32[4,2,3]{2,1,0:T(2,128)S(1)} %copy.15.matching_ref, bf16[9,128,256]{2,1,0:T(8,128)(2,1)} %k1_in.5, bf16[9,128,256]{2,1,0:T(8,128)(2,1)} %get-tuple-element.37.k2t_in, f32[8,512,256]{2,1,0:T(8,128)} %get-tuple-element.35.pre_in.pre_lo.pre_hi, ...), custom_call_target="tpu_custom_call" | custom-call | bytes 2097152 | tf_op jit(solution)/shard_map/rim_in/pallas_call | solution.py:793
  36.1 3.8 %all-to-all-done.recv_in = bf16[32,136,128]{2,1,0:T(8,128)(2,1)} async-done(((bf16[32,136,128]{2,1,0:T(8,128)(2,1)}), bf16[32,136,128]{2,1,0:T(8,128)(2,1)}, u32[]{:S(2)}, u32[]{:S(2)}) %all-to-all-start) | async-done | bytes 1114144 | tf_op jit(solution)/shard_map/all_to_all | solution.py:739
  39.8 4.0 %found.1 = (bf16[2048,256]{1,0:T(8,128)(2,1)S(1)}, f32[8,2048]{1,0:T(8,128)S(1)}, f32[4,512,256]{2,1,0:T(8,128)S(1)}, f32[4,512,256]{2,1,0:T(8,128)S(1)}, f32[4,...) custom-call(bf16[32,136,128]{2,1,0:T(8,128)(2,1)} %all-to-all-done.recv_in, ...), custom_call_target="tpu_custom_call" | custom-call | flops 2147483648 | bytes 6291456 | tf_op jit(solution)/shard_map/found/pallas_call | solution.py:820
  43.8 0.8 %rim.1 = (f32[2,16,256]{2,1,0:T(8,128)S(1)}, f32[2,16,256]{2,1,0:T(8,128)S(1)}, f32[2,2,16,256]{3,2,1,0:T(8,128)S(1)}) custom-call(s32[4,2,3]{2,1,0:T(2,128)S(1)} %copy.15.matching_ref, bf16[2,2,3,128,256]{4,3,2,1,0:T(8,128)(2,1)S(1)} %get-tuple-element.45.taps_ref, f32[2,32,256]{2,1,0:T(8,128)S(1)} %get-tuple-element.46.base_ref, ...), custom_call_target="tpu_custom_call" | custom-call | bytes 1048576 | tf_op jit(solution)/shard_map/rim/pallas_call | solution.py:843
  44.7 1.7 %collective-permute-start.7 = (f32[2,2,16,256]{3,2,1,0:T(8,128)S(1)}, f32[2,2,16,256]{3,2,1,0:T(8,128)S(1)}, u32[]{:S(2)}, u32[]{:S(2)}) collective-permute-start(f32[2,2,16,256]{3,2,1,0:T(8,128)S(1)} %get-tuple-element.55.rest_0_), channel_id=1, source_target_pairs={{8,0},{16,8},{24,16},{0,24},{9,1},{17,9},{25,17},{1,25},{10,2},{18... | collective-permute-start | bytes 196616 | tf_op jit(solution)/shard_map/ppermute | solution.py:718
  46.4 0.9 %collective-permute-start.8 = (f32[2,2,16,256]{3,2,1,0:T(8,128)S(1)}, f32[2,2,16,256]{3,2,1,0:T(8,128)S(1)}, u32[]{:S(2)}, u32[]{:S(2)}) collective-permute-start(f32[2,2,16,256]{3,2,1,0:T(8,128)S(1)} %get-tuple-element.55.rest_0_), channel_id=1, source_target_pairs={{16,0},{24,8},{0,16},{8,24},{17,1},{25,9},{1,17},{9,25},{18,2},{26... | collective-permute-start | bytes 196616 | tf_op jit(solution)/shard_map/ppermute | solution.py:718
  47.3 0.8 %collective-permute-start.9 = (f32[2,2,16,256]{3,2,1,0:T(8,128)S(1)}, f32[2,2,16,256]{3,2,1,0:T(8,128)S(1)}, u32[]{:S(2)}, u32[]{:S(2)}) collective-permute-start(f32[2,2,16,256]{3,2,1,0:T(8,128)S(1)} %get-tuple-element.55.rest_0_), channel_id=1, source_target_pairs={{24,0},{0,8},{8,16},{16,24},{25,1},{1,9},{9,17},{17,25},{26,2},{2,... | collective-permute-start | bytes 196616 | tf_op jit(solution)/shard_map/ppermute | solution.py:718
  48.1 3.8 %border.1 = (bf16[4,512,256]{2,1,0:T(8,128)(2,1)S(1)}, bf16[4,512,256]{2,1,0:T(8,128)(2,1)S(1)}) custom-call(f32[4,512,256]{2,1,0:T(8,128)S(1)} %get-tuple-element.38.pre_b, f32[4,512,256]{2,1,0:T(8,128)S(1)} %get-tuple-element.39.grad_b, f32[4,512,256]{2,1,0:T(8,128)S(1)} %get-tuple-element.40.found_b, ...), custom_call_target="tpu_custom_call" | custom-call | flops 402653184 | bytes 4194304 | tf_op jit(solution)/shard_map/border/pallas_call | solution.py:860
  51.9 1.1 %collective-permute-done.9.rest_3_ = f32[2,2,16,256]{3,2,1,0:T(8,128)S(1)} collective-permute-done((f32[2,2,16,256]{3,2,1,0:T(8,128)S(1)}, f32[2,2,16,256]{3,2,1,0:T(8,128)S(1)}, u32[]{:S(2)}, u32[]{:S(2)}) %collective-permute-start.9) | collective-permute-done | bytes 65568 | tf_op jit(solution)/shard_map/ppermute | solution.py:718
  52.9 1.4 %send_cross.1 = (bf16[4,512,128]{2,1,0:T(8,128)(2,1)S(1)}, f32[2,2,16,128]{3,2,1,0:T(8,128)S(1)}) custom-call(s32[4,2,3]{2,1,0:T(2,128)S(1)} %copy.15.matching_ref, bf16[4,512,256]{2,1,0:T(8,128)(2,1)S(1)} %get-tuple-element.52.inner_ref.inner_b, bf16[4,512,256]{2,1,0:T(8,128)(2,1)S(1)} %get-tuple-element.53.gp_ref.gp_b, bf16[9,256,128]{2,1,0:T(8,128)(2,1)S(1)} %copy-done.6, ...), custom_call_target="tpu_custom_call" | custom-call | flops 201326592 | bytes 3145728 | tf_op jit(solution)/shard_map/send_cross/pallas_call | solution.py:879
  54.4 5.1 %collective-permute-start.11 = (bf16[4,512,128]{2,1,0:T(8,128)(2,1)S(1)}, bf16[4,512,128]{2,1,0:T(8,128)(2,1)S(1)}, u32[]{:S(2)}, u32[]{:S(2)}) collective-permute-start(bf16[4,512,128]{2,1,0:T(8,128)(2,1)S(1)} %get-tuple-element.56._.own_ref), channel_id=1, source_target_pairs={{1,2},{2,1},{3,4},{4,3},{5,6},{6,5},{9,10},{10,9},{11,12},{12,11},... | collective-permute-start | bytes 1572872 | tf_op jit(solution)/shard_map/ppermute | solution.py:888
  59.5 0.7 %send_pair.1._ = bf16[4,512,128]{2,1,0:T(8,128)(2,1)S(1)} custom-call(bf16[4,512,128]{2,1,0:T(8,128)(2,1)S(1)} %get-tuple-element.56._.own_ref, bf16[4,512,256]{2,1,0:T(8,128)(2,1)S(1)} %get-tuple-element.52.inner_ref.inner_b, bf16[4,512,256]{2,1,0:T(8,128)(2,1)S(1)} %get-tuple-element.53.gp_ref.gp_b, bf16[9,256,128]{2,1,0:T(8,128)(2,1)S(1)} %copy-done.6, ...), custom_call_target="tpu_custom_call" | custom-call | flops 201326592 | bytes 3145728 | tf_op jit(solution)/shard_map/send_pair/pallas_call | solution.py:889
  60.3 4.2 %middle.1 = (bf16[4,512,256]{2,1,0:T(8,128)(2,1)S(1)}, bf16[4,512,256]{2,1,0:T(8,128)(2,1)S(1)}) custom-call(bf16[4,512,128]{2,1,0:T(8,128)(2,1)S(1)} %send_pair.1._, bf16[2048,256]{1,0:T(8,128)(2,1)S(1)} %get-tuple-element.58.values, f32[8,2048]{1,0:T(8,128)S(1)} %get-tuple-element.59.keys, f32[8,512,256]{2,1,0:T(8,128)} %get-tuple-element.35.pre_in.pre_lo.pre_hi, ...), custom_call_target="tpu_custom_call" | custom-call | flops 2147483648 | bytes 10485760 | tf_op jit(solution)/shard_map/middle/pallas_call | solution.py:900
  64.6 5.7 %inside.1 = (bf16[8,512,128]{2,1,0:T(8,128)(2,1)}, f32[4,512,128]{2,1,0:T(8,128)S(1)}, f32[8,512,128]{2,1,0:T(8,128)}, f32[4,512,128]{2,1,0:T(8,128)S(1)}) custom-call(bf16[4,512,256]{2,1,0:T(8,128)(2,1)S(1)} %get-tuple-element.52.inner_ref.inner_b, bf16[4,512,256]{2,1,0:T(8,128)(2,1)S(1)} %get-tuple-element.53.gp_ref.gp_b, ...), custom_call_target="tpu_custom_call" | custom-call | flops 4831838208 | bytes 14680064 | tf_op jit(solution)/shard_map/inside/pallas_call | solution.py:915
  70.3 1.4 %collective-permute-done.11.cross_ref = bf16[4,512,128]{2,1,0:T(8,128)(2,1)S(1)} collective-permute-done((bf16[4,512,128]{2,1,0:T(8,128)(2,1)S(1)}, bf16[4,512,128]{2,1,0:T(8,128)(2,1)S(1)}, u32[]{:S(2)}, u32[]{:S(2)}) %collective-permute-start.11) | collective-permute-done | bytes 524320 | tf_op jit(solution)/shard_map/ppermute | solution.py:888
  71.6 1.2 %final.1 = (bf16[8,512,128]{2,1,0:T(8,128)(2,1)}, f32[8,512,128]{2,1,0:T(8,128)}) custom-call(f32[4,512,128]{2,1,0:T(8,128)S(1)} %get-tuple-element.62.ana_b, f32[4,512,128]{2,1,0:T(8,128)S(1)} %get-tuple-element.63.grad_b, bf16[4,512,128]{2,1,0:T(8,128)(2,1)S(1)} %get-tuple-element.56._.own_ref, ...), custom_call_target="tpu_custom_call", output_to_operand_aliasing={{0}: (5, {}), {1}: (6, {})} | custom-call | bytes 6291456 | tf_op jit(solution)/shard_map/final/pallas_call | solution.py:936
  (43 shorter events, 1.3 us)
Async XLA Ops:
  4.4 7.2 %copy-start = (bf16[1,1,2,4,512,128]{5,4,3,2,1,0:T(8,128)(2,1)S(1)}, bf16[1,1,2,4,512,128]{5,4,3,2,1,0:T(8,128)(2,1)}, u32[]{:S(2)}) copy-start(bf16[1,1,2,4,512,128]{5,4,3,2,1,0:T(8,128)(2,1)} %param.10) | copy-start | bytes 3145732
  4.5 7.2 %copy-start.3 = (bf16[1,1,2,4,512,128]{5,4,3,2,1,0:T(8,128)(2,1)S(1)}, bf16[1,1,2,4,512,128]{5,4,3,2,1,0:T(8,128)(2,1)}, u32[]{:S(2)}) copy-start(bf16[1,1,2,4,512,128]{5,4,3,2,1,0:T(8,128)(2,1)} %param.19) | copy-start | bytes 3145732
  4.5 35.4 %all-to-all-start = ((bf16[32,136,128]{2,1,0:T(8,128)(2,1)}), bf16[32,136,128]{2,1,0:T(8,128)(2,1)}, u32[]{:S(2)}, u32[]{:S(2)}) async-start(bf16[32,136,128]{2,1,0:T(8,128)(2,1)} %pack.1), calls=%async_computation | async-start | bytes 2228224 | tf_op jit(solution)/shard_map/all_to_all | solution.py:739
  11.6 4.8 %copy-start.8 = (f32[256]{0:T(256)S(1)}, f32[256]{0:T(256)}, u32[]{:S(2)}) copy-start(f32[256]{0:T(256)} %param.16) | copy-start | bytes 3076
  11.7 14.6 %collective-permute-start = (bf16[4,32,128]{2,1,0:T(8,128)(2,1)S(1)}, bf16[4,32,128]{2,1,0:T(8,128)(2,1)S(1)}, u32[]{:S(2)}, u32[]{:S(2)}) collective-permute-start(bf16[4,32,128]{2,1,0:T(8,128)(2,1)S(1)} %maximum_maximum_fusion), channel_id=1, source_target_pairs={{0,1},{1,0},{2,3},{3,2},{4,5},{5,4},{6,7},{7,6},{8,9},{9,8},{10,11... | collective-permute-start | bytes 98312 | tf_op jit(solution)/shard_map/ppermute | solution.py:702
  12.1 14.2 %collective-permute-start.1 = (bf16[4,32,128]{2,1,0:T(8,128)(2,1)S(1)}, bf16[4,32,128]{2,1,0:T(8,128)(2,1)S(1)}, u32[]{:S(2)}, u32[]{:S(2)}) collective-permute-start(bf16[4,32,128]{2,1,0:T(8,128)(2,1)S(1)} %maximum_maximum_fusion.1), channel_id=1, source_target_pairs={{1,2},{2,1},{3,4},{4,3},{5,6},{6,5},{9,10},{10,9},{11,12},{12,11},... | collective-permute-start | bytes 98312 | tf_op jit(solution)/shard_map/ppermute | solution.py:703
  16.4 13.4 %copy-start.10 = (s32[4,2,3]{0,1,2:T(2,128)S(1)}, s32[4,2,3]{0,1,2:T(2,128)}, u32[]{:S(2)}) copy-start(s32[4,2,3]{0,1,2:T(2,128)} %param.14) | copy-start | bytes 292
  16.4 13.5 %copy-start.1 = (bf16[1,1,2,4,512,128]{5,4,3,2,1,0:T(8,128)(2,1)S(1)}, bf16[1,1,2,4,512,128]{5,4,3,2,1,0:T(8,128)(2,1)}, u32[]{:S(2)}) copy-start(bf16[1,1,2,4,512,128]{5,4,3,2,1,0:T(8,128)(2,1)} %param.10) | copy-start | bytes 3145732
  16.4 13.5 %copy-start.4 = (bf16[1,1,2,4,512,128]{5,4,3,2,1,0:T(8,128)(2,1)S(1)}, bf16[1,1,2,4,512,128]{5,4,3,2,1,0:T(8,128)(2,1)}, u32[]{:S(2)}) copy-start(bf16[1,1,2,4,512,128]{5,4,3,2,1,0:T(8,128)(2,1)} %param.19) | copy-start | bytes 3145732
  26.3 21.8 %collective-permute-start.5 = (bf16[4,512,128]{2,1,0:T(8,128)(2,1)}, bf16[4,512,128]{2,1,0:T(8,128)(2,1)}, u32[]{:S(2)}, u32[]{:S(2)}) collective-permute-start(bf16[4,512,128]{2,1,0:T(8,128)(2,1)} %pad_maximum_fusion), channel_id=1, source_target_pairs={{0,1},{1,0},{2,3},{3,2},{4,5},{5,4},{6,7},{7,6},{8,9},{9,8},{10,11... | collective-permute-start | bytes 1572872 | tf_op jit(solution)/shard_map/ppermute | solution.py:770
  26.3 21.8 %collective-permute-start.6 = (bf16[4,512,128]{2,1,0:T(8,128)(2,1)}, bf16[4,512,128]{2,1,0:T(8,128)(2,1)}, u32[]{:S(2)}, u32[]{:S(2)}) collective-permute-start(bf16[4,512,128]{2,1,0:T(8,128)(2,1)} %pad_maximum_fusion.1), channel_id=1, source_target_pairs={{1,2},{2,1},{3,4},{4,3},{5,6},{6,5},{9,10},{10,9},{11,12},{12,11},... | collective-permute-start | bytes 1572872 | tf_op jit(solution)/shard_map/ppermute | solution.py:771
  29.9 13.9 %collective-permute-start.2 = (f32[2,2,16,128]{3,2,1,0:T(8,128)S(1)}, f32[2,2,16,128]{3,2,1,0:T(8,128)S(1)}, u32[]{:S(2)}, u32[]{:S(2)}) collective-permute-start(f32[2,2,16,128]{3,2,1,0:T(8,128)S(1)} %edges.1.rest_0_), channel_id=1, source_target_pairs={{8,0},{16,8},{24,16},{0,24},{9,1},{17,9},{25,17},{1,25},{10,2},{18... | collective-permute-start | bytes 98312 | tf_op jit(solution)/shard_map/ppermute | solution.py:718
  33.0 10.8 %collective-permute-start.3 = (f32[2,2,16,128]{3,2,1,0:T(8,128)S(1)}, f32[2,2,16,128]{3,2,1,0:T(8,128)S(1)}, u32[]{:S(2)}, u32[]{:S(2)}) collective-permute-start(f32[2,2,16,128]{3,2,1,0:T(8,128)S(1)} %edges.1.rest_0_), channel_id=1, source_target_pairs={{16,0},{24,8},{0,16},{8,24},{17,1},{25,9},{1,17},{9,25},{18,2},{26... | collective-permute-start | bytes 98312 | tf_op jit(solution)/shard_map/ppermute | solution.py:718
  33.0 10.8 %collective-permute-start.4 = (f32[2,2,16,128]{3,2,1,0:T(8,128)S(1)}, f32[2,2,16,128]{3,2,1,0:T(8,128)S(1)}, u32[]{:S(2)}, u32[]{:S(2)}) collective-permute-start(f32[2,2,16,128]{3,2,1,0:T(8,128)S(1)} %edges.1.rest_0_), channel_id=1, source_target_pairs={{24,0},{0,8},{8,16},{16,24},{25,1},{1,9},{9,17},{17,25},{26,2},{2,... | collective-permute-start | bytes 98312 | tf_op jit(solution)/shard_map/ppermute | solution.py:718
  44.7 7.2 %collective-permute-start.7 = (f32[2,2,16,256]{3,2,1,0:T(8,128)S(1)}, f32[2,2,16,256]{3,2,1,0:T(8,128)S(1)}, u32[]{:S(2)}, u32[]{:S(2)}) collective-permute-start(f32[2,2,16,256]{3,2,1,0:T(8,128)S(1)} %get-tuple-element.55.rest_0_), channel_id=1, source_target_pairs={{8,0},{16,8},{24,16},{0,24},{9,1},{17,9},{25,17},{1,25},{10,2},{18... | collective-permute-start | bytes 196616 | tf_op jit(solution)/shard_map/ppermute | solution.py:718
  46.4 5.5 %collective-permute-start.8 = (f32[2,2,16,256]{3,2,1,0:T(8,128)S(1)}, f32[2,2,16,256]{3,2,1,0:T(8,128)S(1)}, u32[]{:S(2)}, u32[]{:S(2)}) collective-permute-start(f32[2,2,16,256]{3,2,1,0:T(8,128)S(1)} %get-tuple-element.55.rest_0_), channel_id=1, source_target_pairs={{16,0},{24,8},{0,16},{8,24},{17,1},{25,9},{1,17},{9,25},{18,2},{26... | collective-permute-start | bytes 196616 | tf_op jit(solution)/shard_map/ppermute | solution.py:718
  47.3 5.6 %collective-permute-start.9 = (f32[2,2,16,256]{3,2,1,0:T(8,128)S(1)}, f32[2,2,16,256]{3,2,1,0:T(8,128)S(1)}, u32[]{:S(2)}, u32[]{:S(2)}) collective-permute-start(f32[2,2,16,256]{3,2,1,0:T(8,128)S(1)} %get-tuple-element.55.rest_0_), channel_id=1, source_target_pairs={{24,0},{0,8},{8,16},{16,24},{25,1},{1,9},{9,17},{17,25},{26,2},{2,... | collective-permute-start | bytes 196616 | tf_op jit(solution)/shard_map/ppermute | solution.py:718
  48.1 4.9 %copy-start.6 = (bf16[9,256,128]{2,1,0:T(8,128)(2,1)S(1)}, bf16[9,256,128]{2,1,0:T(8,128)(2,1)}, u32[]{:S(2)}) copy-start(bf16[9,256,128]{2,1,0:T(8,128)(2,1)} %k2_ref.5) | copy-start | bytes 1769476
  48.1 4.9 %copy-start.7 = (bf16[9,256,128]{2,1,0:T(8,128)(2,1)S(1)}, bf16[9,256,128]{2,1,0:T(8,128)(2,1)}, u32[]{:S(2)}) copy-start(bf16[9,256,128]{2,1,0:T(8,128)(2,1)} %get-tuple-element.54.k1t_ref) | copy-start | bytes 1769476
  54.4 17.3 %collective-permute-start.11 = (bf16[4,512,128]{2,1,0:T(8,128)(2,1)S(1)}, bf16[4,512,128]{2,1,0:T(8,128)(2,1)S(1)}, u32[]{:S(2)}, u32[]{:S(2)}) collective-permute-start(bf16[4,512,128]{2,1,0:T(8,128)(2,1)S(1)} %get-tuple-element.56._.own_ref), channel_id=1, source_target_pairs={{1,2},{2,1},{3,4},{4,3},{5,6},{6,5},{9,10},{10,9},{11,12},{12,11},... | collective-permute-start | bytes 1572872 | tf_op jit(solution)/shard_map/ppermute | solution.py:888
  60.2 10.1 %collective-permute-start.10 = (bf16[4,512,128]{2,1,0:T(8,128)(2,1)S(1)}, bf16[4,512,128]{2,1,0:T(8,128)(2,1)S(1)}, u32[]{:S(2)}, u32[]{:S(2)}) collective-permute-start(bf16[4,512,128]{2,1,0:T(8,128)(2,1)S(1)} %send_pair.1._), channel_id=1, source_target_pairs={{0,1},{1,0},{2,3},{3,2},{4,5},{5,4},{6,7},{7,6},{8,9},{9,8},{10,11... | collective-permute-start | bytes 1572872 | tf_op jit(solution)/shard_map/ppermute | solution.py:898
  60.3 4.2 %copy-start.2 = (bf16[1,1,2,4,512,128]{5,4,3,2,1,0:T(8,128)(2,1)S(1)}, bf16[1,1,2,4,512,128]{5,4,3,2,1,0:T(8,128)(2,1)}, u32[]{:S(2)}) copy-start(bf16[1,1,2,4,512,128]{5,4,3,2,1,0:T(8,128)(2,1)} %param.10) | copy-start | bytes 3145732
  60.3 4.2 %copy-start.5 = (bf16[1,1,2,4,512,128]{5,4,3,2,1,0:T(8,128)(2,1)S(1)}, bf16[1,1,2,4,512,128]{5,4,3,2,1,0:T(8,128)(2,1)}, u32[]{:S(2)}) copy-start(bf16[1,1,2,4,512,128]{5,4,3,2,1,0:T(8,128)(2,1)} %param.19) | copy-start | bytes 3145732
  60.3 4.2 %copy-start.9 = (f32[128]{0:T(128)S(1)}, f32[128]{0:T(128)}, u32[]{:S(2)}) copy-start(f32[128]{0:T(128)} %param.18) | copy-start | bytes 1540

commit v5 on v4

--- a/solution.py
+++ b/solution.py
@@ -129,7 +129,10 @@
         load.start()
     loads[0].wait()
     loads[1].wait()
-    dest_row = dest_ref[...].astype(F32)
+    tiles, faces = lax.axis_size("tile"), lax.axis_size("face")
+    dest = dest_ref[...]
+    dest_face = dest // tiles
+    dest_row = ((dest - dest_face * tiles) * faces + dest_face).astype(F32)
     pixel_row = pixel_ref[...]
     eye = lax.broadcasted_iota(jnp.int32, (block, block), 0) == lax.broadcasted_iota(
         jnp.int32, (block, block), 1
@@ -736,7 +739,7 @@
         cost_estimate=cost(2 * devices * capacity * count * lifted, 2 << 20),
         name="pack",
     )(far(obs_dest.reshape(1, count)), far(obs_pixel.reshape(1, count)), far(obs_values))
-    received = lax.all_to_all(packed, ("face", "tile"), 0, 0, tiled=True)
+    received = lax.all_to_all(packed, ("tile", "face"), 0, 0, tiled=True)
 
     b1 = bias_one.reshape(1, lifted)
     b2 = bias_two.reshape(1, channels)

time: 73.4 us -> 72.3 us (0.985)
  starting transfers between devices: 26.5 us -> 25.5 us
    all_to_all x1, waiting for transfers between devices: 3.78 us -> 4.88 us  [per_device(): received = lax.all_to_all(packed, ('tile', 'face'), 0, 0, tiled=True)]
    ppermute x6, starting transfers between devices: 7 us -> 6.08 us  [exchange(): lax.ppermute(own, 'face', [((i + k) % faces, i) for i in range(faces)])]
    ppermute x1, waiting for transfers between devices: 1.37 us -> 0.49 us  [per_device(): from_cross = lax.ppermute(to_cross, 'tile', crosses)]
  transfers between devices with their start and end apart: 13 -> 13, of which waited for: 3 -> 3; matrix products, arithmetic and copies ran while one was open for 3% -> 3% of each run, Pallas kernels for 42% -> 43%
where the time goes in v5:
time: 72.3 us; the launch traced here: 71.7 us
  Pallas kernels  37.2 us (51%)
  starting transfers between devices  25.5 us (35%)
  waiting for transfers between devices  5.89 us (8%)
  other arithmetic  1.7 us (2%)
  between operations  1.12 us (2%)
    pallas_call x1, Pallas kernels, per_device(): pl.pallas_call(functools.partial(lift_body, rows), in_specs=[hbm] * 4 + [...  9.01 us
    all_to_all x1, starting transfers between devices, per_device(): received = lax.all_to_all(packed, ('tile', 'face'), 0, 0, tiled=True)  7.15 us
    ppermute x6, starting transfers between devices, exchange(): lax.ppermute(own, 'face', [((i + k) % faces, i) for i in range(faces)])  6.08 us
    pallas_call x1, Pallas kernels, per_device(): pl.pallas_call(functools.partial(inside_body, rows), in_specs=[vmem] * 10...  5.71 us
    ppermute x1, starting transfers between devices, per_device(): from_cross = lax.ppermute(to_cross, 'tile', crosses)  4.95 us
    all_to_all x1, waiting for transfers between devices, per_device(): received = lax.all_to_all(packed, ('tile', 'face'), 0, 0, tiled=True)  4.88 us
    pallas_call x1, Pallas kernels, per_device(): pl.pallas_call(functools.partial(middle_body, rows), in_specs=[hbm, vmem,...  4.19 us
    pallas_call x1, Pallas kernels, per_device(): pl.pallas_call(functools.partial(found_body, rows, capacity), in_specs=[h...  3.97 us
  transfers between devices with their start and end apart: 13, of which 3 were waited for; matrix products, arithmetic and copies ran while one was open for 3% of the time, Pallas kernels for 43%

profile of v5, /device:TPU:1, one launch (start us, length us, event | category | flops | bytes accessed | tf_op | source)
XLA Modules:
  0.0 71.7 jit_solution(11911228800146487229)
XLA Ops:
  0.6 3.8 %pack.1 = bf16[32,136,128]{2,1,0:T(8,128)(2,1)} custom-call(s32[1,1024]{1,0:T(1,128)} %bitcast.50, s32[1,1024]{1,0:T(1,128)} %bitcast.51, bf16[1024,256]{1,0:T(8,128)(2,1)} %values_in.1), custom_call_target="tpu_custom_call" | custom-call | flops 1073741824 | bytes 2097152 | tf_op jit(solution)/shard_map/pack/pallas_call | solution.py:725
  4.5 7.2 %all-to-all-start = ((bf16[32,136,128]{2,1,0:T(8,128)(2,1)}), bf16[32,136,128]{2,1,0:T(8,128)(2,1)}, u32[]{:S(2)}, u32[]{:S(2)}) async-start(bf16[32,136,128]{2,1,0:T(8,128)(2,1)} %pack.1), calls=%async_computation | async-start | bytes 2228224 | tf_op jit(solution)/shard_map/all_to_all | solution.py:742
  12.1 3.4 %collective-permute-start.1 = (bf16[4,32,128]{2,1,0:T(8,128)(2,1)S(1)}, bf16[4,32,128]{2,1,0:T(8,128)(2,1)S(1)}, u32[]{:S(2)}, u32[]{:S(2)}) collective-permute-start(bf16[4,32,128]{2,1,0:T(8,128)(2,1)S(1)} %maximum_maximum_fusion.1), channel_id=1, source_target_pairs={{1,2},{2,1},{3,4},{4,3},{5,6},{6,5},{9,10},{10,9},{11,12},{12,11},... | collective-permute-start | bytes 98312 | tf_op jit(solution)/shard_map/ppermute | solution.py:706
  15.6 0.9 %pad_maximum_fusion = bf16[4,512,128]{2,1,0:T(8,128)(2,1)} fusion(bf16[2,512,128]{2,1,0:T(8,128)(2,1)S(1)} %get-tuple-element.79, bf16[2,512,128]{2,1,0:T(8,128)(2,1)S(1)} %get-tuple-element.80), kind=kLoop, calls=%fused_computation | loop fusion | flops 262144 | bytes 1048576 | tf_op jit(solution)/shard_map/concatenate | solution.py:710
  16.4 9.0 %lift.1 = (f32[8,512,256]{2,1,0:T(8,128)}, f32[8,512,256]{2,1,0:T(8,128)}, bf16[9,256,128]{2,1,0:T(8,128)(2,1)}, bf16[9,128,256]{2,1,0:T(8,128)(2,1)}) custom-call(bf16[8,512,128]{2,1,0:T(8,128)(2,1)} %bitcast.32, bf16[8,512,128]{2,1,0:T(8,128)(2,1)} %bitcast.39, bf16[9,128,256]{2,1,0:T(8,128)(2,1)} %k1_in.5, bf16[9,256,128]{2,1,0:T(8,128)(2,1)} %k2_ref.5, ...), custom_call_target="tpu_custom_call" | custom-call | flops 2415919104 | bytes 8388608 | tf_op jit(solution)/shard_map/lift/pallas_call | solution.py:750
  25.4 0.8 %pad_maximum_fusion.1 = bf16[4,512,128]{2,1,0:T(8,128)(2,1)} fusion(bf16[2,512,128]{2,1,0:T(8,128)(2,1)S(1)} %get-tuple-element.78, bf16[2,512,128]{2,1,0:T(8,128)(2,1)S(1)} %get-tuple-element.81), kind=kLoop, calls=%fused_computation.1 | loop fusion | flops 262144 | bytes 1048576 | tf_op jit(solution)/shard_map/concatenate | solution.py:710
  26.3 3.5 %collective-permute-start.6 = (bf16[4,512,128]{2,1,0:T(8,128)(2,1)}, bf16[4,512,128]{2,1,0:T(8,128)(2,1)}, u32[]{:S(2)}, u32[]{:S(2)}) collective-permute-start(bf16[4,512,128]{2,1,0:T(8,128)(2,1)} %pad_maximum_fusion.1), channel_id=1, source_target_pairs={{1,2},{2,1},{3,4},{4,3},{5,6},{6,5},{9,10},{10,9},{11,12},{12,11},... | collective-permute-start | bytes 1572872 | tf_op jit(solution)/shard_map/ppermute | solution.py:774
  29.9 3.1 %collective-permute-start.2 = (f32[2,2,16,128]{3,2,1,0:T(8,128)S(1)}, f32[2,2,16,128]{3,2,1,0:T(8,128)S(1)}, u32[]{:S(2)}, u32[]{:S(2)}) collective-permute-start(f32[2,2,16,128]{3,2,1,0:T(8,128)S(1)} %edges.1.rest_0_), channel_id=1, source_target_pairs={{8,0},{16,8},{24,16},{0,24},{9,1},{17,9},{25,17},{1,25},{10,2},{18... | collective-permute-start | bytes 98312 | tf_op jit(solution)/shard_map/ppermute | solution.py:721
  33.1 0.5 collective-permute-start.4
  33.6 2.5 %rim_in.1 = (f32[2,32,256]{2,1,0:T(8,128)S(1)}, bf16[2,2,3,128,256]{4,3,2,1,0:T(8,128)(2,1)S(1)}) custom-call(s32[4,2,3]{2,1,0:T(2,128)S(1)} %copy.15.matching_ref, bf16[9,128,256]{2,1,0:T(8,128)(2,1)} %k1_in.5, bf16[9,128,256]{2,1,0:T(8,128)(2,1)} %get-tuple-element.37.k2t_in, f32[8,512,256]{2,1,0:T(8,128)} %get-tuple-element.35.pre_in.pre_lo.pre_hi, ...), custom_call_target="tpu_custom_call" | custom-call | bytes 2097152 | tf_op jit(solution)/shard_map/rim_in/pallas_call | solution.py:796
  36.1 4.9 %all-to-all-done.recv_in = bf16[32,136,128]{2,1,0:T(8,128)(2,1)} async-done(((bf16[32,136,128]{2,1,0:T(8,128)(2,1)}), bf16[32,136,128]{2,1,0:T(8,128)(2,1)}, u32[]{:S(2)}, u32[]{:S(2)}) %all-to-all-start) | async-done | bytes 1114144 | tf_op jit(solution)/shard_map/all_to_all | solution.py:742
  40.9 4.0 %found.1 = (bf16[2048,256]{1,0:T(8,128)(2,1)S(1)}, f32[8,2048]{1,0:T(8,128)S(1)}, f32[4,512,256]{2,1,0:T(8,128)S(1)}, f32[4,512,256]{2,1,0:T(8,128)S(1)}, f32[4,...) custom-call(bf16[32,136,128]{2,1,0:T(8,128)(2,1)} %all-to-all-done.recv_in, ...), custom_call_target="tpu_custom_call" | custom-call | flops 2147483648 | bytes 6291456 | tf_op jit(solution)/shard_map/found/pallas_call | solution.py:823
  45.0 0.8 %rim.1 = (f32[2,16,256]{2,1,0:T(8,128)S(1)}, f32[2,16,256]{2,1,0:T(8,128)S(1)}, f32[2,2,16,256]{3,2,1,0:T(8,128)S(1)}) custom-call(s32[4,2,3]{2,1,0:T(2,128)S(1)} %copy.15.matching_ref, bf16[2,2,3,128,256]{4,3,2,1,0:T(8,128)(2,1)S(1)} %get-tuple-element.45.taps_ref, f32[2,32,256]{2,1,0:T(8,128)S(1)} %get-tuple-element.46.base_ref, ...), custom_call_target="tpu_custom_call" | custom-call | bytes 1048576 | tf_op jit(solution)/shard_map/rim/pallas_call | solution.py:846
  46.1 1.3 %collective-permute-start.8 = (f32[2,2,16,256]{3,2,1,0:T(8,128)S(1)}, f32[2,2,16,256]{3,2,1,0:T(8,128)S(1)}, u32[]{:S(2)}, u32[]{:S(2)}) collective-permute-start(f32[2,2,16,256]{3,2,1,0:T(8,128)S(1)} %get-tuple-element.55.rest_0_), channel_id=1, source_target_pairs={{16,0},{24,8},{0,16},{8,24},{17,1},{25,9},{1,17},{9,25},{18,2},{26... | collective-permute-start | bytes 196616 | tf_op jit(solution)/shard_map/ppermute | solution.py:721
  47.5 0.8 %collective-permute-start.9 = (f32[2,2,16,256]{3,2,1,0:T(8,128)S(1)}, f32[2,2,16,256]{3,2,1,0:T(8,128)S(1)}, u32[]{:S(2)}, u32[]{:S(2)}) collective-permute-start(f32[2,2,16,256]{3,2,1,0:T(8,128)S(1)} %get-tuple-element.55.rest_0_), channel_id=1, source_target_pairs={{24,0},{0,8},{8,16},{16,24},{25,1},{1,9},{9,17},{17,25},{26,2},{2,... | collective-permute-start | bytes 196616 | tf_op jit(solution)/shard_map/ppermute | solution.py:721
  48.3 3.8 %border.1 = (bf16[4,512,256]{2,1,0:T(8,128)(2,1)S(1)}, bf16[4,512,256]{2,1,0:T(8,128)(2,1)S(1)}) custom-call(f32[4,512,256]{2,1,0:T(8,128)S(1)} %get-tuple-element.38.pre_b, f32[4,512,256]{2,1,0:T(8,128)S(1)} %get-tuple-element.39.grad_b, f32[4,512,256]{2,1,0:T(8,128)S(1)} %get-tuple-element.40.found_b, ...), custom_call_target="tpu_custom_call" | custom-call | flops 402653184 | bytes 4194304 | tf_op jit(solution)/shard_map/border/pallas_call | solution.py:863
  52.1 0.5 collective-permute-done.9.rest_3_
  52.6 1.4 %send_cross.1 = (bf16[4,512,128]{2,1,0:T(8,128)(2,1)S(1)}, f32[2,2,16,128]{3,2,1,0:T(8,128)S(1)}) custom-call(s32[4,2,3]{2,1,0:T(2,128)S(1)} %copy.15.matching_ref, bf16[4,512,256]{2,1,0:T(8,128)(2,1)S(1)} %get-tuple-element.52.inner_ref.inner_b, bf16[4,512,256]{2,1,0:T(8,128)(2,1)S(1)} %get-tuple-element.53.gp_ref.gp_b, bf16[9,256,128]{2,1,0:T(8,128)(2,1)S(1)} %copy-done.6, ...), custom_call_target="tpu_custom_call" | custom-call | flops 201326592 | bytes 3145728 | tf_op jit(solution)/shard_map/send_cross/pallas_call | solution.py:882
  54.0 4.9 %collective-permute-start.11 = (bf16[4,512,128]{2,1,0:T(8,128)(2,1)S(1)}, bf16[4,512,128]{2,1,0:T(8,128)(2,1)S(1)}, u32[]{:S(2)}, u32[]{:S(2)}) collective-permute-start(bf16[4,512,128]{2,1,0:T(8,128)(2,1)S(1)} %get-tuple-element.56._.own_ref), channel_id=1, source_target_pairs={{1,2},{2,1},{3,4},{4,3},{5,6},{6,5},{9,10},{10,9},{11,12},{12,11},... | collective-permute-start | bytes 1572872 | tf_op jit(solution)/shard_map/ppermute | solution.py:891
  59.0 0.7 %send_pair.1._ = bf16[4,512,128]{2,1,0:T(8,128)(2,1)S(1)} custom-call(bf16[4,512,128]{2,1,0:T(8,128)(2,1)S(1)} %get-tuple-element.56._.own_ref, bf16[4,512,256]{2,1,0:T(8,128)(2,1)S(1)} %get-tuple-element.52.inner_ref.inner_b, bf16[4,512,256]{2,1,0:T(8,128)(2,1)S(1)} %get-tuple-element.53.gp_ref.gp_b, bf16[9,256,128]{2,1,0:T(8,128)(2,1)S(1)} %copy-done.6, ...), custom_call_target="tpu_custom_call" | custom-call | flops 201326592 | bytes 3145728 | tf_op jit(solution)/shard_map/send_pair/pallas_call | solution.py:892
  59.8 4.2 %middle.1 = (bf16[4,512,256]{2,1,0:T(8,128)(2,1)S(1)}, bf16[4,512,256]{2,1,0:T(8,128)(2,1)S(1)}) custom-call(bf16[4,512,128]{2,1,0:T(8,128)(2,1)S(1)} %send_pair.1._, bf16[2048,256]{1,0:T(8,128)(2,1)S(1)} %get-tuple-element.58.values, f32[8,2048]{1,0:T(8,128)S(1)} %get-tuple-element.59.keys, f32[8,512,256]{2,1,0:T(8,128)} %get-tuple-element.35.pre_in.pre_lo.pre_hi, ...), custom_call_target="tpu_custom_call" | custom-call | flops 2147483648 | bytes 10485760 | tf_op jit(solution)/shard_map/middle/pallas_call | solution.py:903
  64.1 5.7 %inside.1 = (bf16[8,512,128]{2,1,0:T(8,128)(2,1)}, f32[4,512,128]{2,1,0:T(8,128)S(1)}, f32[8,512,128]{2,1,0:T(8,128)}, f32[4,512,128]{2,1,0:T(8,128)S(1)}) custom-call(bf16[4,512,256]{2,1,0:T(8,128)(2,1)S(1)} %get-tuple-element.52.inner_ref.inner_b, bf16[4,512,256]{2,1,0:T(8,128)(2,1)S(1)} %get-tuple-element.53.gp_ref.gp_b, ...), custom_call_target="tpu_custom_call" | custom-call | flops 4831838208 | bytes 14680064 | tf_op jit(solution)/shard_map/inside/pallas_call | solution.py:918
  69.8 0.5 collective-permute-done.11.cross_ref
  70.3 1.2 %final.1 = (bf16[8,512,128]{2,1,0:T(8,128)(2,1)}, f32[8,512,128]{2,1,0:T(8,128)}) custom-call(f32[4,512,128]{2,1,0:T(8,128)S(1)} %get-tuple-element.62.ana_b, f32[4,512,128]{2,1,0:T(8,128)S(1)} %get-tuple-element.63.grad_b, bf16[4,512,128]{2,1,0:T(8,128)(2,1)S(1)} %get-tuple-element.56._.own_ref, ...), custom_call_target="tpu_custom_call", output_to_operand_aliasing={{0}: (5, {}), {1}: (6, {})} | custom-call | bytes 6291456 | tf_op jit(solution)/shard_map/final/pallas_call | solution.py:939
  (43 shorter events, 1.1 us)
Async XLA Ops:
  4.5 7.2 %copy-start = (bf16[1,1,2,4,512,128]{5,4,3,2,1,0:T(8,128)(2,1)S(1)}, bf16[1,1,2,4,512,128]{5,4,3,2,1,0:T(8,128)(2,1)}, u32[]{:S(2)}) copy-start(bf16[1,1,2,4,512,128]{5,4,3,2,1,0:T(8,128)(2,1)} %param.10) | copy-start | bytes 3145732
  4.5 7.2 %copy-start.3 = (bf16[1,1,2,4,512,128]{5,4,3,2,1,0:T(8,128)(2,1)S(1)}, bf16[1,1,2,4,512,128]{5,4,3,2,1,0:T(8,128)(2,1)}, u32[]{:S(2)}) copy-start(bf16[1,1,2,4,512,128]{5,4,3,2,1,0:T(8,128)(2,1)} %param.19) | copy-start | bytes 3145732
  4.5 36.5 %all-to-all-start = ((bf16[32,136,128]{2,1,0:T(8,128)(2,1)}), bf16[32,136,128]{2,1,0:T(8,128)(2,1)}, u32[]{:S(2)}, u32[]{:S(2)}) async-start(bf16[32,136,128]{2,1,0:T(8,128)(2,1)} %pack.1), calls=%async_computation | async-start | bytes 2228224 | tf_op jit(solution)/shard_map/all_to_all | solution.py:742
  11.6 4.8 %copy-start.8 = (f32[256]{0:T(256)S(1)}, f32[256]{0:T(256)}, u32[]{:S(2)}) copy-start(f32[256]{0:T(256)} %param.16) | copy-start | bytes 3076
  11.7 14.6 %collective-permute-start = (bf16[4,32,128]{2,1,0:T(8,128)(2,1)S(1)}, bf16[4,32,128]{2,1,0:T(8,128)(2,1)S(1)}, u32[]{:S(2)}, u32[]{:S(2)}) collective-permute-start(bf16[4,32,128]{2,1,0:T(8,128)(2,1)S(1)} %maximum_maximum_fusion), channel_id=1, source_target_pairs={{0,1},{1,0},{2,3},{3,2},{4,5},{5,4},{6,7},{7,6},{8,9},{9,8},{10,11... | collective-permute-start | bytes 98312 | tf_op jit(solution)/shard_map/ppermute | solution.py:705
  12.1 14.2 %collective-permute-start.1 = (bf16[4,32,128]{2,1,0:T(8,128)(2,1)S(1)}, bf16[4,32,128]{2,1,0:T(8,128)(2,1)S(1)}, u32[]{:S(2)}, u32[]{:S(2)}) collective-permute-start(bf16[4,32,128]{2,1,0:T(8,128)(2,1)S(1)} %maximum_maximum_fusion.1), channel_id=1, source_target_pairs={{1,2},{2,1},{3,4},{4,3},{5,6},{6,5},{9,10},{10,9},{11,12},{12,11},... | collective-permute-start | bytes 98312 | tf_op jit(solution)/shard_map/ppermute | solution.py:706
  16.4 13.4 %copy-start.10 = (s32[4,2,3]{0,1,2:T(2,128)S(1)}, s32[4,2,3]{0,1,2:T(2,128)}, u32[]{:S(2)}) copy-start(s32[4,2,3]{0,1,2:T(2,128)} %param.14) | copy-start | bytes 292
  16.4 13.5 %copy-start.1 = (bf16[1,1,2,4,512,128]{5,4,3,2,1,0:T(8,128)(2,1)S(1)}, bf16[1,1,2,4,512,128]{5,4,3,2,1,0:T(8,128)(2,1)}, u32[]{:S(2)}) copy-start(bf16[1,1,2,4,512,128]{5,4,3,2,1,0:T(8,128)(2,1)} %param.10) | copy-start | bytes 3145732
  16.4 13.5 %copy-start.4 = (bf16[1,1,2,4,512,128]{5,4,3,2,1,0:T(8,128)(2,1)S(1)}, bf16[1,1,2,4,512,128]{5,4,3,2,1,0:T(8,128)(2,1)}, u32[]{:S(2)}) copy-start(bf16[1,1,2,4,512,128]{5,4,3,2,1,0:T(8,128)(2,1)} %param.19) | copy-start | bytes 3145732
  26.3 22.0 %collective-permute-start.5 = (bf16[4,512,128]{2,1,0:T(8,128)(2,1)}, bf16[4,512,128]{2,1,0:T(8,128)(2,1)}, u32[]{:S(2)}, u32[]{:S(2)}) collective-permute-start(bf16[4,512,128]{2,1,0:T(8,128)(2,1)} %pad_maximum_fusion), channel_id=1, source_target_pairs={{0,1},{1,0},{2,3},{3,2},{4,5},{5,4},{6,7},{7,6},{8,9},{9,8},{10,11... | collective-permute-start | bytes 1572872 | tf_op jit(solution)/shard_map/ppermute | solution.py:773
  26.3 22.0 %collective-permute-start.6 = (bf16[4,512,128]{2,1,0:T(8,128)(2,1)}, bf16[4,512,128]{2,1,0:T(8,128)(2,1)}, u32[]{:S(2)}, u32[]{:S(2)}) collective-permute-start(bf16[4,512,128]{2,1,0:T(8,128)(2,1)} %pad_maximum_fusion.1), channel_id=1, source_target_pairs={{1,2},{2,1},{3,4},{4,3},{5,6},{6,5},{9,10},{10,9},{11,12},{12,11},... | collective-permute-start | bytes 1572872 | tf_op jit(solution)/shard_map/ppermute | solution.py:774
  29.9 15.0 %collective-permute-start.2 = (f32[2,2,16,128]{3,2,1,0:T(8,128)S(1)}, f32[2,2,16,128]{3,2,1,0:T(8,128)S(1)}, u32[]{:S(2)}, u32[]{:S(2)}) collective-permute-start(f32[2,2,16,128]{3,2,1,0:T(8,128)S(1)} %edges.1.rest_0_), channel_id=1, source_target_pairs={{8,0},{16,8},{24,16},{0,24},{9,1},{17,9},{25,17},{1,25},{10,2},{18... | collective-permute-start | bytes 98312 | tf_op jit(solution)/shard_map/ppermute | solution.py:721
  33.1 11.9 %collective-permute-start.3 = (f32[2,2,16,128]{3,2,1,0:T(8,128)S(1)}, f32[2,2,16,128]{3,2,1,0:T(8,128)S(1)}, u32[]{:S(2)}, u32[]{:S(2)}) collective-permute-start(f32[2,2,16,128]{3,2,1,0:T(8,128)S(1)} %edges.1.rest_0_), channel_id=1, source_target_pairs={{16,0},{24,8},{0,16},{8,24},{17,1},{25,9},{1,17},{9,25},{18,2},{26... | collective-permute-start | bytes 98312 | tf_op jit(solution)/shard_map/ppermute | solution.py:721
  33.1 11.9 %collective-permute-start.4 = (f32[2,2,16,128]{3,2,1,0:T(8,128)S(1)}, f32[2,2,16,128]{3,2,1,0:T(8,128)S(1)}, u32[]{:S(2)}, u32[]{:S(2)}) collective-permute-start(f32[2,2,16,128]{3,2,1,0:T(8,128)S(1)} %edges.1.rest_0_), channel_id=1, source_target_pairs={{24,0},{0,8},{8,16},{16,24},{25,1},{1,9},{9,17},{17,25},{26,2},{2,... | collective-permute-start | bytes 98312 | tf_op jit(solution)/shard_map/ppermute | solution.py:721
  45.8 6.3 %collective-permute-start.7 = (f32[2,2,16,256]{3,2,1,0:T(8,128)S(1)}, f32[2,2,16,256]{3,2,1,0:T(8,128)S(1)}, u32[]{:S(2)}, u32[]{:S(2)}) collective-permute-start(f32[2,2,16,256]{3,2,1,0:T(8,128)S(1)} %get-tuple-element.55.rest_0_), channel_id=1, source_target_pairs={{8,0},{16,8},{24,16},{0,24},{9,1},{17,9},{25,17},{1,25},{10,2},{18... | collective-permute-start | bytes 196616 | tf_op jit(solution)/shard_map/ppermute | solution.py:721
  46.1 5.9 %collective-permute-start.8 = (f32[2,2,16,256]{3,2,1,0:T(8,128)S(1)}, f32[2,2,16,256]{3,2,1,0:T(8,128)S(1)}, u32[]{:S(2)}, u32[]{:S(2)}) collective-permute-start(f32[2,2,16,256]{3,2,1,0:T(8,128)S(1)} %get-tuple-element.55.rest_0_), channel_id=1, source_target_pairs={{16,0},{24,8},{0,16},{8,24},{17,1},{25,9},{1,17},{9,25},{18,2},{26... | collective-permute-start | bytes 196616 | tf_op jit(solution)/shard_map/ppermute | solution.py:721
  47.5 5.1 %collective-permute-start.9 = (f32[2,2,16,256]{3,2,1,0:T(8,128)S(1)}, f32[2,2,16,256]{3,2,1,0:T(8,128)S(1)}, u32[]{:S(2)}, u32[]{:S(2)}) collective-permute-start(f32[2,2,16,256]{3,2,1,0:T(8,128)S(1)} %get-tuple-element.55.rest_0_), channel_id=1, source_target_pairs={{24,0},{0,8},{8,16},{16,24},{25,1},{1,9},{9,17},{17,25},{26,2},{2,... | collective-permute-start | bytes 196616 | tf_op jit(solution)/shard_map/ppermute | solution.py:721
  48.3 4.3 %copy-start.6 = (bf16[9,256,128]{2,1,0:T(8,128)(2,1)S(1)}, bf16[9,256,128]{2,1,0:T(8,128)(2,1)}, u32[]{:S(2)}) copy-start(bf16[9,256,128]{2,1,0:T(8,128)(2,1)} %k2_ref.5) | copy-start | bytes 1769476
  48.3 4.3 %copy-start.7 = (bf16[9,256,128]{2,1,0:T(8,128)(2,1)S(1)}, bf16[9,256,128]{2,1,0:T(8,128)(2,1)}, u32[]{:S(2)}) copy-start(bf16[9,256,128]{2,1,0:T(8,128)(2,1)} %get-tuple-element.54.k1t_ref) | copy-start | bytes 1769476
  54.0 16.3 %collective-permute-start.11 = (bf16[4,512,128]{2,1,0:T(8,128)(2,1)S(1)}, bf16[4,512,128]{2,1,0:T(8,128)(2,1)S(1)}, u32[]{:S(2)}, u32[]{:S(2)}) collective-permute-start(bf16[4,512,128]{2,1,0:T(8,128)(2,1)S(1)} %get-tuple-element.56._.own_ref), channel_id=1, source_target_pairs={{1,2},{2,1},{3,4},{4,3},{5,6},{6,5},{9,10},{10,9},{11,12},{12,11},... | collective-permute-start | bytes 1572872 | tf_op jit(solution)/shard_map/ppermute | solution.py:891
  59.7 10.1 %collective-permute-start.10 = (bf16[4,512,128]{2,1,0:T(8,128)(2,1)S(1)}, bf16[4,512,128]{2,1,0:T(8,128)(2,1)S(1)}, u32[]{:S(2)}, u32[]{:S(2)}) collective-permute-start(bf16[4,512,128]{2,1,0:T(8,128)(2,1)S(1)} %send_pair.1._), channel_id=1, source_target_pairs={{0,1},{1,0},{2,3},{3,2},{4,5},{5,4},{6,7},{7,6},{8,9},{9,8},{10,11... | collective-permute-start | bytes 1572872 | tf_op jit(solution)/shard_map/ppermute | solution.py:901
  59.8 4.2 %copy-start.2 = (bf16[1,1,2,4,512,128]{5,4,3,2,1,0:T(8,128)(2,1)S(1)}, bf16[1,1,2,4,512,128]{5,4,3,2,1,0:T(8,128)(2,1)}, u32[]{:S(2)}) copy-start(bf16[1,1,2,4,512,128]{5,4,3,2,1,0:T(8,128)(2,1)} %param.10) | copy-start | bytes 3145732
  59.8 4.2 %copy-start.5 = (bf16[1,1,2,4,512,128]{5,4,3,2,1,0:T(8,128)(2,1)S(1)}, bf16[1,1,2,4,512,128]{5,4,3,2,1,0:T(8,128)(2,1)}, u32[]{:S(2)}) copy-start(bf16[1,1,2,4,512,128]{5,4,3,2,1,0:T(8,128)(2,1)} %param.19) | copy-start | bytes 3145732
  59.8 4.2 %copy-start.9 = (f32[128]{0:T(128)S(1)}, f32[128]{0:T(128)}, u32[]{:S(2)}) copy-start(f32[128]{0:T(128)} %param.18) | copy-start | bytes 1540

commit v6 on v5

--- a/solution.py
+++ b/solution.py
@@ -767,11 +767,7 @@
         name="lift",
     )(far(x), far(c), far(kernel_one), far(kernel_two), b1)
     pre, grad_inner = far(pre), far(grad_inner)
-    pair_out, cross_out, pair_ends, cross_ends, k1t = lax.optimization_barrier(
-        (pair_out, cross_out, pair_ends, cross_ends, k1t)
-    )
-    pair_rows = lax.ppermute(pair_out, "tile", pairs)
-    cross_rows = lax.ppermute(cross_out, "tile", crosses)
+    pair_ends, cross_ends, k1t = lax.optimization_barrier((pair_ends, cross_ends, k1t))
     low = lambda n: pl.BlockSpec((n, strip, channels), lambda *_: (0, 0, 0))
     high = lambda n, at: pl.BlockSpec((n, strip, channels), lambda *_: (0, at, 0))
     tail = width // strip - 1
@@ -814,6 +810,9 @@
         matching, far(kernel_one), far(k2t), pre, pre, grad_inner, grad_inner, x, x, c, c, pair_ends,
         pair_ends, cross_ends, cross_ends,
     )
+    pair_out, cross_out, side_taps = lax.optimization_barrier((pair_out, cross_out, side_taps))
+    pair_rows = lax.ppermute(pair_out, "tile", pairs)
+    cross_rows = lax.ppermute(cross_out, "tile", crosses)
     side_two = (2, 2, 2 * GROUP, lifted)
     slots = devices * capacity
     onehot_flops = 2 * width * slots * lifted

time: 72.3 us -> 72.1 us (level)
  waiting for transfers between devices: 5.89 us -> 5.16 us
    all_to_all x1, waiting for transfers between devices: 4.88 us -> 4.09 us  [per_device(): received = lax.all_to_all(packed, ('tile', 'face'), 0, 0, tiled=True)]
where the time goes in v6:
time: 72.1 us; the launch traced here: 71.4 us
  Pallas kernels  37.2 us (52%)
  starting transfers between devices  25.9 us (36%)
  waiting for transfers between devices  5.16 us (7%)
  other arithmetic  1.7 us (2%)
  between operations  1.14 us (2%)
    pallas_call x1, Pallas kernels, per_device(): pl.pallas_call(functools.partial(lift_body, rows), in_specs=[hbm] * 4 + [...  9.01 us
    all_to_all x1, starting transfers between devices, per_device(): received = lax.all_to_all(packed, ('tile', 'face'), 0, 0, tiled=True)  7.15 us
    ppermute x6, starting transfers between devices, exchange(): lax.ppermute(own, 'face', [((i + k) % faces, i) for i in range(faces)])  6.78 us
    pallas_call x1, Pallas kernels, per_device(): pl.pallas_call(functools.partial(inside_body, rows), in_specs=[vmem] * 10...  5.71 us
    ppermute x1, starting transfers between devices, per_device(): from_cross = lax.ppermute(to_cross, 'tile', crosses)  4.62 us
    pallas_call x1, Pallas kernels, per_device(): pl.pallas_call(functools.partial(middle_body, rows), in_specs=[hbm, vmem,...  4.19 us
    all_to_all x1, waiting for transfers between devices, per_device(): received = lax.all_to_all(packed, ('tile', 'face'), 0, 0, tiled=True)  4.09 us
    pallas_call x1, Pallas kernels, per_device(): pl.pallas_call(functools.partial(found_body, rows, capacity), in_specs=[h...  3.97 us
  transfers between devices with their start and end apart: 13, of which 3 were waited for; matrix products, arithmetic and copies ran while one was open for 3% of the time, Pallas kernels for 43%

profile of v6, /device:TPU:1, one launch (start us, length us, event | category | flops | bytes accessed | tf_op | source)
XLA Modules:
  0.0 71.4 jit_solution(2135670301107677839)
XLA Ops:
  0.6 3.8 %pack.1 = bf16[32,136,128]{2,1,0:T(8,128)(2,1)} custom-call(s32[1,1024]{1,0:T(1,128)} %bitcast.50, s32[1,1024]{1,0:T(1,128)} %bitcast.51, bf16[1024,256]{1,0:T(8,128)(2,1)} %values_in.1), custom_call_target="tpu_custom_call" | custom-call | flops 1073741824 | bytes 2097152 | tf_op jit(solution)/shard_map/pack/pallas_call | solution.py:725
  4.5 7.2 %all-to-all-start = ((bf16[32,136,128]{2,1,0:T(8,128)(2,1)}), bf16[32,136,128]{2,1,0:T(8,128)(2,1)}, u32[]{:S(2)}, u32[]{:S(2)}) async-start(bf16[32,136,128]{2,1,0:T(8,128)(2,1)} %pack.1), calls=%async_computation | async-start | bytes 2228224 | tf_op jit(solution)/shard_map/all_to_all | solution.py:742
  12.1 3.4 %collective-permute-start.1 = (bf16[4,32,128]{2,1,0:T(8,128)(2,1)S(1)}, bf16[4,32,128]{2,1,0:T(8,128)(2,1)S(1)}, u32[]{:S(2)}, u32[]{:S(2)}) collective-permute-start(bf16[4,32,128]{2,1,0:T(8,128)(2,1)S(1)} %maximum_maximum_fusion.1), channel_id=1, source_target_pairs={{1,2},{2,1},{3,4},{4,3},{5,6},{6,5},{9,10},{10,9},{11,12},{12,11},... | collective-permute-start | bytes 98312 | tf_op jit(solution)/shard_map/ppermute | solution.py:706
  15.6 0.9 %pad_maximum_fusion = bf16[4,512,128]{2,1,0:T(8,128)(2,1)} fusion(bf16[2,512,128]{2,1,0:T(8,128)(2,1)S(1)} %get-tuple-element.81, bf16[2,512,128]{2,1,0:T(8,128)(2,1)S(1)} %get-tuple-element.82), kind=kLoop, calls=%fused_computation | loop fusion | flops 262144 | bytes 1048576 | tf_op jit(solution)/shard_map/concatenate | solution.py:710
  16.4 9.0 %lift.1 = (f32[8,512,256]{2,1,0:T(8,128)}, f32[8,512,256]{2,1,0:T(8,128)}, bf16[9,256,128]{2,1,0:T(8,128)(2,1)}, bf16[9,128,256]{2,1,0:T(8,128)(2,1)}) custom-call(bf16[8,512,128]{2,1,0:T(8,128)(2,1)} %bitcast.32, bf16[8,512,128]{2,1,0:T(8,128)(2,1)} %bitcast.39, bf16[9,128,256]{2,1,0:T(8,128)(2,1)} %k1_in.5, bf16[9,256,128]{2,1,0:T(8,128)(2,1)} %k2_ref.5, ...), custom_call_target="tpu_custom_call" | custom-call | flops 2415919104 | bytes 8388608 | tf_op jit(solution)/shard_map/lift/pallas_call | solution.py:750
  25.4 0.8 %pad_maximum_fusion.1 = bf16[4,512,128]{2,1,0:T(8,128)(2,1)} fusion(bf16[2,512,128]{2,1,0:T(8,128)(2,1)S(1)} %get-tuple-element.80, bf16[2,512,128]{2,1,0:T(8,128)(2,1)S(1)} %get-tuple-element.83), kind=kLoop, calls=%fused_computation.1 | loop fusion | flops 262144 | bytes 1048576 | tf_op jit(solution)/shard_map/concatenate | solution.py:710
  26.4 2.5 %rim_in.1 = (f32[2,32,256]{2,1,0:T(8,128)S(1)}, bf16[2,2,3,128,256]{4,3,2,1,0:T(8,128)(2,1)S(1)}) custom-call(s32[4,2,3]{2,1,0:T(2,128)S(1)} %copy.15.matching_ref, bf16[9,128,256]{2,1,0:T(8,128)(2,1)} %k1_in.5, bf16[9,128,256]{2,1,0:T(8,128)(2,1)} %get-tuple-element.38.k2t_in, f32[8,512,256]{2,1,0:T(8,128)} %get-tuple-element.36.pre_in.pre_lo.pre_hi, ...), custom_call_target="tpu_custom_call" | custom-call | bytes 2097152 | tf_op jit(solution)/shard_map/rim_in/pallas_call | solution.py:792
  29.0 3.5 %collective-permute-start.6 = (bf16[4,512,128]{2,1,0:T(8,128)(2,1)}, bf16[4,512,128]{2,1,0:T(8,128)(2,1)}, u32[]{:S(2)}, u32[]{:S(2)}) collective-permute-start(bf16[4,512,128]{2,1,0:T(8,128)(2,1)} %pad_maximum_fusion.1), channel_id=1, source_target_pairs={{1,2},{2,1},{3,4},{4,3},{5,6},{6,5},{9,10},{10,9},{11,12},{12,11},... | collective-permute-start | bytes 1572872 | tf_op jit(solution)/shard_map/ppermute | solution.py:815
  32.5 3.1 %collective-permute-start.2 = (f32[2,2,16,128]{3,2,1,0:T(8,128)S(1)}, f32[2,2,16,128]{3,2,1,0:T(8,128)S(1)}, u32[]{:S(2)}, u32[]{:S(2)}) collective-permute-start(f32[2,2,16,128]{3,2,1,0:T(8,128)S(1)} %edges.1.rest_0_), channel_id=1, source_target_pairs={{8,0},{16,8},{24,16},{0,24},{9,1},{17,9},{25,17},{1,25},{10,2},{18... | collective-permute-start | bytes 98312 | tf_op jit(solution)/shard_map/ppermute | solution.py:721
  35.6 0.5 collective-permute-start.4
  36.1 4.1 %all-to-all-done.recv_in = bf16[32,136,128]{2,1,0:T(8,128)(2,1)} async-done(((bf16[32,136,128]{2,1,0:T(8,128)(2,1)}), bf16[32,136,128]{2,1,0:T(8,128)(2,1)}, u32[]{:S(2)}, u32[]{:S(2)}) %all-to-all-start) | async-done | bytes 1114144 | tf_op jit(solution)/shard_map/all_to_all | solution.py:742
  40.2 4.0 %found.1 = (bf16[2048,256]{1,0:T(8,128)(2,1)S(1)}, f32[8,2048]{1,0:T(8,128)S(1)}, f32[4,512,256]{2,1,0:T(8,128)S(1)}, f32[4,512,256]{2,1,0:T(8,128)S(1)}, f32[4,...) custom-call(bf16[32,136,128]{2,1,0:T(8,128)(2,1)} %all-to-all-done.recv_in, ...), custom_call_target="tpu_custom_call" | custom-call | flops 2147483648 | bytes 6291456 | tf_op jit(solution)/shard_map/found/pallas_call | solution.py:822
  44.2 0.8 %rim.1 = (f32[2,16,256]{2,1,0:T(8,128)S(1)}, f32[2,16,256]{2,1,0:T(8,128)S(1)}, f32[2,2,16,256]{3,2,1,0:T(8,128)S(1)}) custom-call(s32[4,2,3]{2,1,0:T(2,128)S(1)} %copy.15.matching_ref, bf16[2,2,3,128,256]{4,3,2,1,0:T(8,128)(2,1)S(1)} %get-tuple-element.47.taps_ref, f32[2,32,256]{2,1,0:T(8,128)S(1)} %get-tuple-element.48.base_ref, ...), custom_call_target="tpu_custom_call" | custom-call | bytes 1048576 | tf_op jit(solution)/shard_map/rim/pallas_call | solution.py:845
  45.2 2.3 %collective-permute-start.8 = (f32[2,2,16,256]{3,2,1,0:T(8,128)S(1)}, f32[2,2,16,256]{3,2,1,0:T(8,128)S(1)}, u32[]{:S(2)}, u32[]{:S(2)}) collective-permute-start(f32[2,2,16,256]{3,2,1,0:T(8,128)S(1)} %get-tuple-element.57.rest_0_), channel_id=1, source_target_pairs={{16,0},{24,8},{0,16},{8,24},{17,1},{25,9},{1,17},{9,25},{18,2},{26... | collective-permute-start | bytes 196616 | tf_op jit(solution)/shard_map/ppermute | solution.py:721
  47.5 0.8 %collective-permute-start.9 = (f32[2,2,16,256]{3,2,1,0:T(8,128)S(1)}, f32[2,2,16,256]{3,2,1,0:T(8,128)S(1)}, u32[]{:S(2)}, u32[]{:S(2)}) collective-permute-start(f32[2,2,16,256]{3,2,1,0:T(8,128)S(1)} %get-tuple-element.57.rest_0_), channel_id=1, source_target_pairs={{24,0},{0,8},{8,16},{16,24},{25,1},{1,9},{9,17},{17,25},{26,2},{2,... | collective-permute-start | bytes 196616 | tf_op jit(solution)/shard_map/ppermute | solution.py:721
  48.3 3.8 %border.1 = (bf16[4,512,256]{2,1,0:T(8,128)(2,1)S(1)}, bf16[4,512,256]{2,1,0:T(8,128)(2,1)S(1)}) custom-call(f32[4,512,256]{2,1,0:T(8,128)S(1)} %get-tuple-element.39.pre_b, f32[4,512,256]{2,1,0:T(8,128)S(1)} %get-tuple-element.40.grad_b, f32[4,512,256]{2,1,0:T(8,128)S(1)} %get-tuple-element.41.found_b, ...), custom_call_target="tpu_custom_call" | custom-call | flops 402653184 | bytes 4194304 | tf_op jit(solution)/shard_map/border/pallas_call | solution.py:862
  52.1 0.5 collective-permute-done.9.rest_3_
  52.5 1.4 %send_cross.1 = (bf16[4,512,128]{2,1,0:T(8,128)(2,1)S(1)}, f32[2,2,16,128]{3,2,1,0:T(8,128)S(1)}) custom-call(s32[4,2,3]{2,1,0:T(2,128)S(1)} %copy.15.matching_ref, bf16[4,512,256]{2,1,0:T(8,128)(2,1)S(1)} %get-tuple-element.54.inner_ref.inner_b, bf16[4,512,256]{2,1,0:T(8,128)(2,1)S(1)} %get-tuple-element.55.gp_ref.gp_b, bf16[9,256,128]{2,1,0:T(8,128)(2,1)S(1)} %copy-done.6, ...), custom_call_target="tpu_custom_call" | custom-call | flops 201326592 | bytes 3145728 | tf_op jit(solution)/shard_map/send_cross/pallas_call | solution.py:881
  54.0 4.6 %collective-permute-start.11 = (bf16[4,512,128]{2,1,0:T(8,128)(2,1)S(1)}, bf16[4,512,128]{2,1,0:T(8,128)(2,1)S(1)}, u32[]{:S(2)}, u32[]{:S(2)}) collective-permute-start(bf16[4,512,128]{2,1,0:T(8,128)(2,1)S(1)} %get-tuple-element.58._.own_ref), channel_id=1, source_target_pairs={{1,2},{2,1},{3,4},{4,3},{5,6},{6,5},{9,10},{10,9},{11,12},{12,11},... | collective-permute-start | bytes 1572872 | tf_op jit(solution)/shard_map/ppermute | solution.py:890
  58.6 0.7 %send_pair.1._ = bf16[4,512,128]{2,1,0:T(8,128)(2,1)S(1)} custom-call(bf16[4,512,128]{2,1,0:T(8,128)(2,1)S(1)} %get-tuple-element.58._.own_ref, bf16[4,512,256]{2,1,0:T(8,128)(2,1)S(1)} %get-tuple-element.54.inner_ref.inner_b, bf16[4,512,256]{2,1,0:T(8,128)(2,1)S(1)} %get-tuple-element.55.gp_ref.gp_b, bf16[9,256,128]{2,1,0:T(8,128)(2,1)S(1)} %copy-done.6, ...), custom_call_target="tpu_custom_call" | custom-call | flops 201326592 | bytes 3145728 | tf_op jit(solution)/shard_map/send_pair/pallas_call | solution.py:891
  59.5 4.2 %middle.1 = (bf16[4,512,256]{2,1,0:T(8,128)(2,1)S(1)}, bf16[4,512,256]{2,1,0:T(8,128)(2,1)S(1)}) custom-call(bf16[4,512,128]{2,1,0:T(8,128)(2,1)S(1)} %send_pair.1._, bf16[2048,256]{1,0:T(8,128)(2,1)S(1)} %get-tuple-element.60.values, f32[8,2048]{1,0:T(8,128)S(1)} %get-tuple-element.61.keys, f32[8,512,256]{2,1,0:T(8,128)} %get-tuple-element.36.pre_in.pre_lo.pre_hi, ...), custom_call_target="tpu_custom_call" | custom-call | flops 2147483648 | bytes 10485760 | tf_op jit(solution)/shard_map/middle/pallas_call | solution.py:902
  63.7 5.7 %inside.1 = (bf16[8,512,128]{2,1,0:T(8,128)(2,1)}, f32[4,512,128]{2,1,0:T(8,128)S(1)}, f32[8,512,128]{2,1,0:T(8,128)}, f32[4,512,128]{2,1,0:T(8,128)S(1)}) custom-call(bf16[4,512,256]{2,1,0:T(8,128)(2,1)S(1)} %get-tuple-element.54.inner_ref.inner_b, bf16[4,512,256]{2,1,0:T(8,128)(2,1)S(1)} %get-tuple-element.55.gp_ref.gp_b, ...), custom_call_target="tpu_custom_call" | custom-call | flops 4831838208 | bytes 14680064 | tf_op jit(solution)/shard_map/inside/pallas_call | solution.py:917
  69.4 0.6 collective-permute-done.11.cross_ref
  70.0 1.2 %final.1 = (bf16[8,512,128]{2,1,0:T(8,128)(2,1)}, f32[8,512,128]{2,1,0:T(8,128)}) custom-call(f32[4,512,128]{2,1,0:T(8,128)S(1)} %get-tuple-element.64.ana_b, f32[4,512,128]{2,1,0:T(8,128)S(1)} %get-tuple-element.65.grad_b, bf16[4,512,128]{2,1,0:T(8,128)(2,1)S(1)} %get-tuple-element.58._.own_ref, ...), custom_call_target="tpu_custom_call", output_to_operand_aliasing={{0}: (5, {}), {1}: (6, {})} | custom-call | bytes 6291456 | tf_op jit(solution)/shard_map/final/pallas_call | solution.py:938
  (43 shorter events, 0.9 us)
Async XLA Ops:
  4.5 7.2 %copy-start = (bf16[1,1,2,4,512,128]{5,4,3,2,1,0:T(8,128)(2,1)S(1)}, bf16[1,1,2,4,512,128]{5,4,3,2,1,0:T(8,128)(2,1)}, u32[]{:S(2)}) copy-start(bf16[1,1,2,4,512,128]{5,4,3,2,1,0:T(8,128)(2,1)} %param.10) | copy-start | bytes 3145732
  4.5 7.2 %copy-start.3 = (bf16[1,1,2,4,512,128]{5,4,3,2,1,0:T(8,128)(2,1)S(1)}, bf16[1,1,2,4,512,128]{5,4,3,2,1,0:T(8,128)(2,1)}, u32[]{:S(2)}) copy-start(bf16[1,1,2,4,512,128]{5,4,3,2,1,0:T(8,128)(2,1)} %param.19) | copy-start | bytes 3145732
  4.5 35.8 %all-to-all-start = ((bf16[32,136,128]{2,1,0:T(8,128)(2,1)}), bf16[32,136,128]{2,1,0:T(8,128)(2,1)}, u32[]{:S(2)}, u32[]{:S(2)}) async-start(bf16[32,136,128]{2,1,0:T(8,128)(2,1)} %pack.1), calls=%async_computation | async-start | bytes 2228224 | tf_op jit(solution)/shard_map/all_to_all | solution.py:742
  11.6 4.8 %copy-start.8 = (f32[256]{0:T(256)S(1)}, f32[256]{0:T(256)}, u32[]{:S(2)}) copy-start(f32[256]{0:T(256)} %param.16) | copy-start | bytes 3076
  11.7 14.7 %collective-permute-start = (bf16[4,32,128]{2,1,0:T(8,128)(2,1)S(1)}, bf16[4,32,128]{2,1,0:T(8,128)(2,1)S(1)}, u32[]{:S(2)}, u32[]{:S(2)}) collective-permute-start(bf16[4,32,128]{2,1,0:T(8,128)(2,1)S(1)} %maximum_maximum_fusion), channel_id=1, source_target_pairs={{0,1},{1,0},{2,3},{3,2},{4,5},{5,4},{6,7},{7,6},{8,9},{9,8},{10,11... | collective-permute-start | bytes 98312 | tf_op jit(solution)/shard_map/ppermute | solution.py:705
  12.1 14.3 %collective-permute-start.1 = (bf16[4,32,128]{2,1,0:T(8,128)(2,1)S(1)}, bf16[4,32,128]{2,1,0:T(8,128)(2,1)S(1)}, u32[]{:S(2)}, u32[]{:S(2)}) collective-permute-start(bf16[4,32,128]{2,1,0:T(8,128)(2,1)S(1)} %maximum_maximum_fusion.1), channel_id=1, source_target_pairs={{1,2},{2,1},{3,4},{4,3},{5,6},{6,5},{9,10},{10,9},{11,12},{12,11},... | collective-permute-start | bytes 98312 | tf_op jit(solution)/shard_map/ppermute | solution.py:706
  16.4 9.9 %copy-start.10 = (s32[4,2,3]{0,1,2:T(2,128)S(1)}, s32[4,2,3]{0,1,2:T(2,128)}, u32[]{:S(2)}) copy-start(s32[4,2,3]{0,1,2:T(2,128)} %param.14) | copy-start | bytes 292
  16.4 10.0 %copy-start.1 = (bf16[1,1,2,4,512,128]{5,4,3,2,1,0:T(8,128)(2,1)S(1)}, bf16[1,1,2,4,512,128]{5,4,3,2,1,0:T(8,128)(2,1)}, u32[]{:S(2)}) copy-start(bf16[1,1,2,4,512,128]{5,4,3,2,1,0:T(8,128)(2,1)} %param.10) | copy-start | bytes 3145732
  16.4 10.0 %copy-start.4 = (bf16[1,1,2,4,512,128]{5,4,3,2,1,0:T(8,128)(2,1)S(1)}, bf16[1,1,2,4,512,128]{5,4,3,2,1,0:T(8,128)(2,1)}, u32[]{:S(2)}) copy-start(bf16[1,1,2,4,512,128]{5,4,3,2,1,0:T(8,128)(2,1)} %param.19) | copy-start | bytes 3145732
  28.9 19.3 %collective-permute-start.5 = (bf16[4,512,128]{2,1,0:T(8,128)(2,1)}, bf16[4,512,128]{2,1,0:T(8,128)(2,1)}, u32[]{:S(2)}, u32[]{:S(2)}) collective-permute-start(bf16[4,512,128]{2,1,0:T(8,128)(2,1)} %pad_maximum_fusion), channel_id=1, source_target_pairs={{0,1},{1,0},{2,3},{3,2},{4,5},{5,4},{6,7},{7,6},{8,9},{9,8},{10,11... | collective-permute-start | bytes 1572872 | tf_op jit(solution)/shard_map/ppermute | solution.py:814
  29.0 19.3 %collective-permute-start.6 = (bf16[4,512,128]{2,1,0:T(8,128)(2,1)}, bf16[4,512,128]{2,1,0:T(8,128)(2,1)}, u32[]{:S(2)}, u32[]{:S(2)}) collective-permute-start(bf16[4,512,128]{2,1,0:T(8,128)(2,1)} %pad_maximum_fusion.1), channel_id=1, source_target_pairs={{1,2},{2,1},{3,4},{4,3},{5,6},{6,5},{9,10},{10,9},{11,12},{12,11},... | collective-permute-start | bytes 1572872 | tf_op jit(solution)/shard_map/ppermute | solution.py:815
  32.5 11.7 %collective-permute-start.2 = (f32[2,2,16,128]{3,2,1,0:T(8,128)S(1)}, f32[2,2,16,128]{3,2,1,0:T(8,128)S(1)}, u32[]{:S(2)}, u32[]{:S(2)}) collective-permute-start(f32[2,2,16,128]{3,2,1,0:T(8,128)S(1)} %edges.1.rest_0_), channel_id=1, source_target_pairs={{8,0},{16,8},{24,16},{0,24},{9,1},{17,9},{25,17},{1,25},{10,2},{18... | collective-permute-start | bytes 98312 | tf_op jit(solution)/shard_map/ppermute | solution.py:721
  35.6 8.6 %collective-permute-start.3 = (f32[2,2,16,128]{3,2,1,0:T(8,128)S(1)}, f32[2,2,16,128]{3,2,1,0:T(8,128)S(1)}, u32[]{:S(2)}, u32[]{:S(2)}) collective-permute-start(f32[2,2,16,128]{3,2,1,0:T(8,128)S(1)} %edges.1.rest_0_), channel_id=1, source_target_pairs={{16,0},{24,8},{0,16},{8,24},{17,1},{25,9},{1,17},{9,25},{18,2},{26... | collective-permute-start | bytes 98312 | tf_op jit(solution)/shard_map/ppermute | solution.py:721
  35.6 8.6 %collective-permute-start.4 = (f32[2,2,16,128]{3,2,1,0:T(8,128)S(1)}, f32[2,2,16,128]{3,2,1,0:T(8,128)S(1)}, u32[]{:S(2)}, u32[]{:S(2)}) collective-permute-start(f32[2,2,16,128]{3,2,1,0:T(8,128)S(1)} %edges.1.rest_0_), channel_id=1, source_target_pairs={{24,0},{0,8},{8,16},{16,24},{25,1},{1,9},{9,17},{17,25},{26,2},{2,... | collective-permute-start | bytes 98312 | tf_op jit(solution)/shard_map/ppermute | solution.py:721
  45.1 7.0 %collective-permute-start.7 = (f32[2,2,16,256]{3,2,1,0:T(8,128)S(1)}, f32[2,2,16,256]{3,2,1,0:T(8,128)S(1)}, u32[]{:S(2)}, u32[]{:S(2)}) collective-permute-start(f32[2,2,16,256]{3,2,1,0:T(8,128)S(1)} %get-tuple-element.57.rest_0_), channel_id=1, source_target_pairs={{8,0},{16,8},{24,16},{0,24},{9,1},{17,9},{25,17},{1,25},{10,2},{18... | collective-permute-start | bytes 196616 | tf_op jit(solution)/shard_map/ppermute | solution.py:721
  45.2 6.9 %collective-permute-start.8 = (f32[2,2,16,256]{3,2,1,0:T(8,128)S(1)}, f32[2,2,16,256]{3,2,1,0:T(8,128)S(1)}, u32[]{:S(2)}, u32[]{:S(2)}) collective-permute-start(f32[2,2,16,256]{3,2,1,0:T(8,128)S(1)} %get-tuple-element.57.rest_0_), channel_id=1, source_target_pairs={{16,0},{24,8},{0,16},{8,24},{17,1},{25,9},{1,17},{9,25},{18,2},{26... | collective-permute-start | bytes 196616 | tf_op jit(solution)/shard_map/ppermute | solution.py:721
  47.5 5.1 %collective-permute-start.9 = (f32[2,2,16,256]{3,2,1,0:T(8,128)S(1)}, f32[2,2,16,256]{3,2,1,0:T(8,128)S(1)}, u32[]{:S(2)}, u32[]{:S(2)}) collective-permute-start(f32[2,2,16,256]{3,2,1,0:T(8,128)S(1)} %get-tuple-element.57.rest_0_), channel_id=1, source_target_pairs={{24,0},{0,8},{8,16},{16,24},{25,1},{1,9},{9,17},{17,25},{26,2},{2,... | collective-permute-start | bytes 196616 | tf_op jit(solution)/shard_map/ppermute | solution.py:721
  48.3 4.3 %copy-start.6 = (bf16[9,256,128]{2,1,0:T(8,128)(2,1)S(1)}, bf16[9,256,128]{2,1,0:T(8,128)(2,1)}, u32[]{:S(2)}) copy-start(bf16[9,256,128]{2,1,0:T(8,128)(2,1)} %k2_ref.5) | copy-start | bytes 1769476
  48.3 4.3 %copy-start.7 = (bf16[9,256,128]{2,1,0:T(8,128)(2,1)S(1)}, bf16[9,256,128]{2,1,0:T(8,128)(2,1)}, u32[]{:S(2)}) copy-start(bf16[9,256,128]{2,1,0:T(8,128)(2,1)} %get-tuple-element.56.k1t_ref) | copy-start | bytes 1769476
  54.0 16.0 %collective-permute-start.11 = (bf16[4,512,128]{2,1,0:T(8,128)(2,1)S(1)}, bf16[4,512,128]{2,1,0:T(8,128)(2,1)S(1)}, u32[]{:S(2)}, u32[]{:S(2)}) collective-permute-start(bf16[4,512,128]{2,1,0:T(8,128)(2,1)S(1)} %get-tuple-element.58._.own_ref), channel_id=1, source_target_pairs={{1,2},{2,1},{3,4},{4,3},{5,6},{6,5},{9,10},{10,9},{11,12},{12,11},... | collective-permute-start | bytes 1572872 | tf_op jit(solution)/shard_map/ppermute | solution.py:890
  59.4 10.1 %collective-permute-start.10 = (bf16[4,512,128]{2,1,0:T(8,128)(2,1)S(1)}, bf16[4,512,128]{2,1,0:T(8,128)(2,1)S(1)}, u32[]{:S(2)}, u32[]{:S(2)}) collective-permute-start(bf16[4,512,128]{2,1,0:T(8,128)(2,1)S(1)} %send_pair.1._), channel_id=1, source_target_pairs={{0,1},{1,0},{2,3},{3,2},{4,5},{5,4},{6,7},{7,6},{8,9},{9,8},{10,11... | collective-permute-start | bytes 1572872 | tf_op jit(solution)/shard_map/ppermute | solution.py:900
  59.4 4.2 %copy-start.2 = (bf16[1,1,2,4,512,128]{5,4,3,2,1,0:T(8,128)(2,1)S(1)}, bf16[1,1,2,4,512,128]{5,4,3,2,1,0:T(8,128)(2,1)}, u32[]{:S(2)}) copy-start(bf16[1,1,2,4,512,128]{5,4,3,2,1,0:T(8,128)(2,1)} %param.10) | copy-start | bytes 3145732
  59.4 4.2 %copy-start.5 = (bf16[1,1,2,4,512,128]{5,4,3,2,1,0:T(8,128)(2,1)S(1)}, bf16[1,1,2,4,512,128]{5,4,3,2,1,0:T(8,128)(2,1)}, u32[]{:S(2)}) copy-start(bf16[1,1,2,4,512,128]{5,4,3,2,1,0:T(8,128)(2,1)} %param.19) | copy-start | bytes 3145732
  59.5 4.2 %copy-start.9 = (f32[128]{0:T(128)S(1)}, f32[128]{0:T(128)}, u32[]{:S(2)}) copy-start(f32[128]{0:T(128)} %param.18) | copy-start | bytes 1540
